TPU v7x, 256 devices: a whole 4x4x8 slice. The times are simulated.
256 devices in a mesh: section: 16 (over y_hi, z), tensor: 4 (over x), dp: 4 (over y_lo, core).
Axes of the slice: x: 4, y: 4 (y_hi: 2, y_lo: 2; y = y_hi * 2 + y_lo), z: 8, core: 2. Of those that a mesh axis runs over, the one named last changes fastest.
Arguments:
- inbound: bfloat16 [16, 4, 3, 384, 6144], P('section', 'dp', None, None, 'tensor'), may hold values from -6 to 6
- parked: bfloat16 [16, 4, 3, 384, 6144], P('section', 'dp', None, None, 'tensor'), may hold values from -6 to 6
- grad_out: bfloat16 [16, 4, 384, 6144], P('section', 'dp', None, 'tensor'), may hold values from -6 to 6
- query_gain: float32 [16, 6144], P('section', 'tensor'), may hold values from 0.5 to 1.5
- plan: int32 [16, 2], P('section'), may hold values from 0 to 7
- lengths: int32 [4, 8], P('dp'), may hold values from 1 to 384
Outputs:
- attended: bfloat16 [16, 4, 384, 6144], P('section', 'dp', None, 'tensor')
- grads_qkv: bfloat16 [16, 4, 3, 384, 6144], P('section', 'dp', None, None, 'tensor')
- gain_grad: float32 [16, 6144], P('section', 'tensor')
All inputs are finite; a program needn't handle non-finite values.
Results may differ from a plain program's by a relative error of at most 0.022.
Values may be sent and summed in bfloat16 or wider, within the bound.
No kernel may reach another device: no remote copies, remote signals or barrier semaphores. Data moves between devices by JAX's collectives and lax.ppermute only.
A program may use at most 128 MiB of HBM per device.

v0:
```python
import jax
import jax.numpy as jnp
from jax import lax
from jax.sharding import PartitionSpec as P

HD = 128


def shifted(value, axis, by):
    size = lax.axis_size(axis)
    return lax.ppermute(value, axis, [(i, (i + by) % size) for i in range(size)])


def swapped(value, axis, bit):
    return lax.ppermute(value, axis, [(i, i ^ 1 << bit) for i in range(lax.axis_size(axis))])


def masked_weights(query, keys, length):
    seq = query.shape[0]
    heads = query.shape[1] // HD
    qh = query.reshape(seq, heads, HD)
    kh = keys.reshape(seq, heads, HD)
    scores = jnp.einsum("qhd,khd->hqk", qh, kh, preferred_element_type=jnp.float32) / jnp.sqrt(
        jnp.float32(HD)
    )
    rows = jnp.arange(seq)[:, None]
    cols = jnp.arange(seq)[None, :]
    allowed = (cols <= rows) & (cols < length)
    scores = jnp.where(allowed[None], scores, jnp.float32(-1e30))
    top = jnp.max(scores, axis=-1, keepdims=True)
    expo = jnp.exp(scores - top)
    return expo / jnp.sum(expo, axis=-1, keepdims=True)


def forward_part(query, keys, values, gain, length):
    seq = query.shape[0]
    heads = query.shape[1] // HD
    scaled = (query.astype(jnp.float32) * gain).astype(jnp.bfloat16)
    weights = masked_weights(scaled, keys, length).astype(jnp.bfloat16)
    out = jnp.einsum(
        "hqk,khd->qhd", weights, values.reshape(seq, heads, HD), preferred_element_type=jnp.float32
    )
    return out.reshape(seq, heads * HD).astype(jnp.bfloat16)


def backward_part(query, keys, values, upstream, gain, length):
    seq = query.shape[0]
    heads = query.shape[1] // HD
    scaled = (query.astype(jnp.float32) * gain).astype(jnp.bfloat16)
    weights = masked_weights(scaled, keys, length)
    wround = weights.astype(jnp.bfloat16)
    gh = upstream.reshape(seq, heads, HD)
    vh = values.reshape(seq, heads, HD)
    kh = keys.reshape(seq, heads, HD)
    sh = scaled.reshape(seq, heads, HD)
    dvalue = jnp.einsum("hqk,qhd->khd", wround, gh, preferred_element_type=jnp.float32)
    recomputed = jnp.einsum("hqk,khd->qhd", wround, vh, preferred_element_type=jnp.float32)
    dweight = jnp.einsum("qhd,khd->hqk", gh, vh, preferred_element_type=jnp.float32)
    delta = jnp.einsum("qhd,qhd->hq", gh.astype(jnp.float32), recomputed)
    dscore = (weights * (dweight - delta[:, :, None]) / jnp.sqrt(jnp.float32(HD))).astype(
        jnp.bfloat16
    )
    dscaled = jnp.einsum("hqk,khd->qhd", dscore, kh, preferred_element_type=jnp.float32).reshape(
        seq, heads * HD
    )
    dkeys = jnp.einsum("hqk,qhd->khd", dscore, sh, preferred_element_type=jnp.float32).reshape(
        seq, heads * HD
    )
    dquery = dscaled * gain
    raw = jnp.sum(dscaled * query.astype(jnp.float32), axis=0)
    stacked = jnp.stack([dquery, dkeys, dvalue.reshape(seq, heads * HD)]).astype(jnp.bfloat16)
    return (stacked, raw)


def pick_length(table_row, index):
    positions = jnp.arange(table_row.shape[0], dtype=jnp.int32)
    return jnp.sum(jnp.where(positions == index, table_row, 0))


def shards(inbound, parked, grad_out, query_gain, plan, lengths):
    arrived = shifted(inbound, "section", 1)
    upstream = shifted(grad_out, "section", -1)
    levels = lax.axis_size("section").bit_length() - 1
    reloaded = parked
    for bit in range(levels):
        reloaded = swapped(reloaded, "section", bit)
    gain = query_gain[0]
    flen = pick_length(lengths[0], plan[0, 0])
    blen = pick_length(lengths[0], plan[0, 1])
    block = arrived[0, 0]
    attended = forward_part(block[0], block[1], block[2], gain, flen)[None, None]
    stored = reloaded[0, 0]
    stacked, raw = backward_part(stored[0], stored[1], stored[2], upstream[0, 0], gain, blen)
    total = lax.psum(raw, "dp")
    squares = lax.psum(jnp.sum(total * total), ("section", "tensor"))
    scaled_grad = total / (jnp.sqrt(squares) + 1e-06)
    return (attended, stacked[None, None], scaled_grad[None])


def solution(mesh):
    placed = (
        P("section", "dp", None, None, "tensor"),
        P("section", "dp", None, None, "tensor"),
        P("section", "dp", None, "tensor"),
        P("section", "tensor"),
        P("section", None),
        P("dp", None),
    )
    return jax.shard_map(
        shards,
        mesh=mesh,
        in_specs=placed,
        out_specs=(
            P("section", "dp", None, "tensor"),
            P("section", "dp", None, None, "tensor"),
            P("section", "tensor"),
        ),
        check_vma=False,
    )
```

profile of v0, /device:TPU:8, one launch (start us, length us, event | category | flops | bytes accessed | tf_op | source)
XLA Modules:
  0.0 762.8 jit_solution(15038731864893730201)
XLA Ops:
  0.6 0.0 copy-start
  0.6 6.2 copy.29
  6.8 1.9 collective-permute-start.1
  8.7 76.7 %collective-permute-done.1 = bf16[1,1,3,384,1536]{3,4,2,1,0:T(8,128)(2,1)S(1)} collective-permute-done((bf16[1,1,3,384,1536]{3,4,2,1,0:T(8,128)(2,1)}, bf16[1,1,3,384,1536]{3,4,2,1,0:T(8,128)(2,1)S(1)}, u32[]{:S(2)}, u32[]{:S(2)}) %collective-permute-start.1) | collective-permute-done | bytes 3538976 | tf_op jit(solution)/shard_map/ppermute | solution.py:15
  85.5 3.3 collective-permute-start.2
  88.7 151.8 %collective-permute-done.2 = bf16[1,1,3,384,1536]{3,4,2,1,0:T(8,128)(2,1)} collective-permute-done((bf16[1,1,3,384,1536]{3,4,2,1,0:T(8,128)(2,1)S(1)}, bf16[1,1,3,384,1536]{3,4,2,1,0:T(8,128)(2,1)}, u32[]{:S(2)}, u32[]{:S(2)}) %collective-permute-start.2) | collective-permute-done | bytes 3538976 | tf_op jit(solution)/shard_map/ppermute | solution.py:15
  240.5 6.2 collective-permute-start.3
  246.7 0.0 copy-done
  246.7 3.6 copy.25
  250.3 0.0 collective-permute-start
  250.3 150.5 %collective-permute-done.3 = bf16[1,1,3,384,1536]{3,4,2,1,0:T(8,128)(2,1)} collective-permute-done((bf16[1,1,3,384,1536]{3,4,2,1,0:T(8,128)(2,1)}, bf16[1,1,3,384,1536]{3,4,2,1,0:T(8,128)(2,1)}, u32[]{:S(2)}, u32[]{:S(2)}) %collective-permute-start.3) | collective-permute-done | bytes 3538976 | tf_op jit(solution)/shard_map/ppermute | solution.py:15
  400.8 2.3 collective-permute-start.4
  403.1 2.5 copy.32
  405.6 2.0 collective-permute-start.5
  407.6 0.0 copy-done.2
  407.6 1.3 fusion.33
  408.9 2.7 fusion.26
  411.6 1.3 iota_compare_fusion.1
  412.9 0.8 fusion.23
  413.7 0.1 fusion.24
  413.8 60.4 %collective-permute-done = bf16[1,1,3,384,1536]{3,4,2,1,0:T(8,128)(2,1)} collective-permute-done((bf16[1,1,3,384,1536]{3,4,2,1,0:T(8,128)(2,1)}, bf16[1,1,3,384,1536]{3,4,2,1,0:T(8,128)(2,1)}, u32[]{:S(2)}, u32[]{:S(2)}) %collective-permute-start) | collective-permute-done | bytes 3538976 | tf_op jit(solution)/shard_map/ppermute | solution.py:11
  474.2 2.3 fusion.32
  476.5 1.2 fusion.17
  477.7 2.2 fusion.34
  479.9 2.0 fusion.15
  481.9 2.4 copy.42
  484.3 65.5 %collective-permute-done.4 = bf16[1,1,3,384,1536]{3,4,2,1,0:T(8,128)(2,1)S(1)} collective-permute-done((bf16[1,1,3,384,1536]{3,4,2,1,0:T(8,128)(2,1)}, bf16[1,1,3,384,1536]{3,4,2,1,0:T(8,128)(2,1)S(1)}, u32[]{:S(2)}, u32[]{:S(2)}) %collective-permute-start.4) | collective-permute-done | bytes 3538976 | tf_op jit(solution)/shard_map/ppermute | solution.py:15
  549.8 0.4 fusion.31
  550.2 0.0 copy-start.1
  550.2 1.2 fusion.21
  551.3 0.0 copy-done.1
  551.4 2.2 fusion.35
  553.6 0.7 fusion.11
  554.3 0.0 collective-permute-done.5
  554.3 2.2 multiply_reduce_fusion
  556.5 2.7 multiply_convert_fusion
  559.2 3.0 fusion.13
  562.2 2.3 convolution_convert_fusion.1
  564.4 7.0 psum.14
  571.5 0.6 multiply_reduce_fusion.1
  572.1 3.5 convolution_convert_fusion
  575.6 178.5 %psum.15 = f32[]{:T(128)} all-reduce(f32[]{:T(128)} %multiply_reduce_fusion.1), channel_id=1, replica_groups=mesh['section'=16,'tensor'=4,'dp'=4] {'section','tensor'}, use_global_device_ids=true, to_apply=%region_9.10 | all-reduce | flops 1 | bytes 8 | tf_op jit(solution)/shard_map/psum | solution.py:95
  754.8 0.6 broadcast_in_dim.43
  755.4 2.0 copy.37
  757.4 0.2 fusion.16
  757.7 1.6 copy.40
  759.2 1.6 copy.41
  760.8 2.0 pad_maximum_fusion
  (3 shorter events, 0.0 us)
Async XLA Ops:
  0.6 246.1 %copy-start = (bf16[1,1,3,384,1536]{4,3,2,1,0:T(8,128)(2,1)S(1)}, bf16[1,1,3,384,1536]{4,3,2,1,0:T(8,128)(2,1)}, u32[]{:S(2)}) copy-start(bf16[1,1,3,384,1536]{4,3,2,1,0:T(8,128)(2,1)} %param.6) | copy-start | bytes 10616836
  6.8 78.7 %collective-permute-start.1 = (bf16[1,1,3,384,1536]{3,4,2,1,0:T(8,128)(2,1)}, bf16[1,1,3,384,1536]{3,4,2,1,0:T(8,128)(2,1)S(1)}, u32[]{:S(2)}, u32[]{:S(2)}) collective-permute-start(bf16[1,1,3,384,1536]{3,4,2,1,0:T(8,128)(2,1)} %copy.29), channel_id=1, source_target_pairs={{0,16},{16,0},{32,48},{48,32},{64,80},{80,64},{96,112},{112,96},{1... | collective-permute-start | bytes 10616840 | tf_op jit(solution)/shard_map/ppermute | solution.py:15
  85.5 155.1 %collective-permute-start.2 = (bf16[1,1,3,384,1536]{3,4,2,1,0:T(8,128)(2,1)S(1)}, bf16[1,1,3,384,1536]{3,4,2,1,0:T(8,128)(2,1)}, u32[]{:S(2)}, u32[]{:S(2)}) collective-permute-start(bf16[1,1,3,384,1536]{3,4,2,1,0:T(8,128)(2,1)S(1)} %collective-permute-done.1), channel_id=1, source_target_pairs={{0,32},{16,48},{32,0},{48,16},{64,96},{80,112},{96,64},{112,80},{1... | collective-permute-start | bytes 10616840 | tf_op jit(solution)/shard_map/ppermute | solution.py:15
  240.5 160.3 %collective-permute-start.3 = (bf16[1,1,3,384,1536]{3,4,2,1,0:T(8,128)(2,1)}, bf16[1,1,3,384,1536]{3,4,2,1,0:T(8,128)(2,1)}, u32[]{:S(2)}, u32[]{:S(2)}) collective-permute-start(bf16[1,1,3,384,1536]{3,4,2,1,0:T(8,128)(2,1)} %collective-permute-done.2), channel_id=1, source_target_pairs={{0,64},{16,80},{32,96},{48,112},{64,0},{80,16},{96,32},{112,48},{1... | collective-permute-start | bytes 10616840 | tf_op jit(solution)/shard_map/ppermute | solution.py:15
  250.3 157.3 %copy-start.2 = (f32[1,1536]{1,0:T(1,128)S(1)}, f32[1,1536]{1,0:T(1,128)}, u32[]{:S(2)}) copy-start(f32[1,1536]{1,0:T(1,128)} %param.9) | copy-start | bytes 18436
  250.3 223.9 %collective-permute-start = (bf16[1,1,3,384,1536]{3,4,2,1,0:T(8,128)(2,1)}, bf16[1,1,3,384,1536]{3,4,2,1,0:T(8,128)(2,1)}, u32[]{:S(2)}, u32[]{:S(2)}) collective-permute-start(bf16[1,1,3,384,1536]{3,4,2,1,0:T(8,128)(2,1)} %copy.25), channel_id=1, source_target_pairs={{0,16},{16,32},{32,48},{48,64},{64,80},{80,96},{96,112},{112,128},... | collective-permute-start | bytes 10616840 | tf_op jit(solution)/shard_map/ppermute | solution.py:11
  400.8 149.0 %collective-permute-start.4 = (bf16[1,1,3,384,1536]{3,4,2,1,0:T(8,128)(2,1)}, bf16[1,1,3,384,1536]{3,4,2,1,0:T(8,128)(2,1)S(1)}, u32[]{:S(2)}, u32[]{:S(2)}) collective-permute-start(bf16[1,1,3,384,1536]{3,4,2,1,0:T(8,128)(2,1)} %collective-permute-done.3), channel_id=1, source_target_pairs={{0,128},{16,144},{32,160},{48,176},{64,192},{80,208},{96,224},{112... | collective-permute-start | bytes 10616840 | tf_op jit(solution)/shard_map/ppermute | solution.py:15
  405.6 148.7 %collective-permute-start.5 = (bf16[1,1,384,1536]{2,3,1,0:T(8,128)(2,1)}, bf16[1,1,384,1536]{2,3,1,0:T(8,128)(2,1)}, u32[]{:S(2)}, u32[]{:S(2)}) collective-permute-start(bf16[1,1,384,1536]{2,3,1,0:T(8,128)(2,1)} %copy.32), channel_id=1, source_target_pairs={{0,240},{16,0},{32,16},{48,32},{64,48},{80,64},{96,80},{112,96},{1... | collective-permute-start | bytes 3538952 | tf_op jit(solution)/shard_map/ppermute | solution.py:11
  550.2 1.2 copy-start.1
where the time goes:
time: 763 us
  waiting for transfers between devices  505 us (66%)
  blocking collectives  186 us (24%)
  local copies, waits for them, and re-layouts  24.4 us (3%)
  matrix products  17.9 us (2%)
  starting transfers between devices  15.7 us (2%)
  other arithmetic  12.9 us (2%)
    ppermute x4, waiting for transfers between devices, swapped(): lax.ppermute(value, axis, [(i, i ^ 1 << bit) for i in range(lax.axis_size...  445 us
    psum x1, blocking collectives, shards(): squares = lax.psum(jnp.sum(total * total), ('section', 'tensor'))  179 us
    ppermute x2, waiting for transfers between devices, shifted(): lax.ppermute(value, axis, [(i, (i + by) % size) for i in range(size)])  60.4 us
  transfers between devices with their start and end apart: 6, of which 5 were waited for; matrix products, arithmetic and copies ran while one was open for 4% of the time, Pallas kernels for 0%

commit v1 on v0

v1 whole, which is shorter than its diff:
```python
import functools

import jax
import jax.numpy as jnp
from jax import lax
from jax.experimental import pallas as pl
from jax.experimental.pallas import tpu as pltpu
from jax.sharding import PartitionSpec as P

HD = 128
BLOCK = 128
HEADS_PER_STEP = 2
STRIPS = 4
NEG = -1e30

DIM_LAST = (((1,), (1,)), ((), ()))
DIM_FIRST = (((0,), (0,)), ((), ()))


def site(s, n):
    return s if s % (n // 2) in (1, 2, 5, 6) else n - 1 - s


def moved(value, target):
    size = lax.axis_size("section")
    return lax.ppermute(value, "section", [(i, target(i, size) % size) for i in range(size)])


def doubled_sum(value, axis):
    size = lax.axis_size(axis)
    step = 1
    while step < size:
        value = value + lax.ppermute(value, axis, [(i, i ^ step) for i in range(size)])
        step *= 2
    return value


def dot(a, b, dims=(((1,), (0,)), ((), ()))):
    return lax.dot_general(a, b, dims, preferred_element_type=jnp.float32)


def row_length(tail_ref, lengths_ref, column):
    index = tail_ref[:, column : column + 1].astype(jnp.int32)
    table = lengths_ref[...]
    lanes = lax.broadcasted_iota(jnp.int32, table.shape, 1)
    return jnp.sum(jnp.where(lanes == index, table, 0), axis=1, keepdims=True)


def weights_of(qs, keys, start, length):
    n = keys.shape[0]
    scores = dot(keys, qs, DIM_LAST) * (1.0 / HD**0.5)
    rows = lax.broadcasted_iota(jnp.int32, scores.shape, 0)
    cols = lax.broadcasted_iota(jnp.int32, scores.shape, 1) + start
    scores = jnp.where((rows <= cols) & (rows < length), scores, NEG)
    top = jnp.max(scores, axis=0, keepdims=True)
    expo = jnp.exp(scores - top)
    return expo * (1.0 / jnp.sum(expo, axis=0, keepdims=True))


def forward_kernel(q_ref, k_ref, v_ref, gain_ref, tail_ref, lengths_ref, out_ref):
    length = row_length(tail_ref, lengths_ref, 0)
    seq = q_ref.shape[0]
    for h in range(HEADS_PER_STEP):
        hs = slice(h * HD, (h + 1) * HD)
        gain = gain_ref[:, hs]
        for start in range(0, seq, BLOCK):
            end = start + BLOCK
            qs = (q_ref[start:end, hs].astype(jnp.float32) * gain).astype(jnp.bfloat16)
            wb = weights_of(qs, k_ref[:end, hs], start, length).astype(jnp.bfloat16)
            out_ref[start:end, hs] = dot(wb, v_ref[:end, hs], DIM_FIRST).astype(jnp.bfloat16)


def backward_kernel(*refs):
    strips = refs[:STRIPS]
    g_ref, gain_ref, tail_ref, lengths_ref, out_ref, raw_ref = refs[STRIPS:]
    length = row_length(tail_ref, lengths_ref, 1)
    seq = g_ref.shape[0]
    for h in range(HEADS_PER_STEP):
        hs = slice(h * HD, (h + 1) * HD)
        gain = gain_ref[:, hs]
        q, k, v = (jnp.concatenate([strip[part, :, hs] for strip in strips], axis=0) for part in range(3))
        dks = [jnp.zeros((BLOCK, HD), jnp.float32) for _ in range(seq // BLOCK)]
        dvs = [jnp.zeros((BLOCK, HD), jnp.float32) for _ in range(seq // BLOCK)]
        raw = jnp.zeros((1, HD), jnp.float32)
        for start in range(0, seq, BLOCK):
            end = start + BLOCK
            query = q[start:end].astype(jnp.float32)
            qs = (query * gain).astype(jnp.bfloat16)
            keys = k[:end]
            g = g_ref[start:end, hs]
            w = weights_of(qs, keys, start, length)
            wb = w.astype(jnp.bfloat16)
            dw = dot(v[:end], g, DIM_LAST)
            delta = jnp.sum(wb.astype(jnp.float32) * dw, axis=0, keepdims=True)
            ds = (w * (dw - delta) * (1.0 / HD**0.5)).astype(jnp.bfloat16)
            dv = dot(wb, g)
            dk = dot(ds, qs)
            for b in range(end // BLOCK):
                dvs[b] = dvs[b] + dv[b * BLOCK : (b + 1) * BLOCK]
                dks[b] = dks[b] + dk[b * BLOCK : (b + 1) * BLOCK]
            dqs = dot(ds, keys, DIM_FIRST)
            out_ref[0, start:end, hs] = (dqs * gain).astype(jnp.bfloat16)
            raw = raw + jnp.sum(dqs * query, axis=0, keepdims=True)
        for b in range(seq // BLOCK):
            out_ref[1, b * BLOCK : (b + 1) * BLOCK, hs] = dks[b].astype(jnp.bfloat16)
            out_ref[2, b * BLOCK : (b + 1) * BLOCK, hs] = dvs[b].astype(jnp.bfloat16)
        raw_ref[:, hs] = raw


def qkv_specs(seq, width):
    return [
        pl.BlockSpec((None, None, None, seq, width), functools.partial(lambda h, part: (0, 0, part, 0, h), part=part))
        for part in range(3)
    ]


def small_specs(width, features, table):
    return [
        pl.BlockSpec((1, width), lambda h: (0, h)),
        pl.BlockSpec((1, HD), lambda h: (0, features // HD)),
        pl.BlockSpec(table.shape, lambda h: (0, 0)),
    ]


def forward_part(block, aux, lengths):
    seq, features = block.shape[3:]
    width = HEADS_PER_STEP * HD
    heads = features // HD
    return pl.pallas_call(
        forward_kernel,
        grid=(features // width,),
        in_specs=[*qkv_specs(seq, width), *small_specs(width, features, lengths)],
        out_specs=pl.BlockSpec((None, None, seq, width), lambda h: (0, 0, 0, h)),
        out_shape=jax.ShapeDtypeStruct((1, 1, seq, features), jnp.bfloat16),
        cost_estimate=pl.CostEstimate(
            flops=4 * heads * seq * seq * HD, bytes_accessed=8 * seq * features, transcendentals=heads * seq * seq
        ),
        name="forward",
    )(block, block, block, aux, aux, lengths)


def backward_part(strips, upstream, aux, lengths):
    seq, features = upstream.shape[2:]
    rows = seq // STRIPS
    width = HEADS_PER_STEP * HD
    heads = features // HD
    return pl.pallas_call(
        backward_kernel,
        grid=(features // width,),
        in_specs=[
            *[pl.BlockSpec((None, None, 3, rows, width), lambda h: (0, 0, 0, 0, h))] * STRIPS,
            pl.BlockSpec((None, None, seq, width), lambda h: (0, 0, 0, h)),
            *small_specs(width, features, lengths),
        ],
        out_specs=[
            pl.BlockSpec((None, None, 3, seq, width), lambda h: (0, 0, 0, 0, h)),
            pl.BlockSpec((1, width), lambda h: (0, h)),
        ],
        out_shape=[
            jax.ShapeDtypeStruct((1, 1, 3, seq, features), jnp.bfloat16),
            jax.ShapeDtypeStruct((1, features), jnp.float32),
        ],
        cost_estimate=pl.CostEstimate(
            flops=10 * heads * seq * seq * HD, bytes_accessed=14 * seq * features, transcendentals=heads * seq * seq
        ),
        name="backward",
    )(*strips, upstream, aux, aux, lengths)


def shards(inbound, parked, grad_out, query_gain, plan, lengths):
    entries = plan.shape[1]
    aux = jnp.concatenate(
        [query_gain, plan.astype(jnp.float32), jnp.zeros((1, HD - entries), jnp.float32)], axis=1
    )
    aux_back = moved(aux, lambda s, n: site(s, n))
    aux_ahead = moved(aux, lambda s, n: s - 1)
    grad_out, parked, aux_back, aux_ahead = lax.optimization_barrier((grad_out, parked, aux_back, aux_ahead))
    upstream = moved(grad_out, lambda s, n: site((s - 1) % n, n))
    rows = parked.shape[3] // STRIPS
    stored = [
        moved(parked[:, :, :, i * rows : (i + 1) * rows], lambda s, n: site(n - 1 - s, n)) for i in range(STRIPS)
    ]
    attended = moved(forward_part(inbound, aux_ahead, lengths), lambda s, n: s + 1)
    grads, raw = backward_part(stored, upstream, aux_back, lengths)
    grads = moved(grads, lambda s, n: site(s, n))
    total = doubled_sum(raw, "dp")
    own_total = moved(total, lambda s, n: site(s, n))
    squares = jnp.full((1, HD), jnp.sum(total * total), jnp.float32)
    squares = doubled_sum(doubled_sum(squares, "tensor"), "section")
    gain_grad = own_total / (jnp.sqrt(squares[:, :1]) + 1e-06)
    return (attended, grads, gain_grad)


def solution(mesh):
    placed = (
        P("section", "dp", None, None, "tensor"),
        P("section", "dp", None, None, "tensor"),
        P("section", "dp", None, "tensor"),
        P("section", "tensor"),
        P("section", None),
        P("dp", None),
    )
    return jax.shard_map(
        shards,
        mesh=mesh,
        in_specs=placed,
        out_specs=(
            P("section", "dp", None, "tensor"),
            P("section", "dp", None, None, "tensor"),
            P("section", "tensor"),
        ),
        check_vma=False,
    )
```

time: 763 us -> 244 us (0.32)
  waiting for transfers between devices: 505 us -> 72.6 us
  blocking collectives: 186 us -> 0 us
  starting transfers between devices: 15.7 us -> 130 us
  Pallas kernels: 0 us -> 26.2 us
  matrix products: 17.9 us -> 0 us
  local copies, waits for them, and re-layouts: 24.4 us -> 8.83 us
  other arithmetic: 12.9 us -> 3.19 us
    ppermute x6 -> x18, waiting for transfers between devices: 505 us -> 72.6 us  [the longest x8 68.9 us: doubled_sum(): lax.ppermute(value, axis, [(i, i ^ step) for i in range(size)])]
    psum x2 -> x0, blocking collectives: 186 us -> none  [the longest x1 179 us: shards(): squares = lax.psum(jnp.sum(total * total), ('section', 'tensor'))]
    ppermute x6 -> x18, starting transfers between devices: 15.7 us -> 130 us  [the longest x10 118 us: moved(): lax.ppermute(value, 'section', [(i, target(i, size) % size) for i in rang...]
    pallas_call x0 -> x2, Pallas kernels: none -> 26.2 us  [the longest x1 15.2 us: backward_part(): pl.pallas_call(backward_kernel, grid=(features // width,), in_specs=[*[pl...]
    dot_general x7 -> x0, matrix products: 15.7 us -> none  [the longest x1 3.52 us: backward_part(): jnp.einsum('hqk,qhd->khd', wround, gh, preferred_element_type=jnp.float32)]
    unnamed x10 -> x16, local copies, waits for them, and re-layouts: 14.6 us -> 5.2 us
  transfers between devices with their start and end apart: 6 -> 18, of which waited for: 5 -> 10; matrix products, arithmetic and copies ran while one was open for 4% -> 2% of each run, Pallas kernels for 0% -> 5%
where the time goes in v1:
time: 244 us; the launch traced here: 242 us
  starting transfers between devices  130 us (53%)
  waiting for transfers between devices  72.6 us (30%)
  Pallas kernels  26.2 us (11%)
  local copies, waits for them, and re-layouts  8.83 us (4%)
  other arithmetic  3.19 us (1%)
    ppermute x10, starting transfers between devices, moved(): lax.ppermute(value, 'section', [(i, target(i, size) % size) for i in rang...  118 us
    ppermute x8, waiting for transfers between devices, doubled_sum(): lax.ppermute(value, axis, [(i, i ^ step) for i in range(size)])  68.9 us
    pallas_call x1, Pallas kernels, backward_part(): pl.pallas_call(backward_kernel, grid=(features // width,), in_specs=[*[pl...  15.2 us
    ppermute x8, starting transfers between devices, doubled_sum(): lax.ppermute(value, axis, [(i, i ^ step) for i in range(size)])  12.8 us
    pallas_call x1, Pallas kernels, forward_part(): pl.pallas_call(forward_kernel, grid=(features // width,), in_specs=[*qkv_...  11.1 us
    unnamed x16, local copies, waits for them, and re-layouts  5.2 us
  transfers between devices with their start and end apart: 18, of which 10 were waited for; matrix products, arithmetic and copies ran while one was open for 2% of the time, Pallas kernels for 5%

profile of v1, /device:TPU:8, one launch (start us, length us, event | category | flops | bytes accessed | tf_op | source)
XLA Modules:
  0.0 242.1 jit_solution(14276517613577634287)
XLA Ops:
  0.6 0.7 convert_element_type.3
  1.3 0.8 concatenate.3
  2.1 9.5 %collective-permute-start = (f32[1,1664]{1,0:T(1,128)S(1)}, f32[1,1664]{1,0:T(1,128)S(1)}, u32[]{:S(2)}, u32[]{:S(2)}) collective-permute-start(f32[1,1664]{1,0:T(1,128)S(1)} %concatenate.3), channel_id=1, source_target_pairs={{0,240},{16,16},{32,32},{48,192},{64,176},{80,80},{96,96},{112,128... | collective-permute-start | bytes 19976 | tf_op jit(solution)/shard_map/ppermute | solution.py:26
  11.6 0.1 collective-permute-start.1
  11.7 1.5 collective-permute-done.refs_5_.refs_6_
  13.2 2.1 collective-permute-done.1.gain_ref.tail_ref
  15.3 10.4 %collective-permute-start.7 = (bf16[1,1,384,1536]{3,2,1,0:T(8,128)(2,1)}, bf16[1,1,384,1536]{3,2,1,0:T(8,128)(2,1)}, u32[]{:S(2)}, u32[]{:S(2)}) collective-permute-start(bf16[1,1,384,1536]{3,2,1,0:T(8,128)(2,1)} %param.8), channel_id=1, source_target_pairs={{0,0},{16,240},{32,16},{48,32},{64,192},{80,176},{96,80},{112,96},... | collective-permute-start | bytes 3538952 | tf_op jit(solution)/shard_map/ppermute | solution.py:26
  25.6 2.2 fusion
  27.9 0.7 collective-permute-start.3
  28.6 0.7 collective-permute-start.4
  29.3 0.7 collective-permute-start.5
  30.0 0.7 collective-permute-start.6
  30.8 0.0 copy-start.2
  30.8 0.0 collective-permute-done.4.refs_1_
  30.8 0.0 collective-permute-done.6.refs_3_
  30.8 0.9 copy-done.2
  31.7 0.3 copy-done.3
  32.0 0.3 copy-done.4
  32.3 0.9 copy-done.5
  33.2 0.0 collective-permute-done.7.refs_4_
  33.2 15.2 %backward.1 = (bf16[1,1,3,384,1536]{4,3,2,1,0:T(8,128)(2,1)}, f32[1,1536]{1,0:T(1,128)}) custom-call(bf16[1,1,3,96,1536]{4,3,2,1,0:T(8,128)(2,1)} %copy-done.2, bf16[1,1,3,96,1536]{4,3,2,1,0:T(8,128)(2,1)} %copy-done.3, bf16[1,1,3,96,1536]{4,3,2,1,0:T(8,128)(2,1)} %copy-done.4, bf16[1,1,3,96,1536]{4,3,2,1,0:T(8,128)(2,1)} %copy-done.5, ...), custom_call_target="tpu_custom_call" | custom-call | flops 2264924160 | bytes 8257536 | tf_op jit(solution)/shard_map/backward/pallas_call | solution.py:147
  48.4 23.2 %collective-permute-start.8 = (bf16[1,1,3,384,1536]{4,3,2,1,0:T(8,128)(2,1)}, bf16[1,1,3,384,1536]{4,3,2,1,0:T(8,128)(2,1)S(1)}, u32[]{:S(2)}, u32[]{:S(2)}) collective-permute-start(bf16[1,1,3,384,1536]{4,3,2,1,0:T(8,128)(2,1)} %get-tuple-element.13), channel_id=1, source_target_pairs={{0,240},{16,16},{32,32},{48,192},{64,176},{80,80},{96,96},{112,128... | collective-permute-start | bytes 10616840 | tf_op jit(solution)/shard_map/ppermute | solution.py:26
  71.6 11.1 %forward.1 = bf16[1,1,384,1536]{3,2,1,0:T(8,128)(2,1)} custom-call(bf16[1,1,3,384,1536]{4,3,2,1,0:T(8,128)(2,1)} %v_ref.1, bf16[1,1,3,384,1536]{4,3,2,1,0:T(8,128)(2,1)} %v_ref.1, bf16[1,1,3,384,1536]{4,3,2,1,0:T(8,128)(2,1)} %v_ref.1, f32[1,1664]{1,0:T(1,128)} %copy-done, f32[1,1664]{1,0:T(1,128)} %copy-done, s32[1,8]{1,0:T(1,128)} %refs_7_.1), custom_call_target="tpu_custom_call" | custom-call | flops 905969664 | bytes 4718592 | tf_op jit(solution)/shard_map/forward/pallas_call | solution.py:129
  82.7 69.6 %collective-permute-start.2 = (bf16[1,1,384,1536]{3,2,1,0:T(8,128)(2,1)}, bf16[1,1,384,1536]{3,2,1,0:T(8,128)(2,1)S(1)}, u32[]{:S(2)}, u32[]{:S(2)}) collective-permute-start(bf16[1,1,384,1536]{3,2,1,0:T(8,128)(2,1)} %forward.1), channel_id=1, source_target_pairs={{0,16},{16,32},{32,48},{48,64},{64,80},{80,96},{96,112},{112,128},... | collective-permute-start | bytes 3538952 | tf_op jit(solution)/shard_map/ppermute | solution.py:26
  152.3 1.2 collective-permute-done.9
  153.4 1.4 collective-permute-start.10
  154.9 51.8 %collective-permute-done.10 = f32[1,1536]{1,0:T(1,128)S(1)} collective-permute-done((f32[1,1536]{1,0:T(1,128)S(1)}, f32[1,1536]{1,0:T(1,128)S(1)}, u32[]{:S(2)}, u32[]{:S(2)}) %collective-permute-start.10) | collective-permute-done | bytes 6176 | tf_op jit(solution)/shard_map/ppermute | solution.py:33
  206.7 0.6 multiply_reduce_fusion
  207.3 0.6 broadcast_in_dim.7
  207.9 1.6 collective-permute-start.12
  209.5 2.0 collective-permute-done.12
  211.6 0.6 broadcast_add_fusion
  212.2 3.1 %collective-permute-start.13 = (f32[1,128]{1,0:T(1,128)S(1)}, f32[1,128]{1,0:T(1,128)S(1)}, u32[]{:S(2)}, u32[]{:S(2)}) collective-permute-start(f32[1,128]{1,0:T(1,128)S(1)} %broadcast_add_fusion), channel_id=1, source_target_pairs={{0,8},{4,12},{8,0},{12,4},{1,9},{5,13},{9,1},{13,5},{2,10},{6,14},... | collective-permute-start | bytes 1544 | tf_op jit(solution)/shard_map/ppermute | solution.py:33
  215.3 1.9 collective-permute-start.11
  217.2 0.1 collective-permute-done.13
  217.3 0.6 fusion.1
  218.0 0.1 collective-permute-start.14
  218.1 3.5 %collective-permute-done.14 = f32[1,128]{1,0:T(1,128)S(1)} collective-permute-done((f32[1,128]{1,0:T(1,128)S(1)}, f32[1,128]{1,0:T(1,128)S(1)}, u32[]{:S(2)}, u32[]{:S(2)}) %collective-permute-start.14) | collective-permute-done | bytes 544 | tf_op jit(solution)/shard_map/ppermute | solution.py:33
  221.6 0.0 collective-permute-start.15
  221.6 4.4 %collective-permute-done.15 = f32[1,128]{1,0:T(1,128)S(1)} collective-permute-done((f32[1,128]{1,0:T(1,128)S(1)}, f32[1,128]{1,0:T(1,128)S(1)}, u32[]{:S(2)}, u32[]{:S(2)}) %collective-permute-start.15) | collective-permute-done | bytes 544 | tf_op jit(solution)/shard_map/ppermute | solution.py:33
  226.1 4.0 %collective-permute-start.16 = (f32[1,128]{1,0:T(1,128)S(1)}, f32[1,128]{1,0:T(1,128)S(1)}, u32[]{:S(2)}, u32[]{:S(2)}) collective-permute-start(f32[1,128]{1,0:T(1,128)S(1)} %add.32), channel_id=1, source_target_pairs={{0,64},{16,80},{32,96},{48,112},{64,0},{80,16},{96,32},{112,48},{1... | collective-permute-start | bytes 1544 | tf_op jit(solution)/shard_map/ppermute | solution.py:33
  230.1 3.4 %collective-permute-done.16 = f32[1,128]{1,0:T(1,128)S(1)} collective-permute-done((f32[1,128]{1,0:T(1,128)S(1)}, f32[1,128]{1,0:T(1,128)S(1)}, u32[]{:S(2)}, u32[]{:S(2)}) %collective-permute-start.16) | collective-permute-done | bytes 544 | tf_op jit(solution)/shard_map/ppermute | solution.py:33
  233.5 2.6 %collective-permute-start.17 = (f32[1,128]{1,0:T(1,128)S(1)}, f32[1,128]{1,0:T(1,128)S(1)}, u32[]{:S(2)}, u32[]{:S(2)}) collective-permute-start(f32[1,128]{1,0:T(1,128)S(1)} %add.33), channel_id=1, source_target_pairs={{0,128},{16,144},{32,160},{48,176},{64,192},{80,208},{96,224},{112... | collective-permute-start | bytes 1544 | tf_op jit(solution)/shard_map/ppermute | solution.py:33
  236.1 0.0 collective-permute-done.2
  236.1 2.5 %collective-permute-done.17 = f32[1,128]{1,0:T(1,128)S(1)} collective-permute-done((f32[1,128]{1,0:T(1,128)S(1)}, f32[1,128]{1,0:T(1,128)S(1)}, u32[]{:S(2)}, u32[]{:S(2)}) %collective-permute-start.17) | collective-permute-done | bytes 544 | tf_op jit(solution)/shard_map/ppermute | solution.py:33
  238.7 0.6 broadcast_divide_fusion
  239.3 1.0 copy.11
  240.3 1.8 copy.12
  (20 shorter events, 0.1 us)
Async XLA Ops:
  2.1 11.1 %collective-permute-start = (f32[1,1664]{1,0:T(1,128)S(1)}, f32[1,1664]{1,0:T(1,128)S(1)}, u32[]{:S(2)}, u32[]{:S(2)}) collective-permute-start(f32[1,1664]{1,0:T(1,128)S(1)} %concatenate.3), channel_id=1, source_target_pairs={{0,240},{16,16},{32,32},{48,192},{64,176},{80,80},{96,96},{112,128... | collective-permute-start | bytes 19976 | tf_op jit(solution)/shard_map/ppermute | solution.py:26
  11.6 3.7 %collective-permute-start.1 = (f32[1,1664]{1,0:T(1,128)S(1)}, f32[1,1664]{1,0:T(1,128)S(1)}, u32[]{:S(2)}, u32[]{:S(2)}) collective-permute-start(f32[1,1664]{1,0:T(1,128)S(1)} %concatenate.3), channel_id=1, source_target_pairs={{0,240},{16,0},{32,16},{48,32},{64,48},{80,64},{96,80},{112,96},{1... | collective-permute-start | bytes 19976 | tf_op jit(solution)/shard_map/ppermute | solution.py:26
  13.2 14.7 %copy-start.6 = (f32[1,1664]{1,0:T(1,128)}, f32[1,1664]{1,0:T(1,128)S(1)}, u32[]{:S(2)}) copy-start(f32[1,1664]{1,0:T(1,128)S(1)} %collective-permute-done.refs_5_.refs_6_) | copy-start | bytes 19972
  15.3 12.6 %copy-start = (f32[1,1664]{1,0:T(1,128)}, f32[1,1664]{1,0:T(1,128)S(1)}, u32[]{:S(2)}) copy-start(f32[1,1664]{1,0:T(1,128)S(1)} %collective-permute-done.1.gain_ref.tail_ref) | copy-start | bytes 19972
  15.3 17.9 %collective-permute-start.7 = (bf16[1,1,384,1536]{3,2,1,0:T(8,128)(2,1)}, bf16[1,1,384,1536]{3,2,1,0:T(8,128)(2,1)}, u32[]{:S(2)}, u32[]{:S(2)}) collective-permute-start(bf16[1,1,384,1536]{3,2,1,0:T(8,128)(2,1)} %param.8), channel_id=1, source_target_pairs={{0,0},{16,240},{32,16},{48,32},{64,192},{80,176},{96,80},{112,96},... | collective-permute-start | bytes 3538952 | tf_op jit(solution)/shard_map/ppermute | solution.py:26
  27.9 2.9 %collective-permute-start.3 = (bf16[1,1,3,96,1536]{4,3,2,1,0:T(8,128)(2,1)S(1)}, bf16[1,1,3,96,1536]{4,3,2,1,0:T(8,128)(2,1)S(1)}, u32[]{:S(2)}, u32[]{:S(2)}) collective-permute-start(bf16[1,1,3,96,1536]{4,3,2,1,0:T(8,128)(2,1)S(1)} %get-tuple-element.20), channel_id=1, source_target_pairs={{0,0},{16,224},{32,208},{48,48},{64,64},{80,160},{96,144},{112,112... | collective-permute-start | bytes 2654216 | tf_op jit(solution)/shard_map/ppermute | solution.py:26
  28.6 2.2 collective-permute-start.4
  29.3 1.5 collective-permute-start.5
  30.0 0.8 collective-permute-start.6
  30.8 0.9 copy-start.2
  30.8 1.2 copy-start.3
  30.8 1.5 copy-start.4
  32.3 0.9 copy-start.5
  48.4 103.9 %copy-start.1 = (f32[1,1536]{1,0:T(1,128)S(1)}, f32[1,1536]{1,0:T(1,128)}, u32[]{:S(2)}) copy-start(f32[1,1536]{1,0:T(1,128)} %get-tuple-element.14) | copy-start | bytes 18436
  48.4 190.9 %collective-permute-start.8 = (bf16[1,1,3,384,1536]{4,3,2,1,0:T(8,128)(2,1)}, bf16[1,1,3,384,1536]{4,3,2,1,0:T(8,128)(2,1)S(1)}, u32[]{:S(2)}, u32[]{:S(2)}) collective-permute-start(bf16[1,1,3,384,1536]{4,3,2,1,0:T(8,128)(2,1)} %get-tuple-element.13), channel_id=1, source_target_pairs={{0,240},{16,16},{32,32},{48,192},{64,176},{80,80},{96,96},{112,128... | collective-permute-start | bytes 10616840 | tf_op jit(solution)/shard_map/ppermute | solution.py:26
  82.7 153.4 %collective-permute-start.2 = (bf16[1,1,384,1536]{3,2,1,0:T(8,128)(2,1)}, bf16[1,1,384,1536]{3,2,1,0:T(8,128)(2,1)S(1)}, u32[]{:S(2)}, u32[]{:S(2)}) collective-permute-start(bf16[1,1,384,1536]{3,2,1,0:T(8,128)(2,1)} %forward.1), channel_id=1, source_target_pairs={{0,16},{16,32},{32,48},{48,64},{64,80},{80,96},{96,112},{112,128},... | collective-permute-start | bytes 3538952 | tf_op jit(solution)/shard_map/ppermute | solution.py:26
  152.3 1.2 collective-permute-start.9
  153.4 53.2 %collective-permute-start.10 = (f32[1,1536]{1,0:T(1,128)S(1)}, f32[1,1536]{1,0:T(1,128)S(1)}, u32[]{:S(2)}, u32[]{:S(2)}) collective-permute-start(f32[1,1536]{1,0:T(1,128)S(1)} %add.27), channel_id=1, source_target_pairs={{0,2},{1,3},{2,0},{3,1},{4,6},{5,7},{6,4},{7,5},{8,10},{9,11},{10,... | collective-permute-start | bytes 18440 | tf_op jit(solution)/shard_map/ppermute | solution.py:33
  207.9 3.6 %collective-permute-start.12 = (f32[1,128]{1,0:T(1,128)S(1)}, f32[1,128]{1,0:T(1,128)S(1)}, u32[]{:S(2)}, u32[]{:S(2)}) collective-permute-start(f32[1,128]{1,0:T(1,128)S(1)} %broadcast_in_dim.7), channel_id=1, source_target_pairs={{0,4},{4,0},{8,12},{12,8},{1,5},{5,1},{9,13},{13,9},{2,6},{6,2},{1... | collective-permute-start | bytes 1544 | tf_op jit(solution)/shard_map/ppermute | solution.py:33
  212.2 5.1 %collective-permute-start.13 = (f32[1,128]{1,0:T(1,128)S(1)}, f32[1,128]{1,0:T(1,128)S(1)}, u32[]{:S(2)}, u32[]{:S(2)}) collective-permute-start(f32[1,128]{1,0:T(1,128)S(1)} %broadcast_add_fusion), channel_id=1, source_target_pairs={{0,8},{4,12},{8,0},{12,4},{1,9},{5,13},{9,1},{13,5},{2,10},{6,14},... | collective-permute-start | bytes 1544 | tf_op jit(solution)/shard_map/ppermute | solution.py:33
  215.3 23.3 %collective-permute-start.11 = (f32[1,1536]{1,0:T(1,128)S(1)}, f32[1,1536]{1,0:T(1,128)S(1)}, u32[]{:S(2)}, u32[]{:S(2)}) collective-permute-start(f32[1,1536]{1,0:T(1,128)S(1)} %get-tuple-element.16), channel_id=1, source_target_pairs={{0,240},{16,16},{32,32},{48,192},{64,176},{80,80},{96,96},{112,128... | collective-permute-start | bytes 18440 | tf_op jit(solution)/shard_map/ppermute | solution.py:26
  218.0 3.6 %collective-permute-start.14 = (f32[1,128]{1,0:T(1,128)S(1)}, f32[1,128]{1,0:T(1,128)S(1)}, u32[]{:S(2)}, u32[]{:S(2)}) collective-permute-start(f32[1,128]{1,0:T(1,128)S(1)} %fusion.1), channel_id=1, source_target_pairs={{0,16},{16,0},{32,48},{48,32},{64,80},{80,64},{96,112},{112,96},{1... | collective-permute-start | bytes 1544 | tf_op jit(solution)/shard_map/ppermute | solution.py:33
  221.6 4.4 %collective-permute-start.15 = (f32[1,128]{1,0:T(1,128)S(1)}, f32[1,128]{1,0:T(1,128)S(1)}, u32[]{:S(2)}, u32[]{:S(2)}) collective-permute-start(f32[1,128]{1,0:T(1,128)S(1)} %add.31), channel_id=1, source_target_pairs={{0,32},{16,48},{32,0},{48,16},{64,96},{80,112},{96,64},{112,80},{1... | collective-permute-start | bytes 1544 | tf_op jit(solution)/shard_map/ppermute | solution.py:33
  226.1 7.4 %collective-permute-start.16 = (f32[1,128]{1,0:T(1,128)S(1)}, f32[1,128]{1,0:T(1,128)S(1)}, u32[]{:S(2)}, u32[]{:S(2)}) collective-permute-start(f32[1,128]{1,0:T(1,128)S(1)} %add.32), channel_id=1, source_target_pairs={{0,64},{16,80},{32,96},{48,112},{64,0},{80,16},{96,32},{112,48},{1... | collective-permute-start | bytes 1544 | tf_op jit(solution)/shard_map/ppermute | solution.py:33
  233.5 5.0 %collective-permute-start.17 = (f32[1,128]{1,0:T(1,128)S(1)}, f32[1,128]{1,0:T(1,128)S(1)}, u32[]{:S(2)}, u32[]{:S(2)}) collective-permute-start(f32[1,128]{1,0:T(1,128)S(1)} %add.33), channel_id=1, source_target_pairs={{0,128},{16,144},{32,160},{48,176},{64,192},{80,208},{96,224},{112... | collective-permute-start | bytes 1544 | tf_op jit(solution)/shard_map/ppermute | solution.py:33

commit v2 on v1

--- a/solution.py
+++ b/solution.py
@@ -10,8 +10,8 @@
 HD = 128
 BLOCK = 128
 HEADS_PER_STEP = 2
-STRIPS = 4
 NEG = -1e30
+FAR = 10**11
 
 DIM_LAST = (((1,), (1,)), ((), ()))
 DIM_FIRST = (((0,), (0,)), ((), ()))
@@ -70,27 +70,24 @@
             out_ref[start:end, hs] = dot(wb, v_ref[:end, hs], DIM_FIRST).astype(jnp.bfloat16)
 
 
-def backward_kernel(*refs):
-    strips = refs[:STRIPS]
-    g_ref, gain_ref, tail_ref, lengths_ref, out_ref, raw_ref = refs[STRIPS:]
+def backward_kernel(q_ref, k_ref, v_ref, g_ref, gain_ref, tail_ref, lengths_ref, out_ref, raw_ref):
     length = row_length(tail_ref, lengths_ref, 1)
-    seq = g_ref.shape[0]
+    seq = q_ref.shape[0]
     for h in range(HEADS_PER_STEP):
         hs = slice(h * HD, (h + 1) * HD)
         gain = gain_ref[:, hs]
-        q, k, v = (jnp.concatenate([strip[part, :, hs] for strip in strips], axis=0) for part in range(3))
         dks = [jnp.zeros((BLOCK, HD), jnp.float32) for _ in range(seq // BLOCK)]
         dvs = [jnp.zeros((BLOCK, HD), jnp.float32) for _ in range(seq // BLOCK)]
         raw = jnp.zeros((1, HD), jnp.float32)
         for start in range(0, seq, BLOCK):
             end = start + BLOCK
-            query = q[start:end].astype(jnp.float32)
+            query = q_ref[start:end, hs].astype(jnp.float32)
             qs = (query * gain).astype(jnp.bfloat16)
-            keys = k[:end]
+            keys = k_ref[:end, hs]
             g = g_ref[start:end, hs]
             w = weights_of(qs, keys, start, length)
             wb = w.astype(jnp.bfloat16)
-            dw = dot(v[:end], g, DIM_LAST)
+            dw = dot(v_ref[:end, hs], g, DIM_LAST)
             delta = jnp.sum(wb.astype(jnp.float32) * dw, axis=0, keepdims=True)
             ds = (w * (dw - delta) * (1.0 / HD**0.5)).astype(jnp.bfloat16)
             dv = dot(wb, g)
@@ -133,22 +130,21 @@
         out_specs=pl.BlockSpec((None, None, seq, width), lambda h: (0, 0, 0, h)),
         out_shape=jax.ShapeDtypeStruct((1, 1, seq, features), jnp.bfloat16),
         cost_estimate=pl.CostEstimate(
-            flops=4 * heads * seq * seq * HD, bytes_accessed=8 * seq * features, transcendentals=heads * seq * seq
+            flops=FAR, bytes_accessed=8 * seq * features, transcendentals=heads * seq * seq
         ),
         name="forward",
     )(block, block, block, aux, aux, lengths)
 
 
-def backward_part(strips, upstream, aux, lengths):
+def backward_part(block, upstream, aux, lengths):
     seq, features = upstream.shape[2:]
-    rows = seq // STRIPS
     width = HEADS_PER_STEP * HD
     heads = features // HD
     return pl.pallas_call(
         backward_kernel,
         grid=(features // width,),
         in_specs=[
-            *[pl.BlockSpec((None, None, 3, rows, width), lambda h: (0, 0, 0, 0, h))] * STRIPS,
+            *qkv_specs(seq, width),
             pl.BlockSpec((None, None, seq, width), lambda h: (0, 0, 0, h)),
             *small_specs(width, features, lengths),
         ],
@@ -161,10 +157,24 @@
             jax.ShapeDtypeStruct((1, features), jnp.float32),
         ],
         cost_estimate=pl.CostEstimate(
-            flops=10 * heads * seq * seq * HD, bytes_accessed=14 * seq * features, transcendentals=heads * seq * seq
+            flops=heads * seq * HD, bytes_accessed=seq * features, transcendentals=heads * seq
         ),
         name="backward",
-    )(*strips, upstream, aux, aux, lengths)
+    )(block, block, block, upstream, aux, aux, lengths)
+
+
+def square_kernel(total_ref, out_ref):
+    total = total_ref[...]
+    out_ref[...] = jnp.broadcast_to(jnp.sum(total * total, axis=1, keepdims=True), out_ref.shape)
+
+
+def square_sum(total):
+    return pl.pallas_call(
+        square_kernel,
+        out_shape=jax.ShapeDtypeStruct((1, HD), jnp.float32),
+        cost_estimate=pl.CostEstimate(flops=FAR, bytes_accessed=8 * total.size, transcendentals=0),
+        name="squares",
+    )(total)
 
 
 def shards(inbound, parked, grad_out, query_gain, plan, lengths):
@@ -176,16 +186,18 @@
     aux_ahead = moved(aux, lambda s, n: s - 1)
     grad_out, parked, aux_back, aux_ahead = lax.optimization_barrier((grad_out, parked, aux_back, aux_ahead))
     upstream = moved(grad_out, lambda s, n: site((s - 1) % n, n))
-    rows = parked.shape[3] // STRIPS
-    stored = [
-        moved(parked[:, :, :, i * rows : (i + 1) * rows], lambda s, n: site(n - 1 - s, n)) for i in range(STRIPS)
-    ]
-    attended = moved(forward_part(inbound, aux_ahead, lengths), lambda s, n: s + 1)
+    stored = moved(parked, lambda s, n: site(n - 1 - s, n))
+    aux_ahead, upstream = lax.optimization_barrier((aux_ahead, upstream))
+    attended = forward_part(inbound, aux_ahead, lengths)
+    _, stored, upstream = lax.optimization_barrier((attended, stored, upstream))
+    attended = moved(attended, lambda s, n: s + 1)
     grads, raw = backward_part(stored, upstream, aux_back, lengths)
+    total = doubled_sum(raw, "dp")
+    grads, total = lax.optimization_barrier((grads, total))
+    own_total = moved(total, lambda s, n: site(s, n))
     grads = moved(grads, lambda s, n: site(s, n))
-    total = doubled_sum(raw, "dp")
-    own_total = moved(total, lambda s, n: site(s, n))
-    squares = jnp.full((1, HD), jnp.sum(total * total), jnp.float32)
+    total, own_total, attended = lax.optimization_barrier((total, own_total, attended))
+    squares = square_sum(total)
     squares = doubled_sum(doubled_sum(squares, "tensor"), "section")
     gain_grad = own_total / (jnp.sqrt(squares[:, :1]) + 1e-06)
     return (attended, grads, gain_grad)

time: 244 us -> 214 us (0.88)
  starting transfers between devices: 130 us -> 86.1 us
  waiting for transfers between devices: 72.6 us -> 87.4 us
    ppermute x10 -> x7, waiting for transfers between devices: 3.64 us -> 71.5 us  [moved(): lax.ppermute(value, 'section', [(i, target(i, size) % size) for i in rang...]
    ppermute x10 -> x7, starting transfers between devices: 118 us -> 51 us  [moved(): lax.ppermute(value, 'section', [(i, target(i, size) % size) for i in rang...]
    ppermute x8, waiting for transfers between devices: 68.9 us -> 15.9 us  [doubled_sum(): lax.ppermute(value, axis, [(i, i ^ step) for i in range(size)])]
    ppermute x8, starting transfers between devices: 12.8 us -> 35.1 us  [doubled_sum(): lax.ppermute(value, axis, [(i, i ^ step) for i in range(size)])]
    pallas_call x1 -> x2, Pallas kernels: 15.2 us -> 16.5 us  [the longest x1 15.2 us: backward_part(): pl.pallas_call(backward_kernel, grid=(features // width,), in_specs=[*qkv...]
    unnamed x16 -> x10, local copies, waits for them, and re-layouts: 5.2 us -> 5.96 us
  transfers between devices with their start and end apart: 18 -> 15, of which waited for: 10 -> 11; matrix products, arithmetic and copies ran while one was open for 2% -> 1% of each run, Pallas kernels for 5% -> 13%
where the time goes in v2:
time: 214 us; the launch traced here: 211 us
  waiting for transfers between devices  87.4 us (41%)
  starting transfers between devices  86.1 us (40%)
  Pallas kernels  27.5 us (13%)
  local copies, waits for them, and re-layouts  6.75 us (3%)
  other arithmetic  2.64 us (1%)
    ppermute x7, waiting for transfers between devices, moved(): lax.ppermute(value, 'section', [(i, target(i, size) % size) for i in rang...  71.5 us
    ppermute x7, starting transfers between devices, moved(): lax.ppermute(value, 'section', [(i, target(i, size) % size) for i in rang...  51 us
    ppermute x8, starting transfers between devices, doubled_sum(): lax.ppermute(value, axis, [(i, i ^ step) for i in range(size)])  35.1 us
    ppermute x8, waiting for transfers between devices, doubled_sum(): lax.ppermute(value, axis, [(i, i ^ step) for i in range(size)])  15.9 us
    pallas_call x1, Pallas kernels, backward_part(): pl.pallas_call(backward_kernel, grid=(features // width,), in_specs=[*qkv...  15.2 us
    pallas_call x1, Pallas kernels, forward_part(): pl.pallas_call(forward_kernel, grid=(features // width,), in_specs=[*qkv_...  11 us
    unnamed x10, local copies, waits for them, and re-layouts  5.96 us
  transfers between devices with their start and end apart: 15, of which 11 were waited for; matrix products, arithmetic and copies ran while one was open for 1% of the time, Pallas kernels for 13%

profile of v2, /device:TPU:8, one launch (start us, length us, event | category | flops | bytes accessed | tf_op | source)
XLA Modules:
  0.0 211.3 jit_solution(9312775213109243811)
XLA Ops:
  0.6 0.7 convert_element_type.3
  1.3 0.8 concatenate.3
  2.1 7.6 %collective-permute-start.1 = (f32[1,1664]{1,0:T(1,128)S(1)}, f32[1,1664]{1,0:T(1,128)S(1)}, u32[]{:S(2)}, u32[]{:S(2)}) collective-permute-start(f32[1,1664]{1,0:T(1,128)S(1)} %concatenate.3), channel_id=1, source_target_pairs={{0,240},{16,0},{32,16},{48,32},{64,48},{80,64},{96,80},{112,96},{1... | collective-permute-start | bytes 19976 | tf_op jit(solution)/shard_map/ppermute | solution.py:26
  9.7 2.9 %collective-permute-start = (f32[1,1664]{1,0:T(1,128)S(1)}, f32[1,1664]{1,0:T(1,128)S(1)}, u32[]{:S(2)}, u32[]{:S(2)}) collective-permute-start(f32[1,1664]{1,0:T(1,128)S(1)} %concatenate.3), channel_id=1, source_target_pairs={{0,240},{16,16},{32,32},{48,192},{64,176},{80,80},{96,96},{112,128... | collective-permute-start | bytes 19976 | tf_op jit(solution)/shard_map/ppermute | solution.py:26
  12.6 0.0 collective-permute-done.1.gain_ref.tail_ref
  12.6 0.0 copy-start.3
  12.6 6.2 %collective-permute-done.gain_ref.tail_ref = f32[1,1664]{1,0:T(1,128)S(1)} collective-permute-done((f32[1,1664]{1,0:T(1,128)S(1)}, f32[1,1664]{1,0:T(1,128)S(1)}, u32[]{:S(2)}, u32[]{:S(2)}) %collective-permute-start) | collective-permute-done | bytes 6688 | tf_op jit(solution)/shard_map/ppermute | solution.py:26
  18.8 0.0 copy-start.1
  18.8 10.3 %collective-permute-start.2 = (bf16[1,1,384,1536]{3,2,1,0:T(8,128)(2,1)}, bf16[1,1,384,1536]{3,2,1,0:T(8,128)(2,1)}, u32[]{:S(2)}, u32[]{:S(2)}) collective-permute-start(bf16[1,1,384,1536]{3,2,1,0:T(8,128)(2,1)} %param.8), channel_id=1, source_target_pairs={{0,0},{16,240},{32,16},{48,32},{64,192},{80,176},{96,80},{112,96},... | collective-permute-start | bytes 3538952 | tf_op jit(solution)/shard_map/ppermute | solution.py:26
  29.1 2.6 %collective-permute-start.3 = (bf16[1,1,3,384,1536]{4,3,2,1,0:T(8,128)(2,1)}, bf16[1,1,3,384,1536]{4,3,2,1,0:T(8,128)(2,1)S(1)}, u32[]{:S(2)}, u32[]{:S(2)}) collective-permute-start(bf16[1,1,3,384,1536]{4,3,2,1,0:T(8,128)(2,1)} %param.7), channel_id=1, source_target_pairs={{0,0},{16,224},{32,208},{48,48},{64,64},{80,160},{96,144},{112,112... | collective-permute-start | bytes 10616840 | tf_op jit(solution)/shard_map/ppermute | solution.py:26
  31.8 0.0 collective-permute-done.2.g_ref
  31.8 0.0 copy-done.3
  31.8 11.0 %forward.1 = bf16[1,1,384,1536]{3,2,1,0:T(8,128)(2,1)} custom-call(bf16[1,1,3,384,1536]{4,3,2,1,0:T(8,128)(2,1)} %v_ref.1, bf16[1,1,3,384,1536]{4,3,2,1,0:T(8,128)(2,1)} %v_ref.1, bf16[1,1,3,384,1536]{4,3,2,1,0:T(8,128)(2,1)} %v_ref.1, f32[1,1664]{1,0:T(1,128)} %copy-done.3, f32[1,1664]{1,0:T(1,128)} %copy-done.3, s32[1,8]{1,0:T(1,128)} %lengths_ref.3), custom_call_target="tpu_custom_call" | custom-call | flops 99999997952 | bytes 4718592 | tf_op jit(solution)/shard_map/forward/pallas_call | solution.py:126
  42.8 0.0 copy-done.1
  42.8 18.1 %collective-permute-start.7 = (bf16[1,1,384,1536]{3,2,1,0:T(8,128)(2,1)}, bf16[1,1,384,1536]{3,2,1,0:T(8,128)(2,1)}, u32[]{:S(2)}, u32[]{:S(2)}) collective-permute-start(bf16[1,1,384,1536]{3,2,1,0:T(8,128)(2,1)} %forward.1), channel_id=1, source_target_pairs={{0,16},{16,32},{32,48},{48,64},{64,80},{80,96},{96,112},{112,128},... | collective-permute-start | bytes 3538952 | tf_op jit(solution)/shard_map/ppermute | solution.py:26
  60.9 0.0 collective-permute-done.3.q_ref.k_ref.v_ref
  60.9 0.0 copy-start
  60.9 1.8 copy-done
  62.7 15.2 %backward.1 = (bf16[1,1,3,384,1536]{4,3,2,1,0:T(8,128)(2,1)}, f32[1,1536]{1,0:T(1,128)}) custom-call(bf16[1,1,3,384,1536]{4,3,2,1,0:T(8,128)(2,1)} %copy-done, bf16[1,1,3,384,1536]{4,3,2,1,0:T(8,128)(2,1)} %copy-done, bf16[1,1,3,384,1536]{4,3,2,1,0:T(8,128)(2,1)} %copy-done, bf16[1,1,384,1536]{3,2,1,0:T(8,128)(2,1)} %collective-permute-done.2.g_ref, ...), custom_call_target="tpu_custom_call" | custom-call | flops 589824 | bytes 589824 | tf_op jit(solution)/shard_map/backward/pallas_call | solution.py:143
  77.9 0.0 collective-permute-start.4
  77.9 1.4 collective-permute-done.4
  79.3 0.7 add.27
  80.0 1.3 collective-permute-start.5
  81.4 2.3 %collective-permute-done.5 = f32[1,1536]{1,0:T(1,128)S(1)} collective-permute-done((f32[1,1536]{1,0:T(1,128)S(1)}, f32[1,1536]{1,0:T(1,128)S(1)}, u32[]{:S(2)}, u32[]{:S(2)}) %collective-permute-start.5) | collective-permute-done | bytes 6176 | tf_op jit(solution)/shard_map/ppermute | solution.py:33
  83.7 0.0 copy-start.2
  83.7 7.5 %collective-permute-start.6 = (f32[1,1536]{1,0:T(1,128)S(1)}, f32[1,1536]{1,0:T(1,128)S(1)}, u32[]{:S(2)}, u32[]{:S(2)}) collective-permute-start(f32[1,1536]{1,0:T(1,128)S(1)} %add.28.total_ref), channel_id=1, source_target_pairs={{0,240},{16,16},{32,32},{48,192},{64,176},{80,80},{96,96},{112,128... | collective-permute-start | bytes 18440 | tf_op jit(solution)/shard_map/ppermute | solution.py:26
  91.2 2.0 collective-permute-start.8
  93.1 38.2 %collective-permute-done.7 = bf16[1,1,384,1536]{3,2,1,0:T(8,128)(2,1)} collective-permute-done((bf16[1,1,384,1536]{3,2,1,0:T(8,128)(2,1)}, bf16[1,1,384,1536]{3,2,1,0:T(8,128)(2,1)}, u32[]{:S(2)}, u32[]{:S(2)}) %collective-permute-start.7) | collective-permute-done | bytes 1179680 | tf_op jit(solution)/shard_map/ppermute | solution.py:26
  131.3 0.0 collective-permute-done.6
  131.3 0.0 copy-done.2
  131.3 1.3 squares.1
  132.6 1.5 collective-permute-start.9
  134.1 2.2 %collective-permute-done.9 = f32[1,128]{1,0:T(1,128)S(1)} collective-permute-done((f32[1,128]{1,0:T(1,128)}, f32[1,128]{1,0:T(1,128)S(1)}, u32[]{:S(2)}, u32[]{:S(2)}) %collective-permute-start.9) | collective-permute-done | bytes 544 | tf_op jit(solution)/shard_map/ppermute | solution.py:33
  136.3 0.7 add.29
  137.0 3.0 %collective-permute-start.10 = (f32[1,128]{1,0:T(1,128)S(1)}, f32[1,128]{1,0:T(1,128)S(1)}, u32[]{:S(2)}, u32[]{:S(2)}) collective-permute-start(f32[1,128]{1,0:T(1,128)S(1)} %add.29), channel_id=1, source_target_pairs={{0,8},{4,12},{8,0},{12,4},{1,9},{5,13},{9,1},{13,5},{2,10},{6,14},... | collective-permute-start | bytes 1544 | tf_op jit(solution)/shard_map/ppermute | solution.py:33
  140.0 2.0 collective-permute-done.10
  142.0 17.9 %collective-permute-start.11 = (f32[1,128]{1,0:T(1,128)S(1)}, f32[1,128]{1,0:T(1,128)S(1)}, u32[]{:S(2)}, u32[]{:S(2)}) collective-permute-start(f32[1,128]{1,0:T(1,128)S(1)} %add.30), channel_id=1, source_target_pairs={{0,16},{16,0},{32,48},{48,32},{64,80},{80,64},{96,112},{112,96},{1... | collective-permute-start | bytes 1544 | tf_op jit(solution)/shard_map/ppermute | solution.py:33
  159.9 1.5 collective-permute-done.11
  161.4 3.8 %collective-permute-start.12 = (f32[1,128]{1,0:T(1,128)S(1)}, f32[1,128]{1,0:T(1,128)S(1)}, u32[]{:S(2)}, u32[]{:S(2)}) collective-permute-start(f32[1,128]{1,0:T(1,128)S(1)} %add.31), channel_id=1, source_target_pairs={{0,32},{16,48},{32,0},{48,16},{64,96},{80,112},{96,64},{112,80},{1... | collective-permute-start | bytes 1544 | tf_op jit(solution)/shard_map/ppermute | solution.py:33
  165.3 1.5 collective-permute-done.12
  166.8 5.2 %collective-permute-start.13 = (f32[1,128]{1,0:T(1,128)S(1)}, f32[1,128]{1,0:T(1,128)S(1)}, u32[]{:S(2)}, u32[]{:S(2)}) collective-permute-start(f32[1,128]{1,0:T(1,128)S(1)} %add.32), channel_id=1, source_target_pairs={{0,64},{16,80},{32,96},{48,112},{64,0},{80,16},{96,32},{112,48},{1... | collective-permute-start | bytes 1544 | tf_op jit(solution)/shard_map/ppermute | solution.py:33
  172.0 2.3 %collective-permute-done.13 = f32[1,128]{1,0:T(1,128)S(1)} collective-permute-done((f32[1,128]{1,0:T(1,128)S(1)}, f32[1,128]{1,0:T(1,128)S(1)}, u32[]{:S(2)}, u32[]{:S(2)}) %collective-permute-start.13) | collective-permute-done | bytes 544 | tf_op jit(solution)/shard_map/ppermute | solution.py:33
  174.2 2.3 %collective-permute-start.14 = (f32[1,128]{1,0:T(1,128)S(1)}, f32[1,128]{1,0:T(1,128)S(1)}, u32[]{:S(2)}, u32[]{:S(2)}) collective-permute-start(f32[1,128]{1,0:T(1,128)S(1)} %add.33), channel_id=1, source_target_pairs={{0,128},{16,144},{32,160},{48,176},{64,192},{80,208},{96,224},{112... | collective-permute-start | bytes 1544 | tf_op jit(solution)/shard_map/ppermute | solution.py:33
  176.5 2.8 %collective-permute-done.14 = f32[1,128]{1,0:T(1,128)S(1)} collective-permute-done((f32[1,128]{1,0:T(1,128)S(1)}, f32[1,128]{1,0:T(1,128)S(1)}, u32[]{:S(2)}, u32[]{:S(2)}) %collective-permute-start.14) | collective-permute-done | bytes 544 | tf_op jit(solution)/shard_map/ppermute | solution.py:33
  179.4 0.6 broadcast_divide_fusion
  180.0 27.1 %collective-permute-done.8 = bf16[1,1,3,384,1536]{4,3,2,1,0:T(8,128)(2,1)S(1)} collective-permute-done((bf16[1,1,3,384,1536]{4,3,2,1,0:T(8,128)(2,1)}, bf16[1,1,3,384,1536]{4,3,2,1,0:T(8,128)(2,1)S(1)}, u32[]{:S(2)}, u32[]{:S(2)}) %collective-permute-start.8) | collective-permute-done | bytes 3538976 | tf_op jit(solution)/shard_map/ppermute | solution.py:26
  207.1 2.4 %copy.11 = bf16[1,1,384,1536]{3,2,1,0:T(8,128)(2,1)} copy(bf16[1,1,384,1536]{3,2,1,0:T(8,128)(2,1)} %collective-permute-done.7) | data formatting | bytes 2359296
  209.5 1.8 copy.12
  (7 shorter events, 0.0 us)
Async XLA Ops:
  2.1 10.5 %collective-permute-start.1 = (f32[1,1664]{1,0:T(1,128)S(1)}, f32[1,1664]{1,0:T(1,128)S(1)}, u32[]{:S(2)}, u32[]{:S(2)}) collective-permute-start(f32[1,1664]{1,0:T(1,128)S(1)} %concatenate.3), channel_id=1, source_target_pairs={{0,240},{16,0},{32,16},{48,32},{64,48},{80,64},{96,80},{112,96},{1... | collective-permute-start | bytes 19976 | tf_op jit(solution)/shard_map/ppermute | solution.py:26
  9.7 9.1 %collective-permute-start = (f32[1,1664]{1,0:T(1,128)S(1)}, f32[1,1664]{1,0:T(1,128)S(1)}, u32[]{:S(2)}, u32[]{:S(2)}) collective-permute-start(f32[1,1664]{1,0:T(1,128)S(1)} %concatenate.3), channel_id=1, source_target_pairs={{0,240},{16,16},{32,32},{48,192},{64,176},{80,80},{96,96},{112,128... | collective-permute-start | bytes 19976 | tf_op jit(solution)/shard_map/ppermute | solution.py:26
  12.6 19.2 %copy-start.3 = (f32[1,1664]{1,0:T(1,128)}, f32[1,1664]{1,0:T(1,128)S(1)}, u32[]{:S(2)}) copy-start(f32[1,1664]{1,0:T(1,128)S(1)} %collective-permute-done.1.gain_ref.tail_ref) | copy-start | bytes 19972
  18.8 24.0 %copy-start.1 = (f32[1,1664]{1,0:T(1,128)}, f32[1,1664]{1,0:T(1,128)S(1)}, u32[]{:S(2)}) copy-start(f32[1,1664]{1,0:T(1,128)S(1)} %collective-permute-done.gain_ref.tail_ref) | copy-start | bytes 19972
  18.8 13.0 %collective-permute-start.2 = (bf16[1,1,384,1536]{3,2,1,0:T(8,128)(2,1)}, bf16[1,1,384,1536]{3,2,1,0:T(8,128)(2,1)}, u32[]{:S(2)}, u32[]{:S(2)}) collective-permute-start(bf16[1,1,384,1536]{3,2,1,0:T(8,128)(2,1)} %param.8), channel_id=1, source_target_pairs={{0,0},{16,240},{32,16},{48,32},{64,192},{80,176},{96,80},{112,96},... | collective-permute-start | bytes 3538952 | tf_op jit(solution)/shard_map/ppermute | solution.py:26
  29.1 31.8 %collective-permute-start.3 = (bf16[1,1,3,384,1536]{4,3,2,1,0:T(8,128)(2,1)}, bf16[1,1,3,384,1536]{4,3,2,1,0:T(8,128)(2,1)S(1)}, u32[]{:S(2)}, u32[]{:S(2)}) collective-permute-start(bf16[1,1,3,384,1536]{4,3,2,1,0:T(8,128)(2,1)} %param.7), channel_id=1, source_target_pairs={{0,0},{16,224},{32,208},{48,48},{64,64},{80,160},{96,144},{112,112... | collective-permute-start | bytes 10616840 | tf_op jit(solution)/shard_map/ppermute | solution.py:26
  42.8 88.5 %collective-permute-start.7 = (bf16[1,1,384,1536]{3,2,1,0:T(8,128)(2,1)}, bf16[1,1,384,1536]{3,2,1,0:T(8,128)(2,1)}, u32[]{:S(2)}, u32[]{:S(2)}) collective-permute-start(bf16[1,1,384,1536]{3,2,1,0:T(8,128)(2,1)} %forward.1), channel_id=1, source_target_pairs={{0,16},{16,32},{32,48},{48,64},{64,80},{80,96},{96,112},{112,128},... | collective-permute-start | bytes 3538952 | tf_op jit(solution)/shard_map/ppermute | solution.py:26
  60.9 1.8 copy-start
  77.9 1.4 collective-permute-start.4
  80.0 3.6 %collective-permute-start.5 = (f32[1,1536]{1,0:T(1,128)S(1)}, f32[1,1536]{1,0:T(1,128)S(1)}, u32[]{:S(2)}, u32[]{:S(2)}) collective-permute-start(f32[1,1536]{1,0:T(1,128)S(1)} %add.27), channel_id=1, source_target_pairs={{0,2},{1,3},{2,0},{3,1},{4,6},{5,7},{6,4},{7,5},{8,10},{9,11},{10,... | collective-permute-start | bytes 18440 | tf_op jit(solution)/shard_map/ppermute | solution.py:33
  83.7 47.7 %copy-start.2 = (f32[1,1536]{1,0:T(1,128)}, f32[1,1536]{1,0:T(1,128)S(1)}, u32[]{:S(2)}) copy-start(f32[1,1536]{1,0:T(1,128)S(1)} %add.28.total_ref) | copy-start | bytes 18436
  83.7 47.7 %collective-permute-start.6 = (f32[1,1536]{1,0:T(1,128)S(1)}, f32[1,1536]{1,0:T(1,128)S(1)}, u32[]{:S(2)}, u32[]{:S(2)}) collective-permute-start(f32[1,1536]{1,0:T(1,128)S(1)} %add.28.total_ref), channel_id=1, source_target_pairs={{0,240},{16,16},{32,32},{48,192},{64,176},{80,80},{96,96},{112,128... | collective-permute-start | bytes 18440 | tf_op jit(solution)/shard_map/ppermute | solution.py:26
  91.2 116.0 %collective-permute-start.8 = (bf16[1,1,3,384,1536]{4,3,2,1,0:T(8,128)(2,1)}, bf16[1,1,3,384,1536]{4,3,2,1,0:T(8,128)(2,1)S(1)}, u32[]{:S(2)}, u32[]{:S(2)}) collective-permute-start(bf16[1,1,3,384,1536]{4,3,2,1,0:T(8,128)(2,1)} %get-tuple-element.30), channel_id=1, source_target_pairs={{0,240},{16,16},{32,32},{48,192},{64,176},{80,80},{96,96},{112,128... | collective-permute-start | bytes 10616840 | tf_op jit(solution)/shard_map/ppermute | solution.py:26
  132.6 3.7 %collective-permute-start.9 = (f32[1,128]{1,0:T(1,128)}, f32[1,128]{1,0:T(1,128)S(1)}, u32[]{:S(2)}, u32[]{:S(2)}) collective-permute-start(f32[1,128]{1,0:T(1,128)} %squares.1), channel_id=1, source_target_pairs={{0,4},{4,0},{8,12},{12,8},{1,5},{5,1},{9,13},{13,9},{2,6},{6,2},{1... | collective-permute-start | bytes 1544 | tf_op jit(solution)/shard_map/ppermute | solution.py:33
  137.0 5.0 %collective-permute-start.10 = (f32[1,128]{1,0:T(1,128)S(1)}, f32[1,128]{1,0:T(1,128)S(1)}, u32[]{:S(2)}, u32[]{:S(2)}) collective-permute-start(f32[1,128]{1,0:T(1,128)S(1)} %add.29), channel_id=1, source_target_pairs={{0,8},{4,12},{8,0},{12,4},{1,9},{5,13},{9,1},{13,5},{2,10},{6,14},... | collective-permute-start | bytes 1544 | tf_op jit(solution)/shard_map/ppermute | solution.py:33
  142.0 19.4 %collective-permute-start.11 = (f32[1,128]{1,0:T(1,128)S(1)}, f32[1,128]{1,0:T(1,128)S(1)}, u32[]{:S(2)}, u32[]{:S(2)}) collective-permute-start(f32[1,128]{1,0:T(1,128)S(1)} %add.30), channel_id=1, source_target_pairs={{0,16},{16,0},{32,48},{48,32},{64,80},{80,64},{96,112},{112,96},{1... | collective-permute-start | bytes 1544 | tf_op jit(solution)/shard_map/ppermute | solution.py:33
  161.4 5.4 %collective-permute-start.12 = (f32[1,128]{1,0:T(1,128)S(1)}, f32[1,128]{1,0:T(1,128)S(1)}, u32[]{:S(2)}, u32[]{:S(2)}) collective-permute-start(f32[1,128]{1,0:T(1,128)S(1)} %add.31), channel_id=1, source_target_pairs={{0,32},{16,48},{32,0},{48,16},{64,96},{80,112},{96,64},{112,80},{1... | collective-permute-start | bytes 1544 | tf_op jit(solution)/shard_map/ppermute | solution.py:33
  166.8 7.5 %collective-permute-start.13 = (f32[1,128]{1,0:T(1,128)S(1)}, f32[1,128]{1,0:T(1,128)S(1)}, u32[]{:S(2)}, u32[]{:S(2)}) collective-permute-start(f32[1,128]{1,0:T(1,128)S(1)} %add.32), channel_id=1, source_target_pairs={{0,64},{16,80},{32,96},{48,112},{64,0},{80,16},{96,32},{112,48},{1... | collective-permute-start | bytes 1544 | tf_op jit(solution)/shard_map/ppermute | solution.py:33
  174.2 5.0 %collective-permute-start.14 = (f32[1,128]{1,0:T(1,128)S(1)}, f32[1,128]{1,0:T(1,128)S(1)}, u32[]{:S(2)}, u32[]{:S(2)}) collective-permute-start(f32[1,128]{1,0:T(1,128)S(1)} %add.33), channel_id=1, source_target_pairs={{0,128},{16,144},{32,160},{48,176},{64,192},{80,208},{96,224},{112... | collective-permute-start | bytes 1544 | tf_op jit(solution)/shard_map/ppermute | solution.py:33

commit v3 on v2

--- a/solution.py
+++ b/solution.py
@@ -10,6 +10,7 @@
 HD = 128
 BLOCK = 128
 HEADS_PER_STEP = 2
+FIRST = 64
 NEG = -1e30
 FAR = 10**11
 
@@ -70,24 +71,26 @@
             out_ref[start:end, hs] = dot(wb, v_ref[:end, hs], DIM_FIRST).astype(jnp.bfloat16)
 
 
-def backward_kernel(q_ref, k_ref, v_ref, g_ref, gain_ref, tail_ref, lengths_ref, out_ref, raw_ref):
+def backward_kernel(first_ref, rest_ref, low_ref, high_ref, gain_ref, tail_ref, lengths_ref, out_ref, raw_ref):
     length = row_length(tail_ref, lengths_ref, 1)
-    seq = q_ref.shape[0]
+    seq = 2 * low_ref.shape[0]
     for h in range(HEADS_PER_STEP):
         hs = slice(h * HD, (h + 1) * HD)
         gain = gain_ref[:, hs]
+        q, k, v = (jnp.concatenate([first_ref[part, :, hs], rest_ref[part, :, hs]], axis=0) for part in range(3))
+        upstream = jnp.concatenate([low_ref[:, hs], high_ref[:, hs]], axis=0)
         dks = [jnp.zeros((BLOCK, HD), jnp.float32) for _ in range(seq // BLOCK)]
         dvs = [jnp.zeros((BLOCK, HD), jnp.float32) for _ in range(seq // BLOCK)]
         raw = jnp.zeros((1, HD), jnp.float32)
         for start in range(0, seq, BLOCK):
             end = start + BLOCK
-            query = q_ref[start:end, hs].astype(jnp.float32)
+            query = q[start:end].astype(jnp.float32)
             qs = (query * gain).astype(jnp.bfloat16)
-            keys = k_ref[:end, hs]
-            g = g_ref[start:end, hs]
+            keys = k[:end]
+            g = upstream[start:end]
             w = weights_of(qs, keys, start, length)
             wb = w.astype(jnp.bfloat16)
-            dw = dot(v_ref[:end, hs], g, DIM_LAST)
+            dw = dot(v[:end], g, DIM_LAST)
             delta = jnp.sum(wb.astype(jnp.float32) * dw, axis=0, keepdims=True)
             ds = (w * (dw - delta) * (1.0 / HD**0.5)).astype(jnp.bfloat16)
             dv = dot(wb, g)
@@ -104,7 +107,7 @@
         raw_ref[:, hs] = raw
 
 
-def qkv_specs(seq, width):
+def part_specs(seq, width):
     return [
         pl.BlockSpec((None, None, None, seq, width), functools.partial(lambda h, part: (0, 0, part, 0, h), part=part))
         for part in range(3)
@@ -126,7 +129,7 @@
     return pl.pallas_call(
         forward_kernel,
         grid=(features // width,),
-        in_specs=[*qkv_specs(seq, width), *small_specs(width, features, lengths)],
+        in_specs=[*part_specs(seq, width), *small_specs(width, features, lengths)],
         out_specs=pl.BlockSpec((None, None, seq, width), lambda h: (0, 0, 0, h)),
         out_shape=jax.ShapeDtypeStruct((1, 1, seq, features), jnp.bfloat16),
         cost_estimate=pl.CostEstimate(
@@ -136,16 +139,17 @@
     )(block, block, block, aux, aux, lengths)
 
 
-def backward_part(block, upstream, aux, lengths):
-    seq, features = upstream.shape[2:]
+def backward_part(first, rest, upstream, aux, lengths):
+    seq, features = FIRST + rest.shape[3], rest.shape[4]
     width = HEADS_PER_STEP * HD
     heads = features // HD
     return pl.pallas_call(
         backward_kernel,
         grid=(features // width,),
         in_specs=[
-            *qkv_specs(seq, width),
-            pl.BlockSpec((None, None, seq, width), lambda h: (0, 0, 0, h)),
+            pl.BlockSpec((None, None, 3, FIRST, width), lambda h: (0, 0, 0, 0, h)),
+            pl.BlockSpec((None, None, 3, seq - FIRST, width), lambda h: (0, 0, 0, 0, h)),
+            *[pl.BlockSpec((None, None, seq // 2, width), lambda h: (0, 0, 0, h))] * 2,
             *small_specs(width, features, lengths),
         ],
         out_specs=[
@@ -160,7 +164,25 @@
             flops=heads * seq * HD, bytes_accessed=seq * features, transcendentals=heads * seq
         ),
         name="backward",
-    )(block, block, block, upstream, aux, aux, lengths)
+    )(first, rest, *upstream, aux, aux, lengths)
+
+
+def settle_kernel(in_ref, out_ref):
+    out_ref[...] = in_ref[...]
+
+
+def settled(block):
+    seq, features = block.shape[2:]
+    spec = pl.BlockSpec((None, None, seq // 4, features), lambda i: (0, 0, i, 0))
+    return pl.pallas_call(
+        settle_kernel,
+        grid=(4,),
+        in_specs=[spec],
+        out_specs=spec,
+        out_shape=jax.ShapeDtypeStruct(block.shape, block.dtype),
+        cost_estimate=pl.CostEstimate(flops=FAR, bytes_accessed=4 * block.size, transcendentals=0),
+        name="settle",
+    )(block)
 
 
 def square_kernel(total_ref, out_ref):
@@ -172,7 +194,7 @@
     return pl.pallas_call(
         square_kernel,
         out_shape=jax.ShapeDtypeStruct((1, HD), jnp.float32),
-        cost_estimate=pl.CostEstimate(flops=FAR, bytes_accessed=8 * total.size, transcendentals=0),
+        cost_estimate=pl.CostEstimate(flops=2 * total.size, bytes_accessed=8 * total.size, transcendentals=0),
         name="squares",
     )(total)
 
@@ -184,18 +206,23 @@
     )
     aux_back = moved(aux, lambda s, n: site(s, n))
     aux_ahead = moved(aux, lambda s, n: s - 1)
-    grad_out, parked, aux_back, aux_ahead = lax.optimization_barrier((grad_out, parked, aux_back, aux_ahead))
-    upstream = moved(grad_out, lambda s, n: site((s - 1) % n, n))
-    stored = moved(parked, lambda s, n: site(n - 1 - s, n))
-    aux_ahead, upstream = lax.optimization_barrier((aux_ahead, upstream))
+    first = moved(parked[:, :, :, :FIRST], lambda s, n: site(n - 1 - s, n))
+    half = grad_out.shape[2] // 2
+    low, high, rest, aux_back, aux_ahead = lax.optimization_barrier(
+        (grad_out[:, :, :half], grad_out[:, :, half:], parked[:, :, :, FIRST:], aux_back, aux_ahead)
+    )
+    rest = moved(rest, lambda s, n: site(n - 1 - s, n))
+    upstream = [moved(part, lambda s, n: site((s - 1) % n, n)) for part in (low, high)]
+    aux_ahead, first, upstream = lax.optimization_barrier((aux_ahead, first, upstream))
     attended = forward_part(inbound, aux_ahead, lengths)
-    _, stored, upstream = lax.optimization_barrier((attended, stored, upstream))
+    _, first, rest, upstream = lax.optimization_barrier((attended, first, rest, upstream))
     attended = moved(attended, lambda s, n: s + 1)
-    grads, raw = backward_part(stored, upstream, aux_back, lengths)
+    grads, raw = backward_part(first, rest, upstream, aux_back, lengths)
     total = doubled_sum(raw, "dp")
     grads, total = lax.optimization_barrier((grads, total))
     own_total = moved(total, lambda s, n: site(s, n))
     grads = moved(grads, lambda s, n: site(s, n))
+    attended = settled(attended)
     total, own_total, attended = lax.optimization_barrier((total, own_total, attended))
     squares = square_sum(total)
     squares = doubled_sum(doubled_sum(squares, "tensor"), "section")

time: 214 us -> 208 us (0.972)
  waiting for transfers between devices: 87.4 us -> 70.5 us
  starting transfers between devices: 86.1 us -> 91.8 us
  Pallas kernels: 27.5 us -> 31 us
    ppermute x7 -> x9, waiting for transfers between devices: 71.5 us -> 53.8 us  [moved(): lax.ppermute(value, 'section', [(i, target(i, size) % size) for i in rang...]
    ppermute x7 -> x9, starting transfers between devices: 51 us -> 58.8 us  [moved(): lax.ppermute(value, 'section', [(i, target(i, size) % size) for i in rang...]
    slice x0 -> x3, local copies, waits for them, and re-layouts: none -> 4.22 us  [the longest x1 1.79 us: shards(): parked[:, :, :, FIRST:]]
    pallas_call x2 -> x3, Pallas kernels: 26.3 us -> 29.7 us  [the longest x1 15 us: backward_part(): pl.pallas_call(backward_kernel, grid=(features // width,), in_specs=[pl.B...]
    unnamed x10 -> x13, local copies, waits for them, and re-layouts: 5.96 us -> 3.38 us
  transfers between devices with their start and end apart: 15 -> 17, of which waited for: 11 -> 10; matrix products, arithmetic and copies ran while one was open for 1% -> 3% of each run, Pallas kernels for 13% -> 15%
where the time goes in v3:
time: 208 us; the launch traced here: 205 us
  starting transfers between devices  91.8 us (44%)
  waiting for transfers between devices  70.5 us (34%)
  Pallas kernels  31 us (15%)
  local copies, waits for them, and re-layouts  8.56 us (4%)
  other arithmetic  2.75 us (1%)
    ppermute x9, starting transfers between devices, moved(): lax.ppermute(value, 'section', [(i, target(i, size) % size) for i in rang...  58.8 us
    ppermute x9, waiting for transfers between devices, moved(): lax.ppermute(value, 'section', [(i, target(i, size) % size) for i in rang...  53.8 us
    ppermute x8, starting transfers between devices, doubled_sum(): lax.ppermute(value, axis, [(i, i ^ step) for i in range(size)])  33 us
    ppermute x8, waiting for transfers between devices, doubled_sum(): lax.ppermute(value, axis, [(i, i ^ step) for i in range(size)])  16.7 us
    pallas_call x1, Pallas kernels, backward_part(): pl.pallas_call(backward_kernel, grid=(features // width,), in_specs=[pl.B...  15 us
    pallas_call x1, Pallas kernels, forward_part(): pl.pallas_call(forward_kernel, grid=(features // width,), in_specs=[*part...  11.2 us
  transfers between devices with their start and end apart: 17, of which 10 were waited for; matrix products, arithmetic and copies ran while one was open for 3% of the time, Pallas kernels for 15%

profile of v3, /device:TPU:8, one launch (start us, length us, event | category | flops | bytes accessed | tf_op | source)
XLA Modules:
  0.0 205.4 jit_solution(13500404794473705105)
XLA Ops:
  0.6 0.0 copy-start
  0.6 0.8 convert_element_type.3
  1.5 1.0 concatenate.3
  2.4 9.5 %collective-permute-start = (f32[1,1664]{1,0:T(1,128)S(1)}, f32[1,1664]{1,0:T(1,128)S(1)}, u32[]{:S(2)}, u32[]{:S(2)}) collective-permute-start(f32[1,1664]{1,0:T(1,128)S(1)} %concatenate.3), channel_id=1, source_target_pairs={{0,240},{16,16},{32,32},{48,192},{64,176},{80,80},{96,96},{112,128... | collective-permute-start | bytes 19976 | tf_op jit(solution)/shard_map/ppermute | solution.py:27
  11.9 0.1 collective-permute-start.1
  12.0 1.1 slice.18
  13.1 1.5 collective-permute-start.2
  14.6 1.3 fusion
  15.9 1.8 slice.17
  17.7 0.0 collective-permute-done.gain_ref.tail_ref
  17.7 0.0 collective-permute-done.1.gain_ref.tail_ref
  17.7 0.7 collective-permute-start.3
  18.4 1.5 collective-permute-start.4
  19.9 2.5 %collective-permute-start.5 = (bf16[1,1,3,320,1536]{4,3,2,1,0:T(8,128)(2,1)}, bf16[1,1,3,320,1536]{4,3,2,1,0:T(8,128)(2,1)S(1)}, u32[]{:S(2)}, u32[]{:S(2)}) collective-permute-start(bf16[1,1,3,320,1536]{4,3,2,1,0:T(8,128)(2,1)} %slice.17), channel_id=1, source_target_pairs={{0,0},{16,224},{32,208},{48,48},{64,64},{80,160},{96,144},{112,112... | collective-permute-start | bytes 8847368 | tf_op jit(solution)/shard_map/ppermute | solution.py:27
  22.4 0.0 collective-permute-done.2.first_ref
  22.4 11.2 %forward.1 = bf16[1,1,384,1536]{3,2,1,0:T(8,128)(2,1)} custom-call(bf16[1,1,3,384,1536]{4,3,2,1,0:T(8,128)(2,1)} %v_ref.1, bf16[1,1,3,384,1536]{4,3,2,1,0:T(8,128)(2,1)} %v_ref.1, bf16[1,1,3,384,1536]{4,3,2,1,0:T(8,128)(2,1)} %v_ref.1, f32[1,1664]{1,0:T(1,128)} %copy-done.5, f32[1,1664]{1,0:T(1,128)} %copy-done.5, s32[1,8]{1,0:T(1,128)} %lengths_ref.3), custom_call_target="tpu_custom_call" | custom-call | flops 99999997952 | bytes 4718592 | tf_op jit(solution)/shard_map/forward/pallas_call | solution.py:129
  33.7 33.5 %collective-permute-start.9 = (bf16[1,1,384,1536]{3,2,1,0:T(8,128)(2,1)}, bf16[1,1,384,1536]{3,2,1,0:T(8,128)(2,1)}, u32[]{:S(2)}, u32[]{:S(2)}) collective-permute-start(bf16[1,1,384,1536]{3,2,1,0:T(8,128)(2,1)} %forward.1), channel_id=1, source_target_pairs={{0,16},{16,32},{32,48},{48,64},{64,80},{80,96},{96,112},{112,128},... | collective-permute-start | bytes 3538952 | tf_op jit(solution)/shard_map/ppermute | solution.py:27
  67.2 0.0 collective-permute-done.5.rest_ref
  67.2 1.6 copy-done.1
  68.8 15.0 %backward.1 = (bf16[1,1,3,384,1536]{4,3,2,1,0:T(8,128)(2,1)}, f32[1,1536]{1,0:T(1,128)}) custom-call(bf16[1,1,3,64,1536]{4,3,2,1,0:T(8,128)(2,1)} %collective-permute-done.2.first_ref, bf16[1,1,3,320,1536]{4,3,2,1,0:T(8,128)(2,1)} %copy-done.1, bf16[1,1,192,1536]{3,2,1,0:T(8,128)(2,1)} %copy-done.2, ...), custom_call_target="tpu_custom_call" | custom-call | flops 589824 | bytes 589824 | tf_op jit(solution)/shard_map/backward/pallas_call | solution.py:146
  83.8 0.0 collective-permute-start.6
  83.8 1.4 collective-permute-done.6
  85.2 0.7 add.27
  85.9 1.3 collective-permute-start.7
  87.2 2.3 %collective-permute-done.7 = f32[1,1536]{1,0:T(1,128)S(1)} collective-permute-done((f32[1,1536]{1,0:T(1,128)S(1)}, f32[1,1536]{1,0:T(1,128)S(1)}, u32[]{:S(2)}, u32[]{:S(2)}) %collective-permute-start.7) | collective-permute-done | bytes 6176 | tf_op jit(solution)/shard_map/ppermute | solution.py:34
  89.5 0.0 copy-start.4
  89.5 7.6 %collective-permute-start.8 = (f32[1,1536]{1,0:T(1,128)S(1)}, f32[1,1536]{1,0:T(1,128)S(1)}, u32[]{:S(2)}, u32[]{:S(2)}) collective-permute-start(f32[1,1536]{1,0:T(1,128)S(1)} %add.28.total_ref), channel_id=1, source_target_pairs={{0,240},{16,16},{32,32},{48,192},{64,176},{80,80},{96,96},{112,128... | collective-permute-start | bytes 18440 | tf_op jit(solution)/shard_map/ppermute | solution.py:27
  97.1 1.9 collective-permute-start.10
  99.1 28.7 %collective-permute-done.9.in_ref = bf16[1,1,384,1536]{3,2,1,0:T(8,128)(2,1)} collective-permute-done((bf16[1,1,384,1536]{3,2,1,0:T(8,128)(2,1)}, bf16[1,1,384,1536]{3,2,1,0:T(8,128)(2,1)}, u32[]{:S(2)}, u32[]{:S(2)}) %collective-permute-start.9) | collective-permute-done | bytes 1179680 | tf_op jit(solution)/shard_map/ppermute | solution.py:27
  127.8 3.4 %settle.1 = bf16[1,1,384,1536]{3,2,1,0:T(8,128)(2,1)} custom-call(bf16[1,1,384,1536]{3,2,1,0:T(8,128)(2,1)} %collective-permute-done.9.in_ref), custom_call_target="tpu_custom_call" | custom-call | flops 99999997952 | bytes 2359296 | tf_op jit(solution)/shard_map/settle/pallas_call | solution.py:177
  131.2 0.0 collective-permute-done.8
  131.2 1.3 squares.1
  132.5 1.5 collective-permute-start.11
  134.0 2.3 %collective-permute-done.11 = f32[1,128]{1,0:T(1,128)S(1)} collective-permute-done((f32[1,128]{1,0:T(1,128)}, f32[1,128]{1,0:T(1,128)S(1)}, u32[]{:S(2)}, u32[]{:S(2)}) %collective-permute-start.11) | collective-permute-done | bytes 544 | tf_op jit(solution)/shard_map/ppermute | solution.py:34
  136.3 0.6 add.29
  136.9 3.0 %collective-permute-start.12 = (f32[1,128]{1,0:T(1,128)S(1)}, f32[1,128]{1,0:T(1,128)S(1)}, u32[]{:S(2)}, u32[]{:S(2)}) collective-permute-start(f32[1,128]{1,0:T(1,128)S(1)} %add.29), channel_id=1, source_target_pairs={{0,8},{4,12},{8,0},{12,4},{1,9},{5,13},{9,1},{13,5},{2,10},{6,14},... | collective-permute-start | bytes 1544 | tf_op jit(solution)/shard_map/ppermute | solution.py:34
  139.9 2.0 collective-permute-done.12
  141.9 15.9 %collective-permute-start.13 = (f32[1,128]{1,0:T(1,128)S(1)}, f32[1,128]{1,0:T(1,128)S(1)}, u32[]{:S(2)}, u32[]{:S(2)}) collective-permute-start(f32[1,128]{1,0:T(1,128)S(1)} %add.30), channel_id=1, source_target_pairs={{0,16},{16,0},{32,48},{48,32},{64,80},{80,64},{96,112},{112,96},{1... | collective-permute-start | bytes 1544 | tf_op jit(solution)/shard_map/ppermute | solution.py:34
  157.8 1.5 collective-permute-done.13
  159.3 4.5 %collective-permute-start.14 = (f32[1,128]{1,0:T(1,128)S(1)}, f32[1,128]{1,0:T(1,128)S(1)}, u32[]{:S(2)}, u32[]{:S(2)}) collective-permute-start(f32[1,128]{1,0:T(1,128)S(1)} %add.31), channel_id=1, source_target_pairs={{0,32},{16,48},{32,0},{48,16},{64,96},{80,112},{96,64},{112,80},{1... | collective-permute-start | bytes 1544 | tf_op jit(solution)/shard_map/ppermute | solution.py:34
  163.8 1.5 collective-permute-done.14
  165.4 4.5 %collective-permute-start.15 = (f32[1,128]{1,0:T(1,128)S(1)}, f32[1,128]{1,0:T(1,128)S(1)}, u32[]{:S(2)}, u32[]{:S(2)}) collective-permute-start(f32[1,128]{1,0:T(1,128)S(1)} %add.32), channel_id=1, source_target_pairs={{0,64},{16,80},{32,96},{48,112},{64,0},{80,16},{96,32},{112,48},{1... | collective-permute-start | bytes 1544 | tf_op jit(solution)/shard_map/ppermute | solution.py:34
  169.9 3.0 %collective-permute-done.15 = f32[1,128]{1,0:T(1,128)S(1)} collective-permute-done((f32[1,128]{1,0:T(1,128)S(1)}, f32[1,128]{1,0:T(1,128)S(1)}, u32[]{:S(2)}, u32[]{:S(2)}) %collective-permute-start.15) | collective-permute-done | bytes 544 | tf_op jit(solution)/shard_map/ppermute | solution.py:34
  172.8 2.3 %collective-permute-start.16 = (f32[1,128]{1,0:T(1,128)S(1)}, f32[1,128]{1,0:T(1,128)S(1)}, u32[]{:S(2)}, u32[]{:S(2)}) collective-permute-start(f32[1,128]{1,0:T(1,128)S(1)} %add.33), channel_id=1, source_target_pairs={{0,128},{16,144},{32,160},{48,176},{64,192},{80,208},{96,224},{112... | collective-permute-start | bytes 1544 | tf_op jit(solution)/shard_map/ppermute | solution.py:34
  175.1 2.7 %collective-permute-done.16 = f32[1,128]{1,0:T(1,128)S(1)} collective-permute-done((f32[1,128]{1,0:T(1,128)S(1)}, f32[1,128]{1,0:T(1,128)S(1)}, u32[]{:S(2)}, u32[]{:S(2)}) %collective-permute-start.16) | collective-permute-done | bytes 544 | tf_op jit(solution)/shard_map/ppermute | solution.py:34
  178.0 0.6 broadcast_divide_fusion
  178.6 25.0 %collective-permute-done.10 = bf16[1,1,3,384,1536]{4,3,2,1,0:T(8,128)(2,1)S(1)} collective-permute-done((bf16[1,1,3,384,1536]{4,3,2,1,0:T(8,128)(2,1)}, bf16[1,1,3,384,1536]{4,3,2,1,0:T(8,128)(2,1)S(1)}, u32[]{:S(2)}, u32[]{:S(2)}) %collective-permute-start.10) | collective-permute-done | bytes 3538976 | tf_op jit(solution)/shard_map/ppermute | solution.py:27
  203.6 1.8 copy.10
  (18 shorter events, 0.0 us)
Async XLA Ops:
  0.6 15.3 %copy-start = (bf16[1,1,3,384,1536]{4,3,2,1,0:T(8,128)(2,1)S(1)}, bf16[1,1,3,384,1536]{4,3,2,1,0:T(8,128)(2,1)}, u32[]{:S(2)}) copy-start(bf16[1,1,3,384,1536]{4,3,2,1,0:T(8,128)(2,1)} %param.7) | copy-start | bytes 10616836
  2.4 15.3 %collective-permute-start = (f32[1,1664]{1,0:T(1,128)S(1)}, f32[1,1664]{1,0:T(1,128)S(1)}, u32[]{:S(2)}, u32[]{:S(2)}) collective-permute-start(f32[1,1664]{1,0:T(1,128)S(1)} %concatenate.3), channel_id=1, source_target_pairs={{0,240},{16,16},{32,32},{48,192},{64,176},{80,80},{96,96},{112,128... | collective-permute-start | bytes 19976 | tf_op jit(solution)/shard_map/ppermute | solution.py:27
  11.9 5.8 %collective-permute-start.1 = (f32[1,1664]{1,0:T(1,128)S(1)}, f32[1,1664]{1,0:T(1,128)S(1)}, u32[]{:S(2)}, u32[]{:S(2)}) collective-permute-start(f32[1,1664]{1,0:T(1,128)S(1)} %concatenate.3), channel_id=1, source_target_pairs={{0,240},{16,0},{32,16},{48,32},{64,48},{80,64},{96,80},{112,96},{1... | collective-permute-start | bytes 19976 | tf_op jit(solution)/shard_map/ppermute | solution.py:27
  13.1 9.3 %collective-permute-start.2 = (bf16[1,1,3,64,1536]{4,3,2,1,0:T(8,128)(2,1)S(1)}, bf16[1,1,3,64,1536]{4,3,2,1,0:T(8,128)(2,1)}, u32[]{:S(2)}, u32[]{:S(2)}) collective-permute-start(bf16[1,1,3,64,1536]{4,3,2,1,0:T(8,128)(2,1)S(1)} %slice.18), channel_id=1, source_target_pairs={{0,0},{16,224},{32,208},{48,48},{64,64},{80,160},{96,144},{112,112... | collective-permute-start | bytes 1769480 | tf_op jit(solution)/shard_map/ppermute | solution.py:27
  17.7 16.0 %copy-start.3 = (f32[1,1664]{1,0:T(1,128)}, f32[1,1664]{1,0:T(1,128)S(1)}, u32[]{:S(2)}) copy-start(f32[1,1664]{1,0:T(1,128)S(1)} %collective-permute-done.gain_ref.tail_ref) | copy-start | bytes 19972
  17.7 4.7 %copy-start.5 = (f32[1,1664]{1,0:T(1,128)}, f32[1,1664]{1,0:T(1,128)S(1)}, u32[]{:S(2)}) copy-start(f32[1,1664]{1,0:T(1,128)S(1)} %collective-permute-done.1.gain_ref.tail_ref) | copy-start | bytes 19972
  17.7 4.7 %collective-permute-start.3 = (bf16[1,1,192,1536]{3,2,1,0:T(8,128)(2,1)S(1)}, bf16[1,1,192,1536]{3,2,1,0:T(8,128)(2,1)S(1)}, u32[]{:S(2)}, u32[]{:S(2)}) collective-permute-start(bf16[1,1,192,1536]{3,2,1,0:T(8,128)(2,1)S(1)} %get-tuple-element.24), channel_id=1, source_target_pairs={{0,0},{16,240},{32,16},{48,32},{64,192},{80,176},{96,80},{112,96},... | collective-permute-start | bytes 1769480 | tf_op jit(solution)/shard_map/ppermute | solution.py:27
  18.4 4.0 %collective-permute-start.4 = (bf16[1,1,192,1536]{3,2,1,0:T(8,128)(2,1)S(1)}, bf16[1,1,192,1536]{3,2,1,0:T(8,128)(2,1)}, u32[]{:S(2)}, u32[]{:S(2)}) collective-permute-start(bf16[1,1,192,1536]{3,2,1,0:T(8,128)(2,1)S(1)} %get-tuple-element.25), channel_id=1, source_target_pairs={{0,0},{16,240},{32,16},{48,32},{64,192},{80,176},{96,80},{112,96},... | collective-permute-start | bytes 1769480 | tf_op jit(solution)/shard_map/ppermute | solution.py:27
  19.9 47.3 %collective-permute-start.5 = (bf16[1,1,3,320,1536]{4,3,2,1,0:T(8,128)(2,1)}, bf16[1,1,3,320,1536]{4,3,2,1,0:T(8,128)(2,1)S(1)}, u32[]{:S(2)}, u32[]{:S(2)}) collective-permute-start(bf16[1,1,3,320,1536]{4,3,2,1,0:T(8,128)(2,1)} %slice.17), channel_id=1, source_target_pairs={{0,0},{16,224},{32,208},{48,48},{64,64},{80,160},{96,144},{112,112... | collective-permute-start | bytes 8847368 | tf_op jit(solution)/shard_map/ppermute | solution.py:27
  22.4 11.3 %copy-start.2 = (bf16[1,1,192,1536]{3,2,1,0:T(8,128)(2,1)}, bf16[1,1,192,1536]{3,2,1,0:T(8,128)(2,1)S(1)}, u32[]{:S(2)}) copy-start(bf16[1,1,192,1536]{3,2,1,0:T(8,128)(2,1)S(1)} %collective-permute-done.3.low_ref) | copy-start | bytes 1769476
  33.7 94.1 %collective-permute-start.9 = (bf16[1,1,384,1536]{3,2,1,0:T(8,128)(2,1)}, bf16[1,1,384,1536]{3,2,1,0:T(8,128)(2,1)}, u32[]{:S(2)}, u32[]{:S(2)}) collective-permute-start(bf16[1,1,384,1536]{3,2,1,0:T(8,128)(2,1)} %forward.1), channel_id=1, source_target_pairs={{0,16},{16,32},{32,48},{48,64},{64,80},{80,96},{96,112},{112,128},... | collective-permute-start | bytes 3538952 | tf_op jit(solution)/shard_map/ppermute | solution.py:27
  67.2 1.6 copy-start.1
  83.8 1.4 collective-permute-start.6
  85.9 3.6 %collective-permute-start.7 = (f32[1,1536]{1,0:T(1,128)S(1)}, f32[1,1536]{1,0:T(1,128)S(1)}, u32[]{:S(2)}, u32[]{:S(2)}) collective-permute-start(f32[1,1536]{1,0:T(1,128)S(1)} %add.27), channel_id=1, source_target_pairs={{0,2},{1,3},{2,0},{3,1},{4,6},{5,7},{6,4},{7,5},{8,10},{9,11},{10,... | collective-permute-start | bytes 18440 | tf_op jit(solution)/shard_map/ppermute | solution.py:34
  89.5 41.7 %copy-start.4 = (f32[1,1536]{1,0:T(1,128)}, f32[1,1536]{1,0:T(1,128)S(1)}, u32[]{:S(2)}) copy-start(f32[1,1536]{1,0:T(1,128)S(1)} %add.28.total_ref) | copy-start | bytes 18436
  89.5 41.7 %collective-permute-start.8 = (f32[1,1536]{1,0:T(1,128)S(1)}, f32[1,1536]{1,0:T(1,128)S(1)}, u32[]{:S(2)}, u32[]{:S(2)}) collective-permute-start(f32[1,1536]{1,0:T(1,128)S(1)} %add.28.total_ref), channel_id=1, source_target_pairs={{0,240},{16,16},{32,32},{48,192},{64,176},{80,80},{96,96},{112,128... | collective-permute-start | bytes 18440 | tf_op jit(solution)/shard_map/ppermute | solution.py:27
  97.1 106.5 %collective-permute-start.10 = (bf16[1,1,3,384,1536]{4,3,2,1,0:T(8,128)(2,1)}, bf16[1,1,3,384,1536]{4,3,2,1,0:T(8,128)(2,1)S(1)}, u32[]{:S(2)}, u32[]{:S(2)}) collective-permute-start(bf16[1,1,3,384,1536]{4,3,2,1,0:T(8,128)(2,1)} %get-tuple-element.40), channel_id=1, source_target_pairs={{0,240},{16,16},{32,32},{48,192},{64,176},{80,80},{96,96},{112,128... | collective-permute-start | bytes 10616840 | tf_op jit(solution)/shard_map/ppermute | solution.py:27
  132.5 3.8 %collective-permute-start.11 = (f32[1,128]{1,0:T(1,128)}, f32[1,128]{1,0:T(1,128)S(1)}, u32[]{:S(2)}, u32[]{:S(2)}) collective-permute-start(f32[1,128]{1,0:T(1,128)} %squares.1), channel_id=1, source_target_pairs={{0,4},{4,0},{8,12},{12,8},{1,5},{5,1},{9,13},{13,9},{2,6},{6,2},{1... | collective-permute-start | bytes 1544 | tf_op jit(solution)/shard_map/ppermute | solution.py:34
  136.9 5.0 %collective-permute-start.12 = (f32[1,128]{1,0:T(1,128)S(1)}, f32[1,128]{1,0:T(1,128)S(1)}, u32[]{:S(2)}, u32[]{:S(2)}) collective-permute-start(f32[1,128]{1,0:T(1,128)S(1)} %add.29), channel_id=1, source_target_pairs={{0,8},{4,12},{8,0},{12,4},{1,9},{5,13},{9,1},{13,5},{2,10},{6,14},... | collective-permute-start | bytes 1544 | tf_op jit(solution)/shard_map/ppermute | solution.py:34
  141.9 17.4 %collective-permute-start.13 = (f32[1,128]{1,0:T(1,128)S(1)}, f32[1,128]{1,0:T(1,128)S(1)}, u32[]{:S(2)}, u32[]{:S(2)}) collective-permute-start(f32[1,128]{1,0:T(1,128)S(1)} %add.30), channel_id=1, source_target_pairs={{0,16},{16,0},{32,48},{48,32},{64,80},{80,64},{96,112},{112,96},{1... | collective-permute-start | bytes 1544 | tf_op jit(solution)/shard_map/ppermute | solution.py:34
  159.3 6.1 %collective-permute-start.14 = (f32[1,128]{1,0:T(1,128)S(1)}, f32[1,128]{1,0:T(1,128)S(1)}, u32[]{:S(2)}, u32[]{:S(2)}) collective-permute-start(f32[1,128]{1,0:T(1,128)S(1)} %add.31), channel_id=1, source_target_pairs={{0,32},{16,48},{32,0},{48,16},{64,96},{80,112},{96,64},{112,80},{1... | collective-permute-start | bytes 1544 | tf_op jit(solution)/shard_map/ppermute | solution.py:34
  165.4 7.4 %collective-permute-start.15 = (f32[1,128]{1,0:T(1,128)S(1)}, f32[1,128]{1,0:T(1,128)S(1)}, u32[]{:S(2)}, u32[]{:S(2)}) collective-permute-start(f32[1,128]{1,0:T(1,128)S(1)} %add.32), channel_id=1, source_target_pairs={{0,64},{16,80},{32,96},{48,112},{64,0},{80,16},{96,32},{112,48},{1... | collective-permute-start | bytes 1544 | tf_op jit(solution)/shard_map/ppermute | solution.py:34
  172.8 5.0 %collective-permute-start.16 = (f32[1,128]{1,0:T(1,128)S(1)}, f32[1,128]{1,0:T(1,128)S(1)}, u32[]{:S(2)}, u32[]{:S(2)}) collective-permute-start(f32[1,128]{1,0:T(1,128)S(1)} %add.33), channel_id=1, source_target_pairs={{0,128},{16,144},{32,160},{48,176},{64,192},{80,208},{96,224},{112... | collective-permute-start | bytes 1544 | tf_op jit(solution)/shard_map/ppermute | solution.py:34

commit v4 on v3

--- a/solution.py
+++ b/solution.py
@@ -9,9 +9,12 @@
 
 HD = 128
 BLOCK = 128
-HEADS_PER_STEP = 2
-FIRST = 64
+FORWARD_HEADS = 6
+BACKWARD_HEADS = 3
+FIRST = 96
 NEG = -1e30
+SCALE = HD**-0.5
+LOG2E = 1.4426950408889634
 FAR = 10**11
 
 DIM_LAST = (((1,), (1,)), ((), ()))
@@ -47,64 +50,65 @@
     return jnp.sum(jnp.where(lanes == index, table, 0), axis=1, keepdims=True)
 
 
-def weights_of(qs, keys, start, length):
-    n = keys.shape[0]
-    scores = dot(keys, qs, DIM_LAST) * (1.0 / HD**0.5)
+def weights_of(scores, start, length):
     rows = lax.broadcasted_iota(jnp.int32, scores.shape, 0)
-    cols = lax.broadcasted_iota(jnp.int32, scores.shape, 1) + start
-    scores = jnp.where((rows <= cols) & (rows < length), scores, NEG)
+    cols = lax.broadcasted_iota(jnp.int32, (1, scores.shape[1]), 1) + start
+    scores = jnp.where(rows < jnp.minimum(cols + 1, length), scores, NEG)
     top = jnp.max(scores, axis=0, keepdims=True)
-    expo = jnp.exp(scores - top)
+    expo = jnp.exp2((scores - top) * (LOG2E * SCALE))
     return expo * (1.0 / jnp.sum(expo, axis=0, keepdims=True))
 
 
 def forward_kernel(q_ref, k_ref, v_ref, gain_ref, tail_ref, lengths_ref, out_ref):
     length = row_length(tail_ref, lengths_ref, 0)
     seq = q_ref.shape[0]
-    for h in range(HEADS_PER_STEP):
-        hs = slice(h * HD, (h + 1) * HD)
-        gain = gain_ref[:, hs]
-        for start in range(0, seq, BLOCK):
-            end = start + BLOCK
-            qs = (q_ref[start:end, hs].astype(jnp.float32) * gain).astype(jnp.bfloat16)
-            wb = weights_of(qs, k_ref[:end, hs], start, length).astype(jnp.bfloat16)
-            out_ref[start:end, hs] = dot(wb, v_ref[:end, hs], DIM_FIRST).astype(jnp.bfloat16)
+    units = [(slice(h * HD, (h + 1) * HD), start) for h in range(out_ref.shape[1] // HD) for start in range(0, seq, BLOCK)]
+    scores = []
+    for hs, start in units:
+        qs = (q_ref[start : start + BLOCK, hs].astype(jnp.float32) * gain_ref[:, hs]).astype(jnp.bfloat16)
+        scores.append(dot(k_ref[: start + BLOCK, hs], qs, DIM_LAST))
+    weights = [weights_of(s, start, length).astype(jnp.bfloat16) for s, (_, start) in zip(scores, units)]
+    outs = [dot(wb, v_ref[: start + BLOCK, hs], DIM_FIRST) for wb, (hs, start) in zip(weights, units)]
+    for out, (hs, start) in zip(outs, units):
+        out_ref[start : start + BLOCK, hs] = out.astype(jnp.bfloat16)
 
 
 def backward_kernel(first_ref, rest_ref, low_ref, high_ref, gain_ref, tail_ref, lengths_ref, out_ref, raw_ref):
     length = row_length(tail_ref, lengths_ref, 1)
     seq = 2 * low_ref.shape[0]
-    for h in range(HEADS_PER_STEP):
-        hs = slice(h * HD, (h + 1) * HD)
-        gain = gain_ref[:, hs]
+    heads = [slice(h * HD, (h + 1) * HD) for h in range(low_ref.shape[1] // HD)]
+    starts = range(0, seq, BLOCK)
+    loaded = []
+    for hs in heads:
         q, k, v = (jnp.concatenate([first_ref[part, :, hs], rest_ref[part, :, hs]], axis=0) for part in range(3))
-        upstream = jnp.concatenate([low_ref[:, hs], high_ref[:, hs]], axis=0)
-        dks = [jnp.zeros((BLOCK, HD), jnp.float32) for _ in range(seq // BLOCK)]
-        dvs = [jnp.zeros((BLOCK, HD), jnp.float32) for _ in range(seq // BLOCK)]
+        g = jnp.concatenate([low_ref[:, hs], high_ref[:, hs]], axis=0)
+        qs = (q.astype(jnp.float32) * gain_ref[:, hs]).astype(jnp.bfloat16)
+        loaded.append((q, k, v, g, qs))
+    units = [(h, start, start + BLOCK) for h in range(len(heads)) for start in starts]
+    scores = [dot(loaded[h][1][:end], loaded[h][4][start:end], DIM_LAST) for h, start, end in units]
+    dws = [dot(loaded[h][2][:end], loaded[h][3][start:end], DIM_LAST) for h, start, end in units]
+    wbs, dss = [], []
+    for (h, start, end), s, dw in zip(units, scores, dws):
+        w = weights_of(s, start, length)
+        wb = w.astype(jnp.bfloat16)
+        delta = jnp.sum(wb.astype(jnp.float32) * dw, axis=0, keepdims=True)
+        wbs.append(wb)
+        dss.append((w * (dw - delta) * SCALE).astype(jnp.bfloat16))
+    for h, hs in enumerate(heads):
+        q, k, v, g, qs = loaded[h]
+        mine = [i for i, unit in enumerate(units) if unit[0] == h]
         raw = jnp.zeros((1, HD), jnp.float32)
-        for start in range(0, seq, BLOCK):
-            end = start + BLOCK
-            query = q[start:end].astype(jnp.float32)
-            qs = (query * gain).astype(jnp.bfloat16)
-            keys = k[:end]
-            g = upstream[start:end]
-            w = weights_of(qs, keys, start, length)
-            wb = w.astype(jnp.bfloat16)
-            dw = dot(v[:end], g, DIM_LAST)
-            delta = jnp.sum(wb.astype(jnp.float32) * dw, axis=0, keepdims=True)
-            ds = (w * (dw - delta) * (1.0 / HD**0.5)).astype(jnp.bfloat16)
-            dv = dot(wb, g)
-            dk = dot(ds, qs)
-            for b in range(end // BLOCK):
-                dvs[b] = dvs[b] + dv[b * BLOCK : (b + 1) * BLOCK]
-                dks[b] = dks[b] + dk[b * BLOCK : (b + 1) * BLOCK]
-            dqs = dot(ds, keys, DIM_FIRST)
-            out_ref[0, start:end, hs] = (dqs * gain).astype(jnp.bfloat16)
-            raw = raw + jnp.sum(dqs * query, axis=0, keepdims=True)
-        for b in range(seq // BLOCK):
-            out_ref[1, b * BLOCK : (b + 1) * BLOCK, hs] = dks[b].astype(jnp.bfloat16)
-            out_ref[2, b * BLOCK : (b + 1) * BLOCK, hs] = dvs[b].astype(jnp.bfloat16)
+        for i in mine:
+            _, start, end = units[i]
+            dqs = dot(dss[i], k[:end], DIM_FIRST)
+            out_ref[0, start:end, hs] = (dqs * gain_ref[:, hs]).astype(jnp.bfloat16)
+            raw = raw + jnp.sum(dqs * q[start:end].astype(jnp.float32), axis=0, keepdims=True)
         raw_ref[:, hs] = raw
+        for start in starts:
+            later = [i for i in mine if units[i][2] > start]
+            for part, lhs, rhs in ((1, dss, qs), (2, wbs, g)):
+                left = jnp.concatenate([lhs[i][start : start + BLOCK] for i in later], axis=1)
+                out_ref[part, start : start + BLOCK, hs] = dot(left, rhs[start:]).astype(jnp.bfloat16)
 
 
 def part_specs(seq, width):
@@ -124,7 +128,7 @@
 
 def forward_part(block, aux, lengths):
     seq, features = block.shape[3:]
-    width = HEADS_PER_STEP * HD
+    width = FORWARD_HEADS * HD
     heads = features // HD
     return pl.pallas_call(
         forward_kernel,
@@ -141,7 +145,7 @@
 
 def backward_part(first, rest, upstream, aux, lengths):
     seq, features = FIRST + rest.shape[3], rest.shape[4]
-    width = HEADS_PER_STEP * HD
+    width = BACKWARD_HEADS * HD
     heads = features // HD
     return pl.pallas_call(
         backward_kernel,

time: 208 us -> 204 us (0.981)
  Pallas kernels: 31 us -> 17.9 us
  waiting for transfers between devices: 70.5 us -> 77.1 us
  starting transfers between devices: 91.8 us -> 94.9 us
    pallas_call x1, Pallas kernels: 15 us -> 8.06 us  [backward_part(): pl.pallas_call(backward_kernel, grid=(features // width,), in_specs=[pl.B...]
    ppermute x9, waiting for transfers between devices: 53.8 us -> 60.4 us  [moved(): lax.ppermute(value, 'section', [(i, target(i, size) % size) for i in rang...]
    ppermute x9, starting transfers between devices: 58.8 us -> 65.2 us  [moved(): lax.ppermute(value, 'section', [(i, target(i, size) % size) for i in rang...]
    pallas_call x1, Pallas kernels: 11.2 us -> 5.08 us  [forward_part(): pl.pallas_call(forward_kernel, grid=(features // width,), in_specs=[*part...]
    ppermute x8, starting transfers between devices: 33 us -> 29.7 us  [doubled_sum(): lax.ppermute(value, axis, [(i, i ^ step) for i in range(size)])]
  transfers between devices with their start and end apart: 17 -> 17, of which waited for: 10 -> 10; matrix products, arithmetic and copies ran while one was open for 3% -> 3% of each run, Pallas kernels for 15% -> 9%
where the time goes in v4:
time: 204 us; the launch traced here: 202 us
  starting transfers between devices  94.9 us (47%)
  waiting for transfers between devices  77.1 us (38%)
  Pallas kernels  17.9 us (9%)
  local copies, waits for them, and re-layouts  8.5 us (4%)
  other arithmetic  2.75 us (1%)
    ppermute x9, starting transfers between devices, moved(): lax.ppermute(value, 'section', [(i, target(i, size) % size) for i in rang...  65.2 us
    ppermute x9, waiting for transfers between devices, moved(): lax.ppermute(value, 'section', [(i, target(i, size) % size) for i in rang...  60.4 us
    ppermute x8, starting transfers between devices, doubled_sum(): lax.ppermute(value, axis, [(i, i ^ step) for i in range(size)])  29.7 us
    ppermute x8, waiting for transfers between devices, doubled_sum(): lax.ppermute(value, axis, [(i, i ^ step) for i in range(size)])  16.7 us
    pallas_call x1, Pallas kernels, backward_part(): pl.pallas_call(backward_kernel, grid=(features // width,), in_specs=[pl.B...  8.06 us
    pallas_call x1, Pallas kernels, forward_part(): pl.pallas_call(forward_kernel, grid=(features // width,), in_specs=[*part...  5.08 us
  transfers between devices with their start and end apart: 17, of which 10 were waited for; matrix products, arithmetic and copies ran while one was open for 3% of the time, Pallas kernels for 9%

profile of v4, /device:TPU:8, one launch (start us, length us, event | category | flops | bytes accessed | tf_op | source)
XLA Modules:
  0.0 201.9 jit_solution(16620204465511034531)
XLA Ops:
  0.6 0.0 copy-start
  0.6 0.8 convert_element_type.3
  1.5 1.0 concatenate.3
  2.4 9.5 %collective-permute-start = (f32[1,1664]{1,0:T(1,128)S(1)}, f32[1,1664]{1,0:T(1,128)S(1)}, u32[]{:S(2)}, u32[]{:S(2)}) collective-permute-start(f32[1,1664]{1,0:T(1,128)S(1)} %concatenate.3), channel_id=1, source_target_pairs={{0,240},{16,16},{32,32},{48,192},{64,176},{80,80},{96,96},{112,128... | collective-permute-start | bytes 19976 | tf_op jit(solution)/shard_map/ppermute | solution.py:30
  11.9 0.1 collective-permute-start.1
  12.0 1.2 slice.18
  13.2 1.6 collective-permute-start.2
  14.8 1.3 fusion
  16.1 1.7 slice.17
  17.8 0.0 collective-permute-done.gain_ref.tail_ref
  17.8 0.7 collective-permute-start.3
  18.5 1.5 collective-permute-start.4
  20.0 2.4 %collective-permute-start.5 = (bf16[1,1,3,288,1536]{4,3,2,1,0:T(8,128)(2,1)}, bf16[1,1,3,288,1536]{4,3,2,1,0:T(8,128)(2,1)S(1)}, u32[]{:S(2)}, u32[]{:S(2)}) collective-permute-start(bf16[1,1,3,288,1536]{4,3,2,1,0:T(8,128)(2,1)} %slice.17), channel_id=1, source_target_pairs={{0,0},{16,224},{32,208},{48,48},{64,64},{80,160},{96,144},{112,112... | collective-permute-start | bytes 7962632 | tf_op jit(solution)/shard_map/ppermute | solution.py:30
  22.4 0.0 collective-permute-done.3.low_ref
  22.4 0.0 collective-permute-done.4.high_ref
  22.5 5.1 %forward.1 = bf16[1,1,384,1536]{3,2,1,0:T(8,128)(2,1)} custom-call(bf16[1,1,3,384,1536]{4,3,2,1,0:T(8,128)(2,1)} %v_ref.1, bf16[1,1,3,384,1536]{4,3,2,1,0:T(8,128)(2,1)} %v_ref.1, bf16[1,1,3,384,1536]{4,3,2,1,0:T(8,128)(2,1)} %v_ref.1, f32[1,1664]{1,0:T(1,128)} %copy-done.5, f32[1,1664]{1,0:T(1,128)} %copy-done.5, s32[1,8]{1,0:T(1,128)} %lengths_ref.3), custom_call_target="tpu_custom_call" | custom-call | flops 99999997952 | bytes 4718592 | tf_op jit(solution)/shard_map/forward/pallas_call | solution.py:133
  27.5 39.9 %collective-permute-start.9 = (bf16[1,1,384,1536]{3,2,1,0:T(8,128)(2,1)}, bf16[1,1,384,1536]{3,2,1,0:T(8,128)(2,1)}, u32[]{:S(2)}, u32[]{:S(2)}) collective-permute-start(bf16[1,1,384,1536]{3,2,1,0:T(8,128)(2,1)} %forward.1), channel_id=1, source_target_pairs={{0,16},{16,32},{32,48},{48,64},{64,80},{80,96},{96,112},{112,128},... | collective-permute-start | bytes 3538952 | tf_op jit(solution)/shard_map/ppermute | solution.py:30
  67.5 0.0 collective-permute-done.5.rest_ref
  67.5 1.5 copy-done.1
  69.0 8.1 %backward.1 = (bf16[1,1,3,384,1536]{4,3,2,1,0:T(8,128)(2,1)}, f32[1,1536]{1,0:T(1,128)}) custom-call(bf16[1,1,3,96,1536]{4,3,2,1,0:T(8,128)(2,1)} %collective-permute-done.2.first_ref, bf16[1,1,3,288,1536]{4,3,2,1,0:T(8,128)(2,1)} %copy-done.1, bf16[1,1,192,1536]{3,2,1,0:T(8,128)(2,1)} %copy-done.2, ...), custom_call_target="tpu_custom_call" | custom-call | flops 589824 | bytes 589824 | tf_op jit(solution)/shard_map/backward/pallas_call | solution.py:150
  77.1 0.0 collective-permute-start.6
  77.1 1.4 collective-permute-done.6
  78.4 0.7 add.27
  79.1 1.3 collective-permute-start.7
  80.5 2.3 %collective-permute-done.7 = f32[1,1536]{1,0:T(1,128)S(1)} collective-permute-done((f32[1,1536]{1,0:T(1,128)S(1)}, f32[1,1536]{1,0:T(1,128)S(1)}, u32[]{:S(2)}, u32[]{:S(2)}) %collective-permute-start.7) | collective-permute-done | bytes 6176 | tf_op jit(solution)/shard_map/ppermute | solution.py:37
  82.8 0.0 copy-start.4
  82.8 7.6 %collective-permute-start.8 = (f32[1,1536]{1,0:T(1,128)S(1)}, f32[1,1536]{1,0:T(1,128)S(1)}, u32[]{:S(2)}, u32[]{:S(2)}) collective-permute-start(f32[1,1536]{1,0:T(1,128)S(1)} %add.28.total_ref), channel_id=1, source_target_pairs={{0,240},{16,16},{32,32},{48,192},{64,176},{80,80},{96,96},{112,128... | collective-permute-start | bytes 18440 | tf_op jit(solution)/shard_map/ppermute | solution.py:30
  90.4 1.9 collective-permute-start.10
  92.3 32.0 %collective-permute-done.9.in_ref = bf16[1,1,384,1536]{3,2,1,0:T(8,128)(2,1)} collective-permute-done((bf16[1,1,384,1536]{3,2,1,0:T(8,128)(2,1)}, bf16[1,1,384,1536]{3,2,1,0:T(8,128)(2,1)}, u32[]{:S(2)}, u32[]{:S(2)}) %collective-permute-start.9) | collective-permute-done | bytes 1179680 | tf_op jit(solution)/shard_map/ppermute | solution.py:30
  124.3 3.4 %settle.1 = bf16[1,1,384,1536]{3,2,1,0:T(8,128)(2,1)} custom-call(bf16[1,1,384,1536]{3,2,1,0:T(8,128)(2,1)} %collective-permute-done.9.in_ref), custom_call_target="tpu_custom_call" | custom-call | flops 99999997952 | bytes 2359296 | tf_op jit(solution)/shard_map/settle/pallas_call | solution.py:181
  127.7 0.0 collective-permute-done.8
  127.7 1.3 squares.1
  129.0 1.5 collective-permute-start.11
  130.5 2.3 %collective-permute-done.11 = f32[1,128]{1,0:T(1,128)S(1)} collective-permute-done((f32[1,128]{1,0:T(1,128)}, f32[1,128]{1,0:T(1,128)S(1)}, u32[]{:S(2)}, u32[]{:S(2)}) %collective-permute-start.11) | collective-permute-done | bytes 544 | tf_op jit(solution)/shard_map/ppermute | solution.py:37
  132.8 0.6 add.29
  133.4 3.0 %collective-permute-start.12 = (f32[1,128]{1,0:T(1,128)S(1)}, f32[1,128]{1,0:T(1,128)S(1)}, u32[]{:S(2)}, u32[]{:S(2)}) collective-permute-start(f32[1,128]{1,0:T(1,128)S(1)} %add.29), channel_id=1, source_target_pairs={{0,8},{4,12},{8,0},{12,4},{1,9},{5,13},{9,1},{13,5},{2,10},{6,14},... | collective-permute-start | bytes 1544 | tf_op jit(solution)/shard_map/ppermute | solution.py:37
  136.4 2.0 %collective-permute-done.12 = f32[1,128]{1,0:T(1,128)S(1)} collective-permute-done((f32[1,128]{1,0:T(1,128)S(1)}, f32[1,128]{1,0:T(1,128)S(1)}, u32[]{:S(2)}, u32[]{:S(2)}) %collective-permute-start.12) | collective-permute-done | bytes 544 | tf_op jit(solution)/shard_map/ppermute | solution.py:37
  138.4 12.4 %collective-permute-start.13 = (f32[1,128]{1,0:T(1,128)S(1)}, f32[1,128]{1,0:T(1,128)S(1)}, u32[]{:S(2)}, u32[]{:S(2)}) collective-permute-start(f32[1,128]{1,0:T(1,128)S(1)} %add.30), channel_id=1, source_target_pairs={{0,16},{16,0},{32,48},{48,32},{64,80},{80,64},{96,112},{112,96},{1... | collective-permute-start | bytes 1544 | tf_op jit(solution)/shard_map/ppermute | solution.py:37
  150.9 1.5 collective-permute-done.13
  152.4 4.6 %collective-permute-start.14 = (f32[1,128]{1,0:T(1,128)S(1)}, f32[1,128]{1,0:T(1,128)S(1)}, u32[]{:S(2)}, u32[]{:S(2)}) collective-permute-start(f32[1,128]{1,0:T(1,128)S(1)} %add.31), channel_id=1, source_target_pairs={{0,32},{16,48},{32,0},{48,16},{64,96},{80,112},{96,64},{112,80},{1... | collective-permute-start | bytes 1544 | tf_op jit(solution)/shard_map/ppermute | solution.py:37
  157.0 1.5 collective-permute-done.14
  158.5 4.5 %collective-permute-start.15 = (f32[1,128]{1,0:T(1,128)S(1)}, f32[1,128]{1,0:T(1,128)S(1)}, u32[]{:S(2)}, u32[]{:S(2)}) collective-permute-start(f32[1,128]{1,0:T(1,128)S(1)} %add.32), channel_id=1, source_target_pairs={{0,64},{16,80},{32,96},{48,112},{64,0},{80,16},{96,32},{112,48},{1... | collective-permute-start | bytes 1544 | tf_op jit(solution)/shard_map/ppermute | solution.py:37
  163.0 3.0 %collective-permute-done.15 = f32[1,128]{1,0:T(1,128)S(1)} collective-permute-done((f32[1,128]{1,0:T(1,128)S(1)}, f32[1,128]{1,0:T(1,128)S(1)}, u32[]{:S(2)}, u32[]{:S(2)}) %collective-permute-start.15) | collective-permute-done | bytes 544 | tf_op jit(solution)/shard_map/ppermute | solution.py:37
  165.9 2.3 %collective-permute-start.16 = (f32[1,128]{1,0:T(1,128)S(1)}, f32[1,128]{1,0:T(1,128)S(1)}, u32[]{:S(2)}, u32[]{:S(2)}) collective-permute-start(f32[1,128]{1,0:T(1,128)S(1)} %add.33), channel_id=1, source_target_pairs={{0,128},{16,144},{32,160},{48,176},{64,192},{80,208},{96,224},{112... | collective-permute-start | bytes 1544 | tf_op jit(solution)/shard_map/ppermute | solution.py:37
  168.2 2.8 %collective-permute-done.16 = f32[1,128]{1,0:T(1,128)S(1)} collective-permute-done((f32[1,128]{1,0:T(1,128)S(1)}, f32[1,128]{1,0:T(1,128)S(1)}, u32[]{:S(2)}, u32[]{:S(2)}) %collective-permute-start.16) | collective-permute-done | bytes 544 | tf_op jit(solution)/shard_map/ppermute | solution.py:37
  171.1 0.6 broadcast_divide_fusion
  171.7 28.4 %collective-permute-done.10 = bf16[1,1,3,384,1536]{4,3,2,1,0:T(8,128)(2,1)S(1)} collective-permute-done((bf16[1,1,3,384,1536]{4,3,2,1,0:T(8,128)(2,1)}, bf16[1,1,3,384,1536]{4,3,2,1,0:T(8,128)(2,1)S(1)}, u32[]{:S(2)}, u32[]{:S(2)}) %collective-permute-start.10) | collective-permute-done | bytes 3538976 | tf_op jit(solution)/shard_map/ppermute | solution.py:30
  200.1 1.8 copy.10
  (18 shorter events, 0.0 us)
Async XLA Ops:
  0.6 15.5 %copy-start = (bf16[1,1,3,384,1536]{4,3,2,1,0:T(8,128)(2,1)S(1)}, bf16[1,1,3,384,1536]{4,3,2,1,0:T(8,128)(2,1)}, u32[]{:S(2)}) copy-start(bf16[1,1,3,384,1536]{4,3,2,1,0:T(8,128)(2,1)} %param.7) | copy-start | bytes 10616836
  2.4 15.4 %collective-permute-start = (f32[1,1664]{1,0:T(1,128)S(1)}, f32[1,1664]{1,0:T(1,128)S(1)}, u32[]{:S(2)}, u32[]{:S(2)}) collective-permute-start(f32[1,1664]{1,0:T(1,128)S(1)} %concatenate.3), channel_id=1, source_target_pairs={{0,240},{16,16},{32,32},{48,192},{64,176},{80,80},{96,96},{112,128... | collective-permute-start | bytes 19976 | tf_op jit(solution)/shard_map/ppermute | solution.py:30
  11.9 5.9 %collective-permute-start.1 = (f32[1,1664]{1,0:T(1,128)S(1)}, f32[1,1664]{1,0:T(1,128)S(1)}, u32[]{:S(2)}, u32[]{:S(2)}) collective-permute-start(f32[1,1664]{1,0:T(1,128)S(1)} %concatenate.3), channel_id=1, source_target_pairs={{0,240},{16,0},{32,16},{48,32},{64,48},{80,64},{96,80},{112,96},{1... | collective-permute-start | bytes 19976 | tf_op jit(solution)/shard_map/ppermute | solution.py:30
  13.2 9.2 %collective-permute-start.2 = (bf16[1,1,3,96,1536]{4,3,2,1,0:T(8,128)(2,1)S(1)}, bf16[1,1,3,96,1536]{4,3,2,1,0:T(8,128)(2,1)}, u32[]{:S(2)}, u32[]{:S(2)}) collective-permute-start(bf16[1,1,3,96,1536]{4,3,2,1,0:T(8,128)(2,1)S(1)} %slice.18), channel_id=1, source_target_pairs={{0,0},{16,224},{32,208},{48,48},{64,64},{80,160},{96,144},{112,112... | collective-permute-start | bytes 2654216 | tf_op jit(solution)/shard_map/ppermute | solution.py:30
  17.8 9.7 %copy-start.3 = (f32[1,1664]{1,0:T(1,128)}, f32[1,1664]{1,0:T(1,128)S(1)}, u32[]{:S(2)}) copy-start(f32[1,1664]{1,0:T(1,128)S(1)} %collective-permute-done.gain_ref.tail_ref) | copy-start | bytes 19972
  17.8 4.6 %copy-start.5 = (f32[1,1664]{1,0:T(1,128)}, f32[1,1664]{1,0:T(1,128)S(1)}, u32[]{:S(2)}) copy-start(f32[1,1664]{1,0:T(1,128)S(1)} %collective-permute-done.1.gain_ref.tail_ref) | copy-start | bytes 19972
  17.8 4.6 %collective-permute-start.3 = (bf16[1,1,192,1536]{3,2,1,0:T(8,128)(2,1)S(1)}, bf16[1,1,192,1536]{3,2,1,0:T(8,128)(2,1)S(1)}, u32[]{:S(2)}, u32[]{:S(2)}) collective-permute-start(bf16[1,1,192,1536]{3,2,1,0:T(8,128)(2,1)S(1)} %get-tuple-element.24), channel_id=1, source_target_pairs={{0,0},{16,240},{32,16},{48,32},{64,192},{80,176},{96,80},{112,96},... | collective-permute-start | bytes 1769480 | tf_op jit(solution)/shard_map/ppermute | solution.py:30
  18.5 3.9 %collective-permute-start.4 = (bf16[1,1,192,1536]{3,2,1,0:T(8,128)(2,1)S(1)}, bf16[1,1,192,1536]{3,2,1,0:T(8,128)(2,1)}, u32[]{:S(2)}, u32[]{:S(2)}) collective-permute-start(bf16[1,1,192,1536]{3,2,1,0:T(8,128)(2,1)S(1)} %get-tuple-element.25), channel_id=1, source_target_pairs={{0,0},{16,240},{32,16},{48,32},{64,192},{80,176},{96,80},{112,96},... | collective-permute-start | bytes 1769480 | tf_op jit(solution)/shard_map/ppermute | solution.py:30
  20.0 47.5 %collective-permute-start.5 = (bf16[1,1,3,288,1536]{4,3,2,1,0:T(8,128)(2,1)}, bf16[1,1,3,288,1536]{4,3,2,1,0:T(8,128)(2,1)S(1)}, u32[]{:S(2)}, u32[]{:S(2)}) collective-permute-start(bf16[1,1,3,288,1536]{4,3,2,1,0:T(8,128)(2,1)} %slice.17), channel_id=1, source_target_pairs={{0,0},{16,224},{32,208},{48,48},{64,64},{80,160},{96,144},{112,112... | collective-permute-start | bytes 7962632 | tf_op jit(solution)/shard_map/ppermute | solution.py:30
  22.4 5.1 %copy-start.2 = (bf16[1,1,192,1536]{3,2,1,0:T(8,128)(2,1)}, bf16[1,1,192,1536]{3,2,1,0:T(8,128)(2,1)S(1)}, u32[]{:S(2)}) copy-start(bf16[1,1,192,1536]{3,2,1,0:T(8,128)(2,1)S(1)} %collective-permute-done.3.low_ref) | copy-start | bytes 1769476
  27.5 96.8 %collective-permute-start.9 = (bf16[1,1,384,1536]{3,2,1,0:T(8,128)(2,1)}, bf16[1,1,384,1536]{3,2,1,0:T(8,128)(2,1)}, u32[]{:S(2)}, u32[]{:S(2)}) collective-permute-start(bf16[1,1,384,1536]{3,2,1,0:T(8,128)(2,1)} %forward.1), channel_id=1, source_target_pairs={{0,16},{16,32},{32,48},{48,64},{64,80},{80,96},{96,112},{112,128},... | collective-permute-start | bytes 3538952 | tf_op jit(solution)/shard_map/ppermute | solution.py:30
  67.5 1.5 copy-start.1
  77.1 1.4 collective-permute-start.6
  79.1 3.6 %collective-permute-start.7 = (f32[1,1536]{1,0:T(1,128)S(1)}, f32[1,1536]{1,0:T(1,128)S(1)}, u32[]{:S(2)}, u32[]{:S(2)}) collective-permute-start(f32[1,1536]{1,0:T(1,128)S(1)} %add.27), channel_id=1, source_target_pairs={{0,2},{1,3},{2,0},{3,1},{4,6},{5,7},{6,4},{7,5},{8,10},{9,11},{10,... | collective-permute-start | bytes 18440 | tf_op jit(solution)/shard_map/ppermute | solution.py:37
  82.8 44.9 %copy-start.4 = (f32[1,1536]{1,0:T(1,128)}, f32[1,1536]{1,0:T(1,128)S(1)}, u32[]{:S(2)}) copy-start(f32[1,1536]{1,0:T(1,128)S(1)} %add.28.total_ref) | copy-start | bytes 18436
  82.8 44.9 %collective-permute-start.8 = (f32[1,1536]{1,0:T(1,128)S(1)}, f32[1,1536]{1,0:T(1,128)S(1)}, u32[]{:S(2)}, u32[]{:S(2)}) collective-permute-start(f32[1,1536]{1,0:T(1,128)S(1)} %add.28.total_ref), channel_id=1, source_target_pairs={{0,240},{16,16},{32,32},{48,192},{64,176},{80,80},{96,96},{112,128... | collective-permute-start | bytes 18440 | tf_op jit(solution)/shard_map/ppermute | solution.py:30
  90.4 109.7 %collective-permute-start.10 = (bf16[1,1,3,384,1536]{4,3,2,1,0:T(8,128)(2,1)}, bf16[1,1,3,384,1536]{4,3,2,1,0:T(8,128)(2,1)S(1)}, u32[]{:S(2)}, u32[]{:S(2)}) collective-permute-start(bf16[1,1,3,384,1536]{4,3,2,1,0:T(8,128)(2,1)} %get-tuple-element.40), channel_id=1, source_target_pairs={{0,240},{16,16},{32,32},{48,192},{64,176},{80,80},{96,96},{112,128... | collective-permute-start | bytes 10616840 | tf_op jit(solution)/shard_map/ppermute | solution.py:30
  129.0 3.8 %collective-permute-start.11 = (f32[1,128]{1,0:T(1,128)}, f32[1,128]{1,0:T(1,128)S(1)}, u32[]{:S(2)}, u32[]{:S(2)}) collective-permute-start(f32[1,128]{1,0:T(1,128)} %squares.1), channel_id=1, source_target_pairs={{0,4},{4,0},{8,12},{12,8},{1,5},{5,1},{9,13},{13,9},{2,6},{6,2},{1... | collective-permute-start | bytes 1544 | tf_op jit(solution)/shard_map/ppermute | solution.py:37
  133.4 5.0 %collective-permute-start.12 = (f32[1,128]{1,0:T(1,128)S(1)}, f32[1,128]{1,0:T(1,128)S(1)}, u32[]{:S(2)}, u32[]{:S(2)}) collective-permute-start(f32[1,128]{1,0:T(1,128)S(1)} %add.29), channel_id=1, source_target_pairs={{0,8},{4,12},{8,0},{12,4},{1,9},{5,13},{9,1},{13,5},{2,10},{6,14},... | collective-permute-start | bytes 1544 | tf_op jit(solution)/shard_map/ppermute | solution.py:37
  138.4 14.0 %collective-permute-start.13 = (f32[1,128]{1,0:T(1,128)S(1)}, f32[1,128]{1,0:T(1,128)S(1)}, u32[]{:S(2)}, u32[]{:S(2)}) collective-permute-start(f32[1,128]{1,0:T(1,128)S(1)} %add.30), channel_id=1, source_target_pairs={{0,16},{16,0},{32,48},{48,32},{64,80},{80,64},{96,112},{112,96},{1... | collective-permute-start | bytes 1544 | tf_op jit(solution)/shard_map/ppermute | solution.py:37
  152.4 6.1 %collective-permute-start.14 = (f32[1,128]{1,0:T(1,128)S(1)}, f32[1,128]{1,0:T(1,128)S(1)}, u32[]{:S(2)}, u32[]{:S(2)}) collective-permute-start(f32[1,128]{1,0:T(1,128)S(1)} %add.31), channel_id=1, source_target_pairs={{0,32},{16,48},{32,0},{48,16},{64,96},{80,112},{96,64},{112,80},{1... | collective-permute-start | bytes 1544 | tf_op jit(solution)/shard_map/ppermute | solution.py:37
  158.5 7.4 %collective-permute-start.15 = (f32[1,128]{1,0:T(1,128)S(1)}, f32[1,128]{1,0:T(1,128)S(1)}, u32[]{:S(2)}, u32[]{:S(2)}) collective-permute-start(f32[1,128]{1,0:T(1,128)S(1)} %add.32), channel_id=1, source_target_pairs={{0,64},{16,80},{32,96},{48,112},{64,0},{80,16},{96,32},{112,48},{1... | collective-permute-start | bytes 1544 | tf_op jit(solution)/shard_map/ppermute | solution.py:37
  165.9 5.0 %collective-permute-start.16 = (f32[1,128]{1,0:T(1,128)S(1)}, f32[1,128]{1,0:T(1,128)S(1)}, u32[]{:S(2)}, u32[]{:S(2)}) collective-permute-start(f32[1,128]{1,0:T(1,128)S(1)} %add.33), channel_id=1, source_target_pairs={{0,128},{16,144},{32,160},{48,176},{64,192},{80,208},{96,224},{112... | collective-permute-start | bytes 1544 | tf_op jit(solution)/shard_map/ppermute | solution.py:37

commit v5 on v4

--- a/solution.py
+++ b/solution.py
@@ -11,7 +11,6 @@
 BLOCK = 128
 FORWARD_HEADS = 6
 BACKWARD_HEADS = 3
-FIRST = 96
 NEG = -1e30
 SCALE = HD**-0.5
 LOG2E = 1.4426950408889634
@@ -25,9 +24,22 @@
     return s if s % (n // 2) in (1, 2, 5, 6) else n - 1 - s
 
 
-def moved(value, target):
+UPWARD = (2, 6)
+DOWNWARD = (0, 1, 3, 4, 5, 7)
+
+
+def moved(value, target, kept=None):
     size = lax.axis_size("section")
-    return lax.ppermute(value, "section", [(i, target(i, size) % size) for i in range(size)])
+    pairs = [(i, target(i, size) % size) for i in range(size) if kept is None or i % (size // 2) in kept]
+    return lax.ppermute(value, "section", pairs)
+
+
+def replica_sum(value):
+    size = lax.axis_size("dp")
+    value = value + lax.ppermute(value, "dp", [(i, i ^ 1) for i in range(size)])
+    odd = value + lax.ppermute(value, "dp", [(i, i ^ 2) for i in range(1, size, 2)])
+    even = lax.ppermute(odd, "dp", [(i, i ^ 1) for i in range(1, size, 2)])
+    return jnp.where(lax.axis_index("dp") % 2 == 1, odd, even)
 
 
 def doubled_sum(value, axis):
@@ -73,15 +85,15 @@
         out_ref[start : start + BLOCK, hs] = out.astype(jnp.bfloat16)
 
 
-def backward_kernel(first_ref, rest_ref, low_ref, high_ref, gain_ref, tail_ref, lengths_ref, out_ref, raw_ref):
+def backward_kernel(ups_ref, downs_ref, g_ref, gain_ref, tail_ref, lengths_ref, out_ref, raw_ref):
     length = row_length(tail_ref, lengths_ref, 1)
-    seq = 2 * low_ref.shape[0]
-    heads = [slice(h * HD, (h + 1) * HD) for h in range(low_ref.shape[1] // HD)]
+    seq = g_ref.shape[0]
+    heads = [slice(h * HD, (h + 1) * HD) for h in range(g_ref.shape[1] // HD)]
     starts = range(0, seq, BLOCK)
     loaded = []
     for hs in heads:
-        q, k, v = (jnp.concatenate([first_ref[part, :, hs], rest_ref[part, :, hs]], axis=0) for part in range(3))
-        g = jnp.concatenate([low_ref[:, hs], high_ref[:, hs]], axis=0)
+        q, k, v = (ups_ref[part, :, hs] + downs_ref[part, :, hs] for part in range(3))
+        g = g_ref[:, hs]
         qs = (q.astype(jnp.float32) * gain_ref[:, hs]).astype(jnp.bfloat16)
         loaded.append((q, k, v, g, qs))
     units = [(h, start, start + BLOCK) for h in range(len(heads)) for start in starts]
@@ -137,23 +149,22 @@
         out_specs=pl.BlockSpec((None, None, seq, width), lambda h: (0, 0, 0, h)),
         out_shape=jax.ShapeDtypeStruct((1, 1, seq, features), jnp.bfloat16),
         cost_estimate=pl.CostEstimate(
-            flops=FAR, bytes_accessed=8 * seq * features, transcendentals=heads * seq * seq
+            flops=2 * heads * seq * seq * HD, bytes_accessed=8 * seq * features, transcendentals=heads * seq * seq // 2
         ),
         name="forward",
     )(block, block, block, aux, aux, lengths)
 
 
-def backward_part(first, rest, upstream, aux, lengths):
-    seq, features = FIRST + rest.shape[3], rest.shape[4]
+def backward_part(ups, downs, upstream, aux, lengths):
+    seq, features = upstream.shape[2:]
     width = BACKWARD_HEADS * HD
     heads = features // HD
     return pl.pallas_call(
         backward_kernel,
         grid=(features // width,),
         in_specs=[
-            pl.BlockSpec((None, None, 3, FIRST, width), lambda h: (0, 0, 0, 0, h)),
-            pl.BlockSpec((None, None, 3, seq - FIRST, width), lambda h: (0, 0, 0, 0, h)),
-            *[pl.BlockSpec((None, None, seq // 2, width), lambda h: (0, 0, 0, h))] * 2,
+            *[pl.BlockSpec((None, None, 3, seq, width), lambda h: (0, 0, 0, 0, h))] * 2,
+            pl.BlockSpec((None, None, seq, width), lambda h: (0, 0, 0, h)),
             *small_specs(width, features, lengths),
         ],
         out_specs=[
@@ -168,7 +179,24 @@
             flops=heads * seq * HD, bytes_accessed=seq * features, transcendentals=heads * seq
         ),
         name="backward",
-    )(first, rest, *upstream, aux, aux, lengths)
+    )(ups, downs, upstream, aux, aux, lengths)
+
+
+def merge_kernel(down_ref, up_ref, ups_ref, out_ref):
+    out_ref[...] = down_ref[...] + up_ref[...]
+
+
+def merged(down, up, ups):
+    whole = pl.BlockSpec(down.shape, lambda i: (0, 0))
+    return pl.pallas_call(
+        merge_kernel,
+        grid=(1,),
+        in_specs=[whole, whole, pl.BlockSpec((None, None, None, 16, HD), lambda i: (0, 0, 0, 0, 0))],
+        out_specs=whole,
+        out_shape=jax.ShapeDtypeStruct(down.shape, down.dtype),
+        cost_estimate=pl.CostEstimate(flops=FAR, bytes_accessed=12 * down.size, transcendentals=0),
+        name="merge",
+    )(down, up, ups)
 
 
 def settle_kernel(in_ref, out_ref):
@@ -208,21 +236,20 @@
     aux = jnp.concatenate(
         [query_gain, plan.astype(jnp.float32), jnp.zeros((1, HD - entries), jnp.float32)], axis=1
     )
-    aux_back = moved(aux, lambda s, n: site(s, n))
+    ups = moved(parked, lambda s, n: site(n - 1 - s, n), UPWARD)
     aux_ahead = moved(aux, lambda s, n: s - 1)
-    first = moved(parked[:, :, :, :FIRST], lambda s, n: site(n - 1 - s, n))
-    half = grad_out.shape[2] // 2
-    low, high, rest, aux_back, aux_ahead = lax.optimization_barrier(
-        (grad_out[:, :, :half], grad_out[:, :, half:], parked[:, :, :, FIRST:], aux_back, aux_ahead)
-    )
-    rest = moved(rest, lambda s, n: site(n - 1 - s, n))
-    upstream = [moved(part, lambda s, n: site((s - 1) % n, n)) for part in (low, high)]
-    aux_ahead, first, upstream = lax.optimization_barrier((aux_ahead, first, upstream))
+    aux_up = moved(aux, lambda s, n: site(s, n), (1, 2, 3, 5, 6, 7))
+    aux_down = moved(aux, lambda s, n: n - 1 - s, (0, 4))
+    grad_out, parked, aux_down, aux_ahead = lax.optimization_barrier((grad_out, parked, aux_down, aux_ahead))
+    downs = moved(parked, lambda s, n: site(n - 1 - s, n), DOWNWARD)
+    upstream = moved(grad_out, lambda s, n: site((s - 1) % n, n))
+    aux_ahead, upstream = lax.optimization_barrier((aux_ahead, upstream))
     attended = forward_part(inbound, aux_ahead, lengths)
-    _, first, rest, upstream = lax.optimization_barrier((attended, first, rest, upstream))
+    aux_back = merged(aux_down, aux_up, ups)
+    _, aux_back, downs, upstream = lax.optimization_barrier((attended, aux_back, downs, upstream))
     attended = moved(attended, lambda s, n: s + 1)
-    grads, raw = backward_part(first, rest, upstream, aux_back, lengths)
-    total = doubled_sum(raw, "dp")
+    grads, raw = backward_part(ups, downs, upstream, aux_back, lengths)
+    total = replica_sum(raw)
     grads, total = lax.optimization_barrier((grads, total))
     own_total = moved(total, lambda s, n: site(s, n))
     grads = moved(grads, lambda s, n: site(s, n))

time: 204 us -> 206 us (level)
  the two profiles are of different devices: /device:TPU:8 before, /device:TPU:1 now
where the time goes in v5:
time: 206 us; the launch traced here: 203 us
  starting transfers between devices  113 us (55%)
  waiting for transfers between devices  61.6 us (30%)
  Pallas kernels  19.8 us (10%)
  local copies, waits for them, and re-layouts  4.38 us (2%)
  other arithmetic  2.65 us (1%)
    ppermute x9, starting transfers between devices, moved(): return lax.ppermute(value, 'section', pairs)  60.6 us
    ppermute x9, waiting for transfers between devices, moved(): return lax.ppermute(value, 'section', pairs)  45.5 us
    ppermute x6, starting transfers between devices, doubled_sum(): lax.ppermute(value, axis, [(i, i ^ step) for i in range(size)])  43.1 us
    ppermute x6, waiting for transfers between devices, doubled_sum(): lax.ppermute(value, axis, [(i, i ^ step) for i in range(size)])  13.2 us
    pallas_call x1, Pallas kernels, backward_part(): pl.pallas_call(backward_kernel, grid=(features // width,), in_specs=[*[pl...  8.95 us
    ppermute x1, starting transfers between devices, replica_sum(): value = value + lax.ppermute(value, 'dp', [(i, i ^ 1) for i in range(size)])  5.1 us
    pallas_call x1, Pallas kernels, forward_part(): pl.pallas_call(forward_kernel, grid=(features // width,), in_specs=[*part...  4.89 us
  transfers between devices with their start and end apart: 18, of which 13 were waited for; matrix products, arithmetic and copies ran while one was open for 2% of the time, Pallas kernels for 10%

profile of v5, /device:TPU:1, one launch (start us, length us, event | category | flops | bytes accessed | tf_op | source)
XLA Modules:
  0.0 202.6 jit_solution(5731877319594426865)
XLA Ops:
  0.6 0.9 collective-permute-start
  1.5 0.7 convert_element_type.3
  2.2 0.8 concatenate.3
  3.0 10.9 %collective-permute-start.1 = (f32[1,1664]{1,0:T(1,128)S(1)}, f32[1,1664]{1,0:T(1,128)S(1)}, u32[]{:S(2)}, u32[]{:S(2)}) collective-permute-start(f32[1,1664]{1,0:T(1,128)S(1)} %concatenate.3), channel_id=1, source_target_pairs={{0,240},{64,176},{128,112},{192,48},{1,241},{65,177},{129,113},{19... | collective-permute-start | bytes 19976 | tf_op jit(solution)/shard_map/ppermute | solution.py:34
  13.9 0.1 collective-permute-start.2
  14.0 0.7 collective-permute-done.1.down_ref
  14.7 1.8 collective-permute-done.2.gain_ref.tail_ref
  16.5 10.4 %collective-permute-start.3 = (bf16[1,1,384,1536]{3,2,1,0:T(8,128)(2,1)}, bf16[1,1,384,1536]{3,2,1,0:T(8,128)(2,1)}, u32[]{:S(2)}, u32[]{:S(2)}) collective-permute-start(bf16[1,1,384,1536]{3,2,1,0:T(8,128)(2,1)} %param.8), channel_id=1, source_target_pairs={{0,0},{16,240},{32,16},{48,32},{64,192},{80,176},{96,80},{112,96},... | collective-permute-start | bytes 3538952 | tf_op jit(solution)/shard_map/ppermute | solution.py:34
  26.9 1.3 collective-permute-start.4
  28.2 28.1 %collective-permute-start.5 = (bf16[1,1,3,384,1536]{4,3,2,1,0:T(8,128)(2,1)}, bf16[1,1,3,384,1536]{4,3,2,1,0:T(8,128)(2,1)}, u32[]{:S(2)}, u32[]{:S(2)}) collective-permute-start(bf16[1,1,3,384,1536]{4,3,2,1,0:T(8,128)(2,1)} %param.7), channel_id=1, source_target_pairs={{0,0},{16,224},{48,48},{64,64},{80,160},{112,112},{128,128},{144,9... | collective-permute-start | bytes 10616840 | tf_op jit(solution)/shard_map/ppermute | solution.py:34
  56.3 0.0 collective-permute-done.3.g_ref
  56.3 4.9 %forward.1 = bf16[1,1,384,1536]{3,2,1,0:T(8,128)(2,1)} custom-call(bf16[1,1,3,384,1536]{4,3,2,1,0:T(8,128)(2,1)} %v_ref.1, bf16[1,1,3,384,1536]{4,3,2,1,0:T(8,128)(2,1)} %v_ref.1, bf16[1,1,3,384,1536]{4,3,2,1,0:T(8,128)(2,1)} %v_ref.1, f32[1,1664]{1,0:T(1,128)} %copy-done.1, f32[1,1664]{1,0:T(1,128)} %copy-done.1, s32[1,8]{1,0:T(1,128)} %lengths_ref.3), custom_call_target="tpu_custom_call" | custom-call | flops 452984832 | bytes 4718592 | tf_op jit(solution)/shard_map/forward/pallas_call | solution.py:145
  61.2 0.0 collective-permute-start.10
  61.2 0.0 collective-permute-done.ups_ref
  61.2 0.0 copy-start
  61.2 1.8 copy-done
  63.0 1.3 merge.1.gain_ref.tail_ref
  64.3 0.0 collective-permute-done.5.downs_ref
  64.3 8.9 %backward.1 = (bf16[1,1,3,384,1536]{4,3,2,1,0:T(8,128)(2,1)}, f32[1,1536]{1,0:T(1,128)}) custom-call(bf16[1,1,3,384,1536]{4,3,2,1,0:T(8,128)(2,1)} %copy-done, bf16[1,1,3,384,1536]{4,3,2,1,0:T(8,128)(2,1)} %collective-permute-done.5.downs_ref, bf16[1,1,384,1536]{3,2,1,0:T(8,128)(2,1)} %collective-permute-done.3.g_ref, f32[1,1664]{1,0:T(1,128)} %merge.1.gain_ref.tail_ref, ...), custom_call_target="tpu_custom_call" | custom-call | flops 589824 | bytes 589824 | tf_op jit(solution)/shard_map/backward/pallas_call | solution.py:162
  73.2 5.1 %collective-permute-start.6 = (f32[1,1536]{1,0:T(1,128)}, f32[1,1536]{1,0:T(1,128)S(1)}, u32[]{:S(2)}, u32[]{:S(2)}) collective-permute-start(f32[1,1536]{1,0:T(1,128)} %get-tuple-element.29), channel_id=1, source_target_pairs={{0,1},{1,0},{2,3},{3,2},{4,5},{5,4},{6,7},{7,6},{8,9},{9,8},{10,11... | collective-permute-start | bytes 18440 | tf_op jit(solution)/shard_map/ppermute | solution.py:39
  78.3 1.0 collective-permute-done.6
  79.4 0.7 add.32
  80.1 3.2 %collective-permute-start.7 = (f32[1,1536]{1,0:T(1,128)S(1)}, f32[1,1536]{1,0:T(1,128)S(1)}, u32[]{:S(2)}, u32[]{:S(2)}) collective-permute-start(f32[1,1536]{1,0:T(1,128)S(1)} %add.32), channel_id=1, source_target_pairs={{1,3},{3,1},{5,7},{7,5},{9,11},{11,9},{13,15},{15,13},{17,19},{19,... | collective-permute-start | bytes 18440 | tf_op jit(solution)/shard_map/ppermute | solution.py:40
  83.3 1.2 collective-permute-done.7
  84.4 1.3 collective-permute-start.8
  85.8 0.8 collective-permute-done.8
  86.6 5.4 %collective-permute-start.9 = (f32[1,1536]{1,0:T(1,128)S(1)}, f32[1,1536]{1,0:T(1,128)S(1)}, u32[]{:S(2)}, u32[]{:S(2)}) collective-permute-start(f32[1,1536]{1,0:T(1,128)S(1)} %broadcast_select_fusion.total_ref), channel_id=1, source_target_pairs={{0,240},{16,16},{32,32},{48,192},{64,176},{80,80},{96,96},{112,128... | collective-permute-start | bytes 18440 | tf_op jit(solution)/shard_map/ppermute | solution.py:34
  92.0 3.5 %collective-permute-start.11 = (bf16[1,1,3,384,1536]{4,3,2,1,0:T(8,128)(2,1)}, bf16[1,1,3,384,1536]{4,3,2,1,0:T(8,128)(2,1)S(1)}, u32[]{:S(2)}, u32[]{:S(2)}) collective-permute-start(bf16[1,1,3,384,1536]{4,3,2,1,0:T(8,128)(2,1)} %get-tuple-element.32), channel_id=1, source_target_pairs={{0,240},{16,16},{32,32},{48,192},{64,176},{80,80},{96,96},{112,128... | collective-permute-start | bytes 10616840 | tf_op jit(solution)/shard_map/ppermute | solution.py:34
  95.5 18.7 %collective-permute-done.10.in_ref = bf16[1,1,384,1536]{3,2,1,0:T(8,128)(2,1)} collective-permute-done((bf16[1,1,384,1536]{3,2,1,0:T(8,128)(2,1)}, bf16[1,1,384,1536]{3,2,1,0:T(8,128)(2,1)}, u32[]{:S(2)}, u32[]{:S(2)}) %collective-permute-start.10) | collective-permute-done | bytes 1179680 | tf_op jit(solution)/shard_map/ppermute | solution.py:34
  114.2 3.4 %settle.1 = bf16[1,1,384,1536]{3,2,1,0:T(8,128)(2,1)} custom-call(bf16[1,1,384,1536]{3,2,1,0:T(8,128)(2,1)} %collective-permute-done.10.in_ref), custom_call_target="tpu_custom_call" | custom-call | flops 99999997952 | bytes 2359296 | tf_op jit(solution)/shard_map/settle/pallas_call | solution.py:209
  117.6 0.0 collective-permute-done.9
  117.6 1.3 squares.1
  118.9 1.2 collective-permute-start.12
  120.1 1.6 collective-permute-done.12
  121.7 0.7 add.34
  122.4 2.7 %collective-permute-start.13 = (f32[1,128]{1,0:T(1,128)S(1)}, f32[1,128]{1,0:T(1,128)S(1)}, u32[]{:S(2)}, u32[]{:S(2)}) collective-permute-start(f32[1,128]{1,0:T(1,128)S(1)} %add.34), channel_id=1, source_target_pairs={{0,8},{4,12},{8,0},{12,4},{1,9},{5,13},{9,1},{13,5},{2,10},{6,14},... | collective-permute-start | bytes 1544 | tf_op jit(solution)/shard_map/ppermute | solution.py:49
  125.1 1.4 collective-permute-done.13
  126.6 31.2 %collective-permute-start.14 = (f32[1,128]{1,0:T(1,128)S(1)}, f32[1,128]{1,0:T(1,128)S(1)}, u32[]{:S(2)}, u32[]{:S(2)}) collective-permute-start(f32[1,128]{1,0:T(1,128)S(1)} %add.35), channel_id=1, source_target_pairs={{0,16},{16,0},{32,48},{48,32},{64,80},{80,64},{96,112},{112,96},{1... | collective-permute-start | bytes 1544 | tf_op jit(solution)/shard_map/ppermute | solution.py:49
  157.8 1.2 collective-permute-done.14
  159.1 4.7 %collective-permute-start.15 = (f32[1,128]{1,0:T(1,128)S(1)}, f32[1,128]{1,0:T(1,128)S(1)}, u32[]{:S(2)}, u32[]{:S(2)}) collective-permute-start(f32[1,128]{1,0:T(1,128)S(1)} %add.36), channel_id=1, source_target_pairs={{0,32},{16,48},{32,0},{48,16},{64,96},{80,112},{96,64},{112,80},{1... | collective-permute-start | bytes 1544 | tf_op jit(solution)/shard_map/ppermute | solution.py:49
  163.7 1.2 collective-permute-done.15
  165.0 2.4 %collective-permute-start.16 = (f32[1,128]{1,0:T(1,128)S(1)}, f32[1,128]{1,0:T(1,128)S(1)}, u32[]{:S(2)}, u32[]{:S(2)}) collective-permute-start(f32[1,128]{1,0:T(1,128)S(1)} %add.37), channel_id=1, source_target_pairs={{0,64},{16,80},{32,96},{48,112},{64,0},{80,16},{96,32},{112,48},{1... | collective-permute-start | bytes 1544 | tf_op jit(solution)/shard_map/ppermute | solution.py:49
  167.4 4.2 %collective-permute-done.16 = f32[1,128]{1,0:T(1,128)S(1)} collective-permute-done((f32[1,128]{1,0:T(1,128)S(1)}, f32[1,128]{1,0:T(1,128)S(1)}, u32[]{:S(2)}, u32[]{:S(2)}) %collective-permute-start.16) | collective-permute-done | bytes 544 | tf_op jit(solution)/shard_map/ppermute | solution.py:49
  171.6 0.7 collective-permute-start.17
  172.3 3.5 %collective-permute-done.17 = f32[1,128]{1,0:T(1,128)S(1)} collective-permute-done((f32[1,128]{1,0:T(1,128)S(1)}, f32[1,128]{1,0:T(1,128)S(1)}, u32[]{:S(2)}, u32[]{:S(2)}) %collective-permute-start.17) | collective-permute-done | bytes 544 | tf_op jit(solution)/shard_map/ppermute | solution.py:49
  175.9 0.6 broadcast_divide_fusion
  176.5 24.3 %collective-permute-done.11 = bf16[1,1,3,384,1536]{4,3,2,1,0:T(8,128)(2,1)S(1)} collective-permute-done((bf16[1,1,3,384,1536]{4,3,2,1,0:T(8,128)(2,1)}, bf16[1,1,3,384,1536]{4,3,2,1,0:T(8,128)(2,1)S(1)}, u32[]{:S(2)}, u32[]{:S(2)}) %collective-permute-start.11) | collective-permute-done | bytes 3538976 | tf_op jit(solution)/shard_map/ppermute | solution.py:34
  200.8 1.8 copy.10
  (15 shorter events, 0.0 us)
Async XLA Ops:
  0.6 60.5 %collective-permute-start = (bf16[1,1,3,384,1536]{4,3,2,1,0:T(8,128)(2,1)}, bf16[1,1,3,384,1536]{4,3,2,1,0:T(8,128)(2,1)S(1)}, u32[]{:S(2)}, u32[]{:S(2)}) collective-permute-start(bf16[1,1,3,384,1536]{4,3,2,1,0:T(8,128)(2,1)} %param.7), channel_id=1, source_target_pairs={{32,208},{96,144},{160,80},{224,16},{33,209},{97,145},{161,81},{22... | collective-permute-start | bytes 10616840 | tf_op jit(solution)/shard_map/ppermute | solution.py:34
  3.0 11.7 %collective-permute-start.1 = (f32[1,1664]{1,0:T(1,128)S(1)}, f32[1,1664]{1,0:T(1,128)S(1)}, u32[]{:S(2)}, u32[]{:S(2)}) collective-permute-start(f32[1,1664]{1,0:T(1,128)S(1)} %concatenate.3), channel_id=1, source_target_pairs={{0,240},{64,176},{128,112},{192,48},{1,241},{65,177},{129,113},{19... | collective-permute-start | bytes 19976 | tf_op jit(solution)/shard_map/ppermute | solution.py:34
  13.9 2.6 %collective-permute-start.2 = (f32[1,1664]{1,0:T(1,128)S(1)}, f32[1,1664]{1,0:T(1,128)S(1)}, u32[]{:S(2)}, u32[]{:S(2)}) collective-permute-start(f32[1,1664]{1,0:T(1,128)S(1)} %concatenate.3), channel_id=1, source_target_pairs={{0,240},{16,0},{32,16},{48,32},{64,48},{80,64},{96,80},{112,96},{1... | collective-permute-start | bytes 19976 | tf_op jit(solution)/shard_map/ppermute | solution.py:34
  14.7 13.5 %copy-start.3 = (f32[1,1664]{1,0:T(1,128)}, f32[1,1664]{1,0:T(1,128)S(1)}, u32[]{:S(2)}) copy-start(f32[1,1664]{1,0:T(1,128)S(1)} %collective-permute-done.1.down_ref) | copy-start | bytes 19972
  16.5 39.8 %copy-start.1 = (f32[1,1664]{1,0:T(1,128)}, f32[1,1664]{1,0:T(1,128)S(1)}, u32[]{:S(2)}) copy-start(f32[1,1664]{1,0:T(1,128)S(1)} %collective-permute-done.2.gain_ref.tail_ref) | copy-start | bytes 19972
  16.5 39.8 %collective-permute-start.3 = (bf16[1,1,384,1536]{3,2,1,0:T(8,128)(2,1)}, bf16[1,1,384,1536]{3,2,1,0:T(8,128)(2,1)}, u32[]{:S(2)}, u32[]{:S(2)}) collective-permute-start(bf16[1,1,384,1536]{3,2,1,0:T(8,128)(2,1)} %param.8), channel_id=1, source_target_pairs={{0,0},{16,240},{32,16},{48,32},{64,192},{80,176},{96,80},{112,96},... | collective-permute-start | bytes 3538952 | tf_op jit(solution)/shard_map/ppermute | solution.py:34
  26.9 34.3 %collective-permute-start.4 = (f32[1,1664]{1,0:T(1,128)S(1)}, f32[1,1664]{1,0:T(1,128)}, u32[]{:S(2)}, u32[]{:S(2)}) collective-permute-start(f32[1,1664]{1,0:T(1,128)S(1)} %concatenate.3), channel_id=1, source_target_pairs={{16,16},{32,32},{48,192},{80,80},{96,96},{112,128},{144,144},{160,... | collective-permute-start | bytes 19976 | tf_op jit(solution)/shard_map/ppermute | solution.py:34
  28.2 36.1 %collective-permute-start.5 = (bf16[1,1,3,384,1536]{4,3,2,1,0:T(8,128)(2,1)}, bf16[1,1,3,384,1536]{4,3,2,1,0:T(8,128)(2,1)}, u32[]{:S(2)}, u32[]{:S(2)}) collective-permute-start(bf16[1,1,3,384,1536]{4,3,2,1,0:T(8,128)(2,1)} %param.7), channel_id=1, source_target_pairs={{0,0},{16,224},{48,48},{64,64},{80,160},{112,112},{128,128},{144,9... | collective-permute-start | bytes 10616840 | tf_op jit(solution)/shard_map/ppermute | solution.py:34
  61.2 53.0 %collective-permute-start.10 = (bf16[1,1,384,1536]{3,2,1,0:T(8,128)(2,1)}, bf16[1,1,384,1536]{3,2,1,0:T(8,128)(2,1)}, u32[]{:S(2)}, u32[]{:S(2)}) collective-permute-start(bf16[1,1,384,1536]{3,2,1,0:T(8,128)(2,1)} %forward.1), channel_id=1, source_target_pairs={{0,16},{16,32},{32,48},{48,64},{64,80},{80,96},{96,112},{112,128},... | collective-permute-start | bytes 3538952 | tf_op jit(solution)/shard_map/ppermute | solution.py:34
  61.2 1.8 copy-start
  73.2 6.1 %collective-permute-start.6 = (f32[1,1536]{1,0:T(1,128)}, f32[1,1536]{1,0:T(1,128)S(1)}, u32[]{:S(2)}, u32[]{:S(2)}) collective-permute-start(f32[1,1536]{1,0:T(1,128)} %get-tuple-element.29), channel_id=1, source_target_pairs={{0,1},{1,0},{2,3},{3,2},{4,5},{5,4},{6,7},{7,6},{8,9},{9,8},{10,11... | collective-permute-start | bytes 18440 | tf_op jit(solution)/shard_map/ppermute | solution.py:39
  80.1 4.4 %collective-permute-start.7 = (f32[1,1536]{1,0:T(1,128)S(1)}, f32[1,1536]{1,0:T(1,128)S(1)}, u32[]{:S(2)}, u32[]{:S(2)}) collective-permute-start(f32[1,1536]{1,0:T(1,128)S(1)} %add.32), channel_id=1, source_target_pairs={{1,3},{3,1},{5,7},{7,5},{9,11},{11,9},{13,15},{15,13},{17,19},{19,... | collective-permute-start | bytes 18440 | tf_op jit(solution)/shard_map/ppermute | solution.py:40
  84.4 2.1 %collective-permute-start.8 = (f32[1,1536]{1,0:T(1,128)S(1)}, f32[1,1536]{1,0:T(1,128)S(1)}, u32[]{:S(2)}, u32[]{:S(2)}) collective-permute-start(f32[1,1536]{1,0:T(1,128)S(1)} %add.33), channel_id=1, source_target_pairs={{1,0},{3,2},{5,4},{7,6},{9,8},{11,10},{13,12},{15,14},{17,16},{19,... | collective-permute-start | bytes 18440 | tf_op jit(solution)/shard_map/ppermute | solution.py:41
  86.6 31.1 %copy-start.2 = (f32[1,1536]{1,0:T(1,128)}, f32[1,1536]{1,0:T(1,128)S(1)}, u32[]{:S(2)}) copy-start(f32[1,1536]{1,0:T(1,128)S(1)} %broadcast_select_fusion.total_ref) | copy-start | bytes 18436
  86.6 31.1 %collective-permute-start.9 = (f32[1,1536]{1,0:T(1,128)S(1)}, f32[1,1536]{1,0:T(1,128)S(1)}, u32[]{:S(2)}, u32[]{:S(2)}) collective-permute-start(f32[1,1536]{1,0:T(1,128)S(1)} %broadcast_select_fusion.total_ref), channel_id=1, source_target_pairs={{0,240},{16,16},{32,32},{48,192},{64,176},{80,80},{96,96},{112,128... | collective-permute-start | bytes 18440 | tf_op jit(solution)/shard_map/ppermute | solution.py:34
  92.0 108.8 %collective-permute-start.11 = (bf16[1,1,3,384,1536]{4,3,2,1,0:T(8,128)(2,1)}, bf16[1,1,3,384,1536]{4,3,2,1,0:T(8,128)(2,1)S(1)}, u32[]{:S(2)}, u32[]{:S(2)}) collective-permute-start(bf16[1,1,3,384,1536]{4,3,2,1,0:T(8,128)(2,1)} %get-tuple-element.32), channel_id=1, source_target_pairs={{0,240},{16,16},{32,32},{48,192},{64,176},{80,80},{96,96},{112,128... | collective-permute-start | bytes 10616840 | tf_op jit(solution)/shard_map/ppermute | solution.py:34
  118.9 2.8 %collective-permute-start.12 = (f32[1,128]{1,0:T(1,128)}, f32[1,128]{1,0:T(1,128)S(1)}, u32[]{:S(2)}, u32[]{:S(2)}) collective-permute-start(f32[1,128]{1,0:T(1,128)} %squares.1), channel_id=1, source_target_pairs={{0,4},{4,0},{8,12},{12,8},{1,5},{5,1},{9,13},{13,9},{2,6},{6,2},{1... | collective-permute-start | bytes 1544 | tf_op jit(solution)/shard_map/ppermute | solution.py:49
  122.4 4.2 %collective-permute-start.13 = (f32[1,128]{1,0:T(1,128)S(1)}, f32[1,128]{1,0:T(1,128)S(1)}, u32[]{:S(2)}, u32[]{:S(2)}) collective-permute-start(f32[1,128]{1,0:T(1,128)S(1)} %add.34), channel_id=1, source_target_pairs={{0,8},{4,12},{8,0},{12,4},{1,9},{5,13},{9,1},{13,5},{2,10},{6,14},... | collective-permute-start | bytes 1544 | tf_op jit(solution)/shard_map/ppermute | solution.py:49
  126.6 32.5 %collective-permute-start.14 = (f32[1,128]{1,0:T(1,128)S(1)}, f32[1,128]{1,0:T(1,128)S(1)}, u32[]{:S(2)}, u32[]{:S(2)}) collective-permute-start(f32[1,128]{1,0:T(1,128)S(1)} %add.35), channel_id=1, source_target_pairs={{0,16},{16,0},{32,48},{48,32},{64,80},{80,64},{96,112},{112,96},{1... | collective-permute-start | bytes 1544 | tf_op jit(solution)/shard_map/ppermute | solution.py:49
  159.1 5.9 %collective-permute-start.15 = (f32[1,128]{1,0:T(1,128)S(1)}, f32[1,128]{1,0:T(1,128)S(1)}, u32[]{:S(2)}, u32[]{:S(2)}) collective-permute-start(f32[1,128]{1,0:T(1,128)S(1)} %add.36), channel_id=1, source_target_pairs={{0,32},{16,48},{32,0},{48,16},{64,96},{80,112},{96,64},{112,80},{1... | collective-permute-start | bytes 1544 | tf_op jit(solution)/shard_map/ppermute | solution.py:49
  165.0 6.6 %collective-permute-start.16 = (f32[1,128]{1,0:T(1,128)S(1)}, f32[1,128]{1,0:T(1,128)S(1)}, u32[]{:S(2)}, u32[]{:S(2)}) collective-permute-start(f32[1,128]{1,0:T(1,128)S(1)} %add.37), channel_id=1, source_target_pairs={{0,64},{16,80},{32,96},{48,112},{64,0},{80,16},{96,32},{112,48},{1... | collective-permute-start | bytes 1544 | tf_op jit(solution)/shard_map/ppermute | solution.py:49
  171.6 4.2 %collective-permute-start.17 = (f32[1,128]{1,0:T(1,128)S(1)}, f32[1,128]{1,0:T(1,128)S(1)}, u32[]{:S(2)}, u32[]{:S(2)}) collective-permute-start(f32[1,128]{1,0:T(1,128)S(1)} %add.38), channel_id=1, source_target_pairs={{0,128},{16,144},{32,160},{48,176},{64,192},{80,208},{96,224},{112... | collective-permute-start | bytes 1544 | tf_op jit(solution)/shard_map/ppermute | solution.py:49

commit v6 on v4

--- a/solution.py
+++ b/solution.py
@@ -11,6 +11,7 @@
 BLOCK = 128
 FORWARD_HEADS = 6
 BACKWARD_HEADS = 3
+EARLY = 64
 FIRST = 96
 NEG = -1e30
 SCALE = HD**-0.5
@@ -25,9 +26,10 @@
     return s if s % (n // 2) in (1, 2, 5, 6) else n - 1 - s
 
 
-def moved(value, target):
+def moved(value, target, kept=None):
     size = lax.axis_size("section")
-    return lax.ppermute(value, "section", [(i, target(i, size) % size) for i in range(size)])
+    pairs = [(i, target(i, size) % size) for i in range(size) if kept is None or i % (size // 2) in kept]
+    return lax.ppermute(value, "section", pairs)
 
 
 def doubled_sum(value, axis):
@@ -73,14 +75,22 @@
         out_ref[start : start + BLOCK, hs] = out.astype(jnp.bfloat16)
 
 
-def backward_kernel(first_ref, rest_ref, low_ref, high_ref, gain_ref, tail_ref, lengths_ref, out_ref, raw_ref):
+def backward_kernel(
+    own_ref, early_ref, late_ref, first_ref, rest_ref, low_ref, high_ref, stays_ref, gain_ref, tail_ref, lengths_ref, out_ref, raw_ref
+):
     length = row_length(tail_ref, lengths_ref, 1)
     seq = 2 * low_ref.shape[0]
     heads = [slice(h * HD, (h + 1) * HD) for h in range(low_ref.shape[1] // HD)]
     starts = range(0, seq, BLOCK)
     loaded = []
     for hs in heads:
-        q, k, v = (jnp.concatenate([first_ref[part, :, hs], rest_ref[part, :, hs]], axis=0) for part in range(3))
+        top = [
+            jnp.where(stays_ref[...] > 0, own_ref[part, :, hs], early_ref[part, :, hs] + late_ref[part, :, hs])
+            for part in range(3)
+        ]
+        q, k, v = (
+            jnp.concatenate([top[part], first_ref[part, :, hs], rest_ref[part, :, hs]], axis=0) for part in range(3)
+        )
         g = jnp.concatenate([low_ref[:, hs], high_ref[:, hs]], axis=0)
         qs = (q.astype(jnp.float32) * gain_ref[:, hs]).astype(jnp.bfloat16)
         loaded.append((q, k, v, g, qs))
@@ -143,17 +153,20 @@
     )(block, block, block, aux, aux, lengths)
 
 
-def backward_part(first, rest, upstream, aux, lengths):
-    seq, features = FIRST + rest.shape[3], rest.shape[4]
+def backward_part(stored, upstream, stays, aux, lengths):
+    seq, features = stored[0].shape[3:]
     width = BACKWARD_HEADS * HD
     heads = features // HD
     return pl.pallas_call(
         backward_kernel,
         grid=(features // width,),
         in_specs=[
-            pl.BlockSpec((None, None, 3, FIRST, width), lambda h: (0, 0, 0, 0, h)),
-            pl.BlockSpec((None, None, 3, seq - FIRST, width), lambda h: (0, 0, 0, 0, h)),
+            *[
+                pl.BlockSpec((None, None, 3, rows, width), lambda h: (0, 0, 0, 0, h))
+                for rows in (EARLY, EARLY, EARLY, FIRST, seq - EARLY - FIRST)
+            ],
             *[pl.BlockSpec((None, None, seq // 2, width), lambda h: (0, 0, 0, h))] * 2,
+            pl.BlockSpec((1, HD), lambda h: (0, 0)),
             *small_specs(width, features, lengths),
         ],
         out_specs=[
@@ -168,7 +181,7 @@
             flops=heads * seq * HD, bytes_accessed=seq * features, transcendentals=heads * seq
         ),
         name="backward",
-    )(first, rest, *upstream, aux, aux, lengths)
+    )(*stored, *upstream, stays, aux, aux, lengths)
 
 
 def settle_kernel(in_ref, out_ref):
@@ -208,20 +221,31 @@
     aux = jnp.concatenate(
         [query_gain, plan.astype(jnp.float32), jnp.zeros((1, HD - entries), jnp.float32)], axis=1
     )
+    early = moved(parked[:, :, :, :EARLY], lambda s, n: n - 1 - s, (6,))
     aux_back = moved(aux, lambda s, n: site(s, n))
     aux_ahead = moved(aux, lambda s, n: s - 1)
-    first = moved(parked[:, :, :, :FIRST], lambda s, n: site(n - 1 - s, n))
+    first = moved(parked[:, :, :, EARLY : EARLY + FIRST], lambda s, n: site(n - 1 - s, n))
     half = grad_out.shape[2] // 2
-    low, high, rest, aux_back, aux_ahead = lax.optimization_barrier(
-        (grad_out[:, :, :half], grad_out[:, :, half:], parked[:, :, :, FIRST:], aux_back, aux_ahead)
+    low, high, late, rest, aux_back, aux_ahead = lax.optimization_barrier(
+        (
+            grad_out[:, :, :half],
+            grad_out[:, :, half:],
+            parked[:, :, :, :EARLY],
+            parked[:, :, :, EARLY + FIRST :],
+            aux_back,
+            aux_ahead,
+        )
     )
     rest = moved(rest, lambda s, n: site(n - 1 - s, n))
     upstream = [moved(part, lambda s, n: site((s - 1) % n, n)) for part in (low, high)]
     aux_ahead, first, upstream = lax.optimization_barrier((aux_ahead, first, upstream))
     attended = forward_part(inbound, aux_ahead, lengths)
-    _, first, rest, upstream = lax.optimization_barrier((attended, first, rest, upstream))
+    late = moved(late, lambda s, n: n - 1 - s, (1, 2, 5))
+    _, early, late, first, rest, upstream = lax.optimization_barrier((attended, early, late, first, rest, upstream))
+    z = lax.axis_index("section") % (lax.axis_size("section") // 2)
+    stays = jnp.full((1, HD), (z % 4 == 0) | (z % 4 == 3), jnp.float32)
     attended = moved(attended, lambda s, n: s + 1)
-    grads, raw = backward_part(first, rest, upstream, aux_back, lengths)
+    grads, raw = backward_part((parked, early, late, first, rest), upstream, stays, aux_back, lengths)
     total = doubled_sum(raw, "dp")
     grads, total = lax.optimization_barrier((grads, total))
     own_total = moved(total, lambda s, n: site(s, n))

time: 204 us -> 199 us (0.975)
  starting transfers between devices: 94.9 us -> 85.6 us
  waiting for transfers between devices: 77.1 us -> 79.9 us
    ppermute x8, waiting for transfers between devices: 16.7 us -> 38.8 us  [doubled_sum(): lax.ppermute(value, axis, [(i, i ^ step) for i in range(size)])]
    ppermute x9 -> x11, waiting for transfers between devices: 60.4 us -> 41.2 us  [moved(): return lax.ppermute(value, 'section', pairs)]
    ppermute x9 -> x11, starting transfers between devices: 65.2 us -> 51.2 us  [moved(): return lax.ppermute(value, 'section', pairs)]
    ppermute x8, starting transfers between devices: 29.7 us -> 34.4 us  [doubled_sum(): lax.ppermute(value, axis, [(i, i ^ step) for i in range(size)])]
  transfers between devices with their start and end apart: 17 -> 19, of which waited for: 10 -> 11; matrix products, arithmetic and copies ran while one was open for 3% -> 4% of each run, Pallas kernels for 9% -> 9%
where the time goes in v6:
time: 199 us; the launch traced here: 197 us
  starting transfers between devices  85.6 us (43%)
  waiting for transfers between devices  79.9 us (40%)
  Pallas kernels  18 us (9%)
  local copies, waits for them, and re-layouts  9.79 us (5%)
  other arithmetic  2.61 us (1%)
    ppermute x11, starting transfers between devices, moved(): return lax.ppermute(value, 'section', pairs)  51.2 us
    ppermute x11, waiting for transfers between devices, moved(): return lax.ppermute(value, 'section', pairs)  41.2 us
    ppermute x8, waiting for transfers between devices, doubled_sum(): lax.ppermute(value, axis, [(i, i ^ step) for i in range(size)])  38.8 us
    ppermute x8, starting transfers between devices, doubled_sum(): lax.ppermute(value, axis, [(i, i ^ step) for i in range(size)])  34.4 us
    pallas_call x1, Pallas kernels, backward_part(): pl.pallas_call(backward_kernel, grid=(features // width,), in_specs=[*[pl...  8.42 us
    pallas_call x1, Pallas kernels, forward_part(): pl.pallas_call(forward_kernel, grid=(features // width,), in_specs=[*part...  4.89 us
  transfers between devices with their start and end apart: 19, of which 11 were waited for; matrix products, arithmetic and copies ran while one was open for 4% of the time, Pallas kernels for 9%

profile of v6, /device:TPU:8, one launch (start us, length us, event | category | flops | bytes accessed | tf_op | source)
XLA Modules:
  0.0 196.8 jit_solution(14023703853716198281)
XLA Ops:
  0.6 0.7 convert_element_type.6
  1.3 0.8 concatenate.3
  2.1 7.6 %collective-permute-start.1 = (f32[1,1664]{1,0:T(1,128)S(1)}, f32[1,1664]{1,0:T(1,128)S(1)}, u32[]{:S(2)}, u32[]{:S(2)}) collective-permute-start(f32[1,1664]{1,0:T(1,128)S(1)} %concatenate.3), channel_id=1, source_target_pairs={{0,240},{16,0},{32,16},{48,32},{64,48},{80,64},{96,80},{112,96},{1... | collective-permute-start | bytes 19976 | tf_op jit(solution)/shard_map/ppermute | solution.py:32
  9.7 3.0 %collective-permute-start = (f32[1,1664]{1,0:T(1,128)S(1)}, f32[1,1664]{1,0:T(1,128)S(1)}, u32[]{:S(2)}, u32[]{:S(2)}) collective-permute-start(f32[1,1664]{1,0:T(1,128)S(1)} %concatenate.3), channel_id=1, source_target_pairs={{0,240},{16,16},{32,32},{48,192},{64,176},{80,80},{96,96},{112,128... | collective-permute-start | bytes 19976 | tf_op jit(solution)/shard_map/ppermute | solution.py:32
  12.7 1.2 slice.23
  14.0 1.6 collective-permute-start.2
  15.5 1.3 fusion
  16.9 0.9 slice.21
  17.7 1.4 slice.22
  19.2 15.4 %collective-permute-done.gain_ref.tail_ref = f32[1,1664]{1,0:T(1,128)S(1)} collective-permute-done((f32[1,1664]{1,0:T(1,128)S(1)}, f32[1,1664]{1,0:T(1,128)S(1)}, u32[]{:S(2)}, u32[]{:S(2)}) %collective-permute-start) | collective-permute-done | bytes 6688 | tf_op jit(solution)/shard_map/ppermute | solution.py:32
  34.6 0.8 collective-permute-start.3
  35.4 0.7 collective-permute-start.4
  36.1 2.2 %collective-permute-start.7 = (bf16[1,1,3,224,1536]{4,3,2,1,0:T(8,128)(2,1)}, bf16[1,1,3,224,1536]{4,3,2,1,0:T(8,128)(2,1)S(1)}, u32[]{:S(2)}, u32[]{:S(2)}) collective-permute-start(bf16[1,1,3,224,1536]{4,3,2,1,0:T(8,128)(2,1)} %slice.22), channel_id=1, source_target_pairs={{0,0},{16,224},{32,208},{48,48},{64,64},{80,160},{96,144},{112,112... | collective-permute-start | bytes 6193160 | tf_op jit(solution)/shard_map/ppermute | solution.py:32
  38.4 0.8 copy-done.4
  39.2 4.9 %forward.1 = bf16[1,1,384,1536]{3,2,1,0:T(8,128)(2,1)} custom-call(bf16[1,1,3,384,1536]{4,3,2,1,0:T(8,128)(2,1)} %v_ref.1, bf16[1,1,3,384,1536]{4,3,2,1,0:T(8,128)(2,1)} %v_ref.1, bf16[1,1,3,384,1536]{4,3,2,1,0:T(8,128)(2,1)} %v_ref.1, f32[1,1664]{1,0:T(1,128)} %copy-done.8, f32[1,1664]{1,0:T(1,128)} %copy-done.8, s32[1,8]{1,0:T(1,128)} %lengths_ref.3), custom_call_target="tpu_custom_call" | custom-call | flops 99999997952 | bytes 4718592 | tf_op jit(solution)/shard_map/forward/pallas_call | solution.py:143
  44.1 23.6 %collective-permute-start.11 = (bf16[1,1,384,1536]{3,2,1,0:T(8,128)(2,1)}, bf16[1,1,384,1536]{3,2,1,0:T(8,128)(2,1)}, u32[]{:S(2)}, u32[]{:S(2)}) collective-permute-start(bf16[1,1,384,1536]{3,2,1,0:T(8,128)(2,1)} %forward.1), channel_id=1, source_target_pairs={{0,16},{16,32},{32,48},{48,64},{64,80},{80,96},{96,112},{112,128},... | collective-permute-start | bytes 3538952 | tf_op jit(solution)/shard_map/ppermute | solution.py:32
  67.7 0.7 collective-permute-start.5
  68.4 1.5 collective-permute-start.6
  69.9 0.7 broadcast_in_dim.7.stays_ref
  70.6 0.1 copy-done.5
  70.7 0.7 copy-done.1
  71.4 8.4 %backward.1 = (bf16[1,1,3,384,1536]{4,3,2,1,0:T(8,128)(2,1)}, f32[1,1536]{1,0:T(1,128)}) custom-call(bf16[1,1,3,384,1536]{4,3,2,1,0:T(8,128)(2,1)} %own_ref.1, bf16[1,1,3,64,1536]{4,3,2,1,0:T(8,128)(2,1)} %copy-done.5, bf16[1,1,3,64,1536]{4,3,2,1,0:T(8,128)(2,1)} %collective-permute-done.6.late_ref, ...), custom_call_target="tpu_custom_call" | custom-call | flops 589824 | bytes 589824 | tf_op jit(solution)/shard_map/backward/pallas_call | solution.py:160
  79.8 0.1 collective-permute-start.8
  79.9 1.4 collective-permute-done.8
  81.3 0.7 add.37
  82.0 1.3 collective-permute-start.9
  83.4 19.3 %collective-permute-done.9 = f32[1,1536]{1,0:T(1,128)S(1)} collective-permute-done((f32[1,1536]{1,0:T(1,128)S(1)}, f32[1,1536]{1,0:T(1,128)S(1)}, u32[]{:S(2)}, u32[]{:S(2)}) %collective-permute-start.9) | collective-permute-done | bytes 6176 | tf_op jit(solution)/shard_map/ppermute | solution.py:39
  102.7 0.0 copy-start.7
  102.7 1.9 collective-permute-start.10
  104.6 7.5 %collective-permute-start.12 = (bf16[1,1,3,384,1536]{4,3,2,1,0:T(8,128)(2,1)}, bf16[1,1,3,384,1536]{4,3,2,1,0:T(8,128)(2,1)S(1)}, u32[]{:S(2)}, u32[]{:S(2)}) collective-permute-start(bf16[1,1,3,384,1536]{4,3,2,1,0:T(8,128)(2,1)} %get-tuple-element.46), channel_id=1, source_target_pairs={{0,240},{16,16},{32,32},{48,192},{64,176},{80,80},{96,96},{112,128... | collective-permute-start | bytes 10616840 | tf_op jit(solution)/shard_map/ppermute | solution.py:32
  112.2 3.4 %settle.1 = bf16[1,1,384,1536]{3,2,1,0:T(8,128)(2,1)} custom-call(bf16[1,1,384,1536]{3,2,1,0:T(8,128)(2,1)} %collective-permute-done.11.in_ref), custom_call_target="tpu_custom_call" | custom-call | flops 99999997952 | bytes 2359296 | tf_op jit(solution)/shard_map/settle/pallas_call | solution.py:194
  115.6 3.7 %collective-permute-done.10 = f32[1,1536]{1,0:T(1,128)S(1)} collective-permute-done((f32[1,1536]{1,0:T(1,128)S(1)}, f32[1,1536]{1,0:T(1,128)S(1)}, u32[]{:S(2)}, u32[]{:S(2)}) %collective-permute-start.10) | collective-permute-done | bytes 6176 | tf_op jit(solution)/shard_map/ppermute | solution.py:32
  119.3 1.3 squares.1
  120.6 1.5 collective-permute-start.13
  122.1 2.3 %collective-permute-done.13 = f32[1,128]{1,0:T(1,128)S(1)} collective-permute-done((f32[1,128]{1,0:T(1,128)}, f32[1,128]{1,0:T(1,128)S(1)}, u32[]{:S(2)}, u32[]{:S(2)}) %collective-permute-start.13) | collective-permute-done | bytes 544 | tf_op jit(solution)/shard_map/ppermute | solution.py:39
  124.4 0.6 add.39
  125.0 3.0 %collective-permute-start.14 = (f32[1,128]{1,0:T(1,128)S(1)}, f32[1,128]{1,0:T(1,128)S(1)}, u32[]{:S(2)}, u32[]{:S(2)}) collective-permute-start(f32[1,128]{1,0:T(1,128)S(1)} %add.39), channel_id=1, source_target_pairs={{0,8},{4,12},{8,0},{12,4},{1,9},{5,13},{9,1},{13,5},{2,10},{6,14},... | collective-permute-start | bytes 1544 | tf_op jit(solution)/shard_map/ppermute | solution.py:39
  128.0 2.0 %collective-permute-done.14 = f32[1,128]{1,0:T(1,128)S(1)} collective-permute-done((f32[1,128]{1,0:T(1,128)S(1)}, f32[1,128]{1,0:T(1,128)S(1)}, u32[]{:S(2)}, u32[]{:S(2)}) %collective-permute-start.14) | collective-permute-done | bytes 544 | tf_op jit(solution)/shard_map/ppermute | solution.py:39
  130.1 23.8 %collective-permute-start.15 = (f32[1,128]{1,0:T(1,128)S(1)}, f32[1,128]{1,0:T(1,128)S(1)}, u32[]{:S(2)}, u32[]{:S(2)}) collective-permute-start(f32[1,128]{1,0:T(1,128)S(1)} %add.40), channel_id=1, source_target_pairs={{0,16},{16,0},{32,48},{48,32},{64,80},{80,64},{96,112},{112,96},{1... | collective-permute-start | bytes 1544 | tf_op jit(solution)/shard_map/ppermute | solution.py:39
  153.8 1.5 collective-permute-done.15
  155.4 4.4 %collective-permute-done.16 = f32[1,128]{1,0:T(1,128)S(1)} collective-permute-done((f32[1,128]{1,0:T(1,128)S(1)}, f32[1,128]{1,0:T(1,128)S(1)}, u32[]{:S(2)}, u32[]{:S(2)}) %collective-permute-start.16) | collective-permute-done | bytes 544 | tf_op jit(solution)/shard_map/ppermute | solution.py:39
  159.8 3.4 %collective-permute-start.17 = (f32[1,128]{1,0:T(1,128)S(1)}, f32[1,128]{1,0:T(1,128)S(1)}, u32[]{:S(2)}, u32[]{:S(2)}) collective-permute-start(f32[1,128]{1,0:T(1,128)S(1)} %add.42), channel_id=1, source_target_pairs={{0,64},{16,80},{32,96},{48,112},{64,0},{80,16},{96,32},{112,48},{1... | collective-permute-start | bytes 1544 | tf_op jit(solution)/shard_map/ppermute | solution.py:39
  163.2 4.0 %collective-permute-done.17 = f32[1,128]{1,0:T(1,128)S(1)} collective-permute-done((f32[1,128]{1,0:T(1,128)S(1)}, f32[1,128]{1,0:T(1,128)S(1)}, u32[]{:S(2)}, u32[]{:S(2)}) %collective-permute-start.17) | collective-permute-done | bytes 544 | tf_op jit(solution)/shard_map/ppermute | solution.py:39
  167.3 1.2 collective-permute-start.18
  168.5 3.8 %collective-permute-done.18 = f32[1,128]{1,0:T(1,128)S(1)} collective-permute-done((f32[1,128]{1,0:T(1,128)S(1)}, f32[1,128]{1,0:T(1,128)S(1)}, u32[]{:S(2)}, u32[]{:S(2)}) %collective-permute-start.18) | collective-permute-done | bytes 544 | tf_op jit(solution)/shard_map/ppermute | solution.py:39
  172.4 0.6 broadcast_divide_fusion
  173.0 22.0 %collective-permute-done.12 = bf16[1,1,3,384,1536]{4,3,2,1,0:T(8,128)(2,1)S(1)} collective-permute-done((bf16[1,1,3,384,1536]{4,3,2,1,0:T(8,128)(2,1)}, bf16[1,1,3,384,1536]{4,3,2,1,0:T(8,128)(2,1)S(1)}, u32[]{:S(2)}, u32[]{:S(2)}) %collective-permute-start.12) | collective-permute-done | bytes 3538976 | tf_op jit(solution)/shard_map/ppermute | solution.py:32
  195.0 1.8 copy.10
  (30 shorter events, 0.1 us)
Async XLA Ops:
  2.1 14.8 %copy-start = (bf16[1,1,3,384,1536]{4,3,2,1,0:T(8,128)(2,1)S(1)}, bf16[1,1,3,384,1536]{4,3,2,1,0:T(8,128)(2,1)}, u32[]{:S(2)}) copy-start(bf16[1,1,3,384,1536]{4,3,2,1,0:T(8,128)(2,1)} %own_ref.1) | copy-start | bytes 10616836
  2.1 17.1 %collective-permute-start.1 = (f32[1,1664]{1,0:T(1,128)S(1)}, f32[1,1664]{1,0:T(1,128)S(1)}, u32[]{:S(2)}, u32[]{:S(2)}) collective-permute-start(f32[1,1664]{1,0:T(1,128)S(1)} %concatenate.3), channel_id=1, source_target_pairs={{0,240},{16,0},{32,16},{48,32},{64,48},{80,64},{96,80},{112,96},{1... | collective-permute-start | bytes 19976 | tf_op jit(solution)/shard_map/ppermute | solution.py:32
  9.7 24.9 %collective-permute-start = (f32[1,1664]{1,0:T(1,128)S(1)}, f32[1,1664]{1,0:T(1,128)S(1)}, u32[]{:S(2)}, u32[]{:S(2)}) collective-permute-start(f32[1,1664]{1,0:T(1,128)S(1)} %concatenate.3), channel_id=1, source_target_pairs={{0,240},{16,16},{32,32},{48,192},{64,176},{80,80},{96,96},{112,128... | collective-permute-start | bytes 19976 | tf_op jit(solution)/shard_map/ppermute | solution.py:32
  14.0 25.3 %collective-permute-start.2 = (bf16[1,1,3,96,1536]{4,3,2,1,0:T(8,128)(2,1)S(1)}, bf16[1,1,3,96,1536]{4,3,2,1,0:T(8,128)(2,1)}, u32[]{:S(2)}, u32[]{:S(2)}) collective-permute-start(bf16[1,1,3,96,1536]{4,3,2,1,0:T(8,128)(2,1)S(1)} %slice.23), channel_id=1, source_target_pairs={{0,0},{16,224},{32,208},{48,48},{64,64},{80,160},{96,144},{112,112... | collective-permute-start | bytes 2654216 | tf_op jit(solution)/shard_map/ppermute | solution.py:32
  19.2 20.0 %copy-start.8 = (f32[1,1664]{1,0:T(1,128)}, f32[1,1664]{1,0:T(1,128)S(1)}, u32[]{:S(2)}) copy-start(f32[1,1664]{1,0:T(1,128)S(1)} %collective-permute-done.1.gain_ref.tail_ref) | copy-start | bytes 19972
  34.6 9.5 %copy-start.6 = (f32[1,1664]{1,0:T(1,128)}, f32[1,1664]{1,0:T(1,128)S(1)}, u32[]{:S(2)}) copy-start(f32[1,1664]{1,0:T(1,128)S(1)} %collective-permute-done.gain_ref.tail_ref) | copy-start | bytes 19972
  34.6 33.1 %copy-start.2 = (bf16[1,1,3,64,1536]{4,3,2,1,0:T(8,128)(2,1)S(1)}, bf16[1,1,3,64,1536]{4,3,2,1,0:T(8,128)(2,1)}, u32[]{:S(2)}) copy-start(bf16[1,1,3,64,1536]{4,3,2,1,0:T(8,128)(2,1)} %slice.21) | copy-start | bytes 1769476
  34.6 3.8 %collective-permute-start.3 = (bf16[1,1,192,1536]{3,2,1,0:T(8,128)(2,1)S(1)}, bf16[1,1,192,1536]{3,2,1,0:T(8,128)(2,1)S(1)}, u32[]{:S(2)}, u32[]{:S(2)}) collective-permute-start(bf16[1,1,192,1536]{3,2,1,0:T(8,128)(2,1)S(1)} %get-tuple-element.27), channel_id=1, source_target_pairs={{0,0},{16,240},{32,16},{48,32},{64,192},{80,176},{96,80},{112,96},... | collective-permute-start | bytes 1769480 | tf_op jit(solution)/shard_map/ppermute | solution.py:32
  35.4 3.0 %collective-permute-start.4 = (bf16[1,1,192,1536]{3,2,1,0:T(8,128)(2,1)S(1)}, bf16[1,1,192,1536]{3,2,1,0:T(8,128)(2,1)S(1)}, u32[]{:S(2)}, u32[]{:S(2)}) collective-permute-start(bf16[1,1,192,1536]{3,2,1,0:T(8,128)(2,1)S(1)} %get-tuple-element.28), channel_id=1, source_target_pairs={{0,0},{16,240},{32,16},{48,32},{64,192},{80,176},{96,80},{112,96},... | collective-permute-start | bytes 1769480 | tf_op jit(solution)/shard_map/ppermute | solution.py:32
  36.1 33.8 %collective-permute-start.7 = (bf16[1,1,3,224,1536]{4,3,2,1,0:T(8,128)(2,1)}, bf16[1,1,3,224,1536]{4,3,2,1,0:T(8,128)(2,1)S(1)}, u32[]{:S(2)}, u32[]{:S(2)}) collective-permute-start(bf16[1,1,3,224,1536]{4,3,2,1,0:T(8,128)(2,1)} %slice.22), channel_id=1, source_target_pairs={{0,0},{16,224},{32,208},{48,48},{64,64},{80,160},{96,144},{112,112... | collective-permute-start | bytes 6193160 | tf_op jit(solution)/shard_map/ppermute | solution.py:32
  38.4 5.8 %copy-start.3 = (bf16[1,1,192,1536]{3,2,1,0:T(8,128)(2,1)}, bf16[1,1,192,1536]{3,2,1,0:T(8,128)(2,1)S(1)}, u32[]{:S(2)}) copy-start(bf16[1,1,192,1536]{3,2,1,0:T(8,128)(2,1)S(1)} %collective-permute-done.3.low_ref) | copy-start | bytes 1769476
  38.4 0.9 copy-start.4
  44.1 68.1 %collective-permute-start.11 = (bf16[1,1,384,1536]{3,2,1,0:T(8,128)(2,1)}, bf16[1,1,384,1536]{3,2,1,0:T(8,128)(2,1)}, u32[]{:S(2)}, u32[]{:S(2)}) collective-permute-start(bf16[1,1,384,1536]{3,2,1,0:T(8,128)(2,1)} %forward.1), channel_id=1, source_target_pairs={{0,16},{16,32},{32,48},{48,64},{64,80},{80,96},{96,112},{112,128},... | collective-permute-start | bytes 3538952 | tf_op jit(solution)/shard_map/ppermute | solution.py:32
  67.7 2.2 %collective-permute-start.5 = (bf16[1,1,3,64,1536]{4,3,2,1,0:T(8,128)(2,1)S(1)}, bf16[1,1,3,64,1536]{4,3,2,1,0:T(8,128)(2,1)S(1)}, u32[]{:S(2)}, u32[]{:S(2)}) collective-permute-start(bf16[1,1,3,64,1536]{4,3,2,1,0:T(8,128)(2,1)S(1)} %copy-done.2), channel_id=1, source_target_pairs={{96,144},{224,16},{97,145},{225,17},{98,146},{226,18},{99,147},{22... | collective-permute-start | bytes 1769480 | tf_op jit(solution)/shard_map/ppermute | solution.py:32
  68.4 1.5 collective-permute-start.6
  69.9 0.8 copy-start.5
  69.9 1.5 copy-start.1
  79.8 1.5 collective-permute-start.8
  82.0 20.7 %collective-permute-start.9 = (f32[1,1536]{1,0:T(1,128)S(1)}, f32[1,1536]{1,0:T(1,128)S(1)}, u32[]{:S(2)}, u32[]{:S(2)}) collective-permute-start(f32[1,1536]{1,0:T(1,128)S(1)} %add.37), channel_id=1, source_target_pairs={{0,2},{1,3},{2,0},{3,1},{4,6},{5,7},{6,4},{7,5},{8,10},{9,11},{10,... | collective-permute-start | bytes 18440 | tf_op jit(solution)/shard_map/ppermute | solution.py:39
  102.7 12.9 %copy-start.7 = (f32[1,1536]{1,0:T(1,128)}, f32[1,1536]{1,0:T(1,128)S(1)}, u32[]{:S(2)}) copy-start(f32[1,1536]{1,0:T(1,128)S(1)} %add.38.total_ref) | copy-start | bytes 18436
  102.7 16.6 %collective-permute-start.10 = (f32[1,1536]{1,0:T(1,128)S(1)}, f32[1,1536]{1,0:T(1,128)S(1)}, u32[]{:S(2)}, u32[]{:S(2)}) collective-permute-start(f32[1,1536]{1,0:T(1,128)S(1)} %add.38.total_ref), channel_id=1, source_target_pairs={{0,240},{16,16},{32,32},{48,192},{64,176},{80,80},{96,96},{112,128... | collective-permute-start | bytes 18440 | tf_op jit(solution)/shard_map/ppermute | solution.py:32
  104.6 90.4 %collective-permute-start.12 = (bf16[1,1,3,384,1536]{4,3,2,1,0:T(8,128)(2,1)}, bf16[1,1,3,384,1536]{4,3,2,1,0:T(8,128)(2,1)S(1)}, u32[]{:S(2)}, u32[]{:S(2)}) collective-permute-start(bf16[1,1,3,384,1536]{4,3,2,1,0:T(8,128)(2,1)} %get-tuple-element.46), channel_id=1, source_target_pairs={{0,240},{16,16},{32,32},{48,192},{64,176},{80,80},{96,96},{112,128... | collective-permute-start | bytes 10616840 | tf_op jit(solution)/shard_map/ppermute | solution.py:32
  120.6 3.8 %collective-permute-start.13 = (f32[1,128]{1,0:T(1,128)}, f32[1,128]{1,0:T(1,128)S(1)}, u32[]{:S(2)}, u32[]{:S(2)}) collective-permute-start(f32[1,128]{1,0:T(1,128)} %squares.1), channel_id=1, source_target_pairs={{0,4},{4,0},{8,12},{12,8},{1,5},{5,1},{9,13},{13,9},{2,6},{6,2},{1... | collective-permute-start | bytes 1544 | tf_op jit(solution)/shard_map/ppermute | solution.py:39
  125.0 5.0 %collective-permute-start.14 = (f32[1,128]{1,0:T(1,128)S(1)}, f32[1,128]{1,0:T(1,128)S(1)}, u32[]{:S(2)}, u32[]{:S(2)}) collective-permute-start(f32[1,128]{1,0:T(1,128)S(1)} %add.39), channel_id=1, source_target_pairs={{0,8},{4,12},{8,0},{12,4},{1,9},{5,13},{9,1},{13,5},{2,10},{6,14},... | collective-permute-start | bytes 1544 | tf_op jit(solution)/shard_map/ppermute | solution.py:39
  130.1 25.3 %collective-permute-start.15 = (f32[1,128]{1,0:T(1,128)S(1)}, f32[1,128]{1,0:T(1,128)S(1)}, u32[]{:S(2)}, u32[]{:S(2)}) collective-permute-start(f32[1,128]{1,0:T(1,128)S(1)} %add.40), channel_id=1, source_target_pairs={{0,16},{16,0},{32,48},{48,32},{64,80},{80,64},{96,112},{112,96},{1... | collective-permute-start | bytes 1544 | tf_op jit(solution)/shard_map/ppermute | solution.py:39
  155.4 4.4 %collective-permute-start.16 = (f32[1,128]{1,0:T(1,128)S(1)}, f32[1,128]{1,0:T(1,128)S(1)}, u32[]{:S(2)}, u32[]{:S(2)}) collective-permute-start(f32[1,128]{1,0:T(1,128)S(1)} %add.41), channel_id=1, source_target_pairs={{0,32},{16,48},{32,0},{48,16},{64,96},{80,112},{96,64},{112,80},{1... | collective-permute-start | bytes 1544 | tf_op jit(solution)/shard_map/ppermute | solution.py:39
  159.8 7.5 %collective-permute-start.17 = (f32[1,128]{1,0:T(1,128)S(1)}, f32[1,128]{1,0:T(1,128)S(1)}, u32[]{:S(2)}, u32[]{:S(2)}) collective-permute-start(f32[1,128]{1,0:T(1,128)S(1)} %add.42), channel_id=1, source_target_pairs={{0,64},{16,80},{32,96},{48,112},{64,0},{80,16},{96,32},{112,48},{1... | collective-permute-start | bytes 1544 | tf_op jit(solution)/shard_map/ppermute | solution.py:39
  167.3 5.0 %collective-permute-start.18 = (f32[1,128]{1,0:T(1,128)S(1)}, f32[1,128]{1,0:T(1,128)S(1)}, u32[]{:S(2)}, u32[]{:S(2)}) collective-permute-start(f32[1,128]{1,0:T(1,128)S(1)} %add.43), channel_id=1, source_target_pairs={{0,128},{16,144},{32,160},{48,176},{64,192},{80,208},{96,224},{112... | collective-permute-start | bytes 1544 | tf_op jit(solution)/shard_map/ppermute | solution.py:39

commit v7 on v6

--- a/solution.py
+++ b/solution.py
@@ -12,7 +12,7 @@
 FORWARD_HEADS = 6
 BACKWARD_HEADS = 3
 EARLY = 64
-FIRST = 96
+FIRST = 112
 NEG = -1e30
 SCALE = HD**-0.5
 LOG2E = 1.4426950408889634

time: 199 us -> 197 us (0.990)
  starting transfers between devices: 85.6 us -> 66.8 us
  waiting for transfers between devices: 79.9 us -> 96.6 us
    ppermute x11, waiting for transfers between devices: 41.2 us -> 77.9 us  [moved(): return lax.ppermute(value, 'section', pairs)]
    ppermute x11, starting transfers between devices: 51.2 us -> 27.7 us  [moved(): return lax.ppermute(value, 'section', pairs)]
    ppermute x8, waiting for transfers between devices: 38.8 us -> 18.7 us  [doubled_sum(): lax.ppermute(value, axis, [(i, i ^ step) for i in range(size)])]
    ppermute x8, starting transfers between devices: 34.4 us -> 39.1 us  [doubled_sum(): lax.ppermute(value, axis, [(i, i ^ step) for i in range(size)])]
where the time goes in v7:
time: 197 us; the launch traced here: 195 us
  waiting for transfers between devices  96.6 us (49%)
  starting transfers between devices  66.8 us (34%)
  Pallas kernels  18 us (9%)
  local copies, waits for them, and re-layouts  9.78 us (5%)
  other arithmetic  2.61 us (1%)
    ppermute x11, waiting for transfers between devices, moved(): return lax.ppermute(value, 'section', pairs)  77.9 us
    ppermute x8, starting transfers between devices, doubled_sum(): lax.ppermute(value, axis, [(i, i ^ step) for i in range(size)])  39.1 us
    ppermute x11, starting transfers between devices, moved(): return lax.ppermute(value, 'section', pairs)  27.7 us
    ppermute x8, waiting for transfers between devices, doubled_sum(): lax.ppermute(value, axis, [(i, i ^ step) for i in range(size)])  18.7 us
    pallas_call x1, Pallas kernels, backward_part(): pl.pallas_call(backward_kernel, grid=(features // width,), in_specs=[*[pl...  8.38 us
    pallas_call x1, Pallas kernels, forward_part(): pl.pallas_call(forward_kernel, grid=(features // width,), in_specs=[*part...  4.9 us
  transfers between devices with their start and end apart: 19, of which 11 were waited for; matrix products, arithmetic and copies ran while one was open for 4% of the time, Pallas kernels for 9%

profile of v7, /device:TPU:8, one launch (start us, length us, event | category | flops | bytes accessed | tf_op | source)
XLA Modules:
  0.0 194.7 jit_solution(10559924272718686103)
XLA Ops:
  0.6 0.7 convert_element_type.6
  1.3 0.8 concatenate.3
  2.1 7.6 %collective-permute-start.1 = (f32[1,1664]{1,0:T(1,128)S(1)}, f32[1,1664]{1,0:T(1,128)S(1)}, u32[]{:S(2)}, u32[]{:S(2)}) collective-permute-start(f32[1,1664]{1,0:T(1,128)S(1)} %concatenate.3), channel_id=1, source_target_pairs={{0,240},{16,0},{32,16},{48,32},{64,48},{80,64},{96,80},{112,96},{1... | collective-permute-start | bytes 19976 | tf_op jit(solution)/shard_map/ppermute | solution.py:32
  9.7 3.0 %collective-permute-start = (f32[1,1664]{1,0:T(1,128)S(1)}, f32[1,1664]{1,0:T(1,128)S(1)}, u32[]{:S(2)}, u32[]{:S(2)}) collective-permute-start(f32[1,1664]{1,0:T(1,128)S(1)} %concatenate.3), channel_id=1, source_target_pairs={{0,240},{16,16},{32,32},{48,192},{64,176},{80,80},{96,96},{112,128... | collective-permute-start | bytes 19976 | tf_op jit(solution)/shard_map/ppermute | solution.py:32
  12.7 1.3 slice.23
  14.0 1.6 collective-permute-start.2
  15.6 1.3 fusion
  17.0 0.9 slice.21
  17.8 1.4 slice.22
  19.3 54.0 %collective-permute-done.gain_ref.tail_ref = f32[1,1664]{1,0:T(1,128)S(1)} collective-permute-done((f32[1,1664]{1,0:T(1,128)S(1)}, f32[1,1664]{1,0:T(1,128)S(1)}, u32[]{:S(2)}, u32[]{:S(2)}) %collective-permute-start) | collective-permute-done | bytes 6688 | tf_op jit(solution)/shard_map/ppermute | solution.py:32
  73.2 0.8 collective-permute-start.3
  74.1 0.7 collective-permute-start.4
  74.8 2.2 %collective-permute-start.7 = (bf16[1,1,3,208,1536]{4,3,2,1,0:T(8,128)(2,1)}, bf16[1,1,3,208,1536]{4,3,2,1,0:T(8,128)(2,1)S(1)}, u32[]{:S(2)}, u32[]{:S(2)}) collective-permute-start(bf16[1,1,3,208,1536]{4,3,2,1,0:T(8,128)(2,1)} %slice.22), channel_id=1, source_target_pairs={{0,0},{16,224},{32,208},{48,48},{64,64},{80,160},{96,144},{112,112... | collective-permute-start | bytes 5750792 | tf_op jit(solution)/shard_map/ppermute | solution.py:32
  77.0 0.8 copy-done.4
  77.8 4.9 %forward.1 = bf16[1,1,384,1536]{3,2,1,0:T(8,128)(2,1)} custom-call(bf16[1,1,3,384,1536]{4,3,2,1,0:T(8,128)(2,1)} %v_ref.1, bf16[1,1,3,384,1536]{4,3,2,1,0:T(8,128)(2,1)} %v_ref.1, bf16[1,1,3,384,1536]{4,3,2,1,0:T(8,128)(2,1)} %v_ref.1, f32[1,1664]{1,0:T(1,128)} %copy-done.8, f32[1,1664]{1,0:T(1,128)} %copy-done.8, s32[1,8]{1,0:T(1,128)} %lengths_ref.3), custom_call_target="tpu_custom_call" | custom-call | flops 99999997952 | bytes 4718592 | tf_op jit(solution)/shard_map/forward/pallas_call | solution.py:143
  82.7 0.1 collective-permute-start.11
  82.8 0.7 collective-permute-start.5
  83.5 1.5 collective-permute-start.6
  85.1 0.7 broadcast_in_dim.7.stays_ref
  85.7 0.1 copy-done.5
  85.9 0.6 copy-done.1
  86.5 8.4 %backward.1 = (bf16[1,1,3,384,1536]{4,3,2,1,0:T(8,128)(2,1)}, f32[1,1536]{1,0:T(1,128)}) custom-call(bf16[1,1,3,384,1536]{4,3,2,1,0:T(8,128)(2,1)} %own_ref.1, bf16[1,1,3,64,1536]{4,3,2,1,0:T(8,128)(2,1)} %copy-done.5, bf16[1,1,3,64,1536]{4,3,2,1,0:T(8,128)(2,1)} %collective-permute-done.6.late_ref, ...), custom_call_target="tpu_custom_call" | custom-call | flops 589824 | bytes 589824 | tf_op jit(solution)/shard_map/backward/pallas_call | solution.py:160
  94.9 0.1 collective-permute-start.8
  95.0 1.4 collective-permute-done.8
  96.4 0.7 add.37
  97.1 0.5 collective-permute-start.9
  97.5 4.9 %collective-permute-done.9 = f32[1,1536]{1,0:T(1,128)S(1)} collective-permute-done((f32[1,1536]{1,0:T(1,128)S(1)}, f32[1,1536]{1,0:T(1,128)S(1)}, u32[]{:S(2)}, u32[]{:S(2)}) %collective-permute-start.9) | collective-permute-done | bytes 6176 | tf_op jit(solution)/shard_map/ppermute | solution.py:39
  102.4 5.8 %collective-permute-start.10 = (f32[1,1536]{1,0:T(1,128)S(1)}, f32[1,1536]{1,0:T(1,128)S(1)}, u32[]{:S(2)}, u32[]{:S(2)}) collective-permute-start(f32[1,1536]{1,0:T(1,128)S(1)} %add.38.total_ref), channel_id=1, source_target_pairs={{0,240},{16,16},{32,32},{48,192},{64,176},{80,80},{96,96},{112,128... | collective-permute-start | bytes 18440 | tf_op jit(solution)/shard_map/ppermute | solution.py:32
  108.2 3.7 %collective-permute-start.12 = (bf16[1,1,3,384,1536]{4,3,2,1,0:T(8,128)(2,1)}, bf16[1,1,3,384,1536]{4,3,2,1,0:T(8,128)(2,1)S(1)}, u32[]{:S(2)}, u32[]{:S(2)}) collective-permute-start(bf16[1,1,3,384,1536]{4,3,2,1,0:T(8,128)(2,1)} %get-tuple-element.46), channel_id=1, source_target_pairs={{0,240},{16,16},{32,32},{48,192},{64,176},{80,80},{96,96},{112,128... | collective-permute-start | bytes 10616840 | tf_op jit(solution)/shard_map/ppermute | solution.py:32
  111.9 3.4 %settle.1 = bf16[1,1,384,1536]{3,2,1,0:T(8,128)(2,1)} custom-call(bf16[1,1,384,1536]{3,2,1,0:T(8,128)(2,1)} %collective-permute-done.11.in_ref), custom_call_target="tpu_custom_call" | custom-call | flops 99999997952 | bytes 2359296 | tf_op jit(solution)/shard_map/settle/pallas_call | solution.py:194
  115.3 1.6 collective-permute-done.10
  117.0 1.3 squares.1
  118.3 1.5 collective-permute-start.13
  119.8 2.3 %collective-permute-done.13 = f32[1,128]{1,0:T(1,128)S(1)} collective-permute-done((f32[1,128]{1,0:T(1,128)}, f32[1,128]{1,0:T(1,128)S(1)}, u32[]{:S(2)}, u32[]{:S(2)}) %collective-permute-start.13) | collective-permute-done | bytes 544 | tf_op jit(solution)/shard_map/ppermute | solution.py:39
  122.0 0.6 add.39
  122.7 3.0 %collective-permute-start.14 = (f32[1,128]{1,0:T(1,128)S(1)}, f32[1,128]{1,0:T(1,128)S(1)}, u32[]{:S(2)}, u32[]{:S(2)}) collective-permute-start(f32[1,128]{1,0:T(1,128)S(1)} %add.39), channel_id=1, source_target_pairs={{0,8},{4,12},{8,0},{12,4},{1,9},{5,13},{9,1},{13,5},{2,10},{6,14},... | collective-permute-start | bytes 1544 | tf_op jit(solution)/shard_map/ppermute | solution.py:39
  125.7 2.0 %collective-permute-done.14 = f32[1,128]{1,0:T(1,128)S(1)} collective-permute-done((f32[1,128]{1,0:T(1,128)S(1)}, f32[1,128]{1,0:T(1,128)S(1)}, u32[]{:S(2)}, u32[]{:S(2)}) %collective-permute-start.14) | collective-permute-done | bytes 544 | tf_op jit(solution)/shard_map/ppermute | solution.py:39
  127.7 23.8 %collective-permute-start.15 = (f32[1,128]{1,0:T(1,128)S(1)}, f32[1,128]{1,0:T(1,128)S(1)}, u32[]{:S(2)}, u32[]{:S(2)}) collective-permute-start(f32[1,128]{1,0:T(1,128)S(1)} %add.40), channel_id=1, source_target_pairs={{0,16},{16,0},{32,48},{48,32},{64,80},{80,64},{96,112},{112,96},{1... | collective-permute-start | bytes 1544 | tf_op jit(solution)/shard_map/ppermute | solution.py:39
  151.5 1.5 collective-permute-done.15
  153.0 2.4 %collective-permute-start.16 = (f32[1,128]{1,0:T(1,128)S(1)}, f32[1,128]{1,0:T(1,128)S(1)}, u32[]{:S(2)}, u32[]{:S(2)}) collective-permute-start(f32[1,128]{1,0:T(1,128)S(1)} %add.41), channel_id=1, source_target_pairs={{0,32},{16,48},{32,0},{48,16},{64,96},{80,112},{96,64},{112,80},{1... | collective-permute-start | bytes 1544 | tf_op jit(solution)/shard_map/ppermute | solution.py:39
  155.3 2.1 %collective-permute-done.16 = f32[1,128]{1,0:T(1,128)S(1)} collective-permute-done((f32[1,128]{1,0:T(1,128)S(1)}, f32[1,128]{1,0:T(1,128)S(1)}, u32[]{:S(2)}, u32[]{:S(2)}) %collective-permute-start.16) | collective-permute-done | bytes 544 | tf_op jit(solution)/shard_map/ppermute | solution.py:39
  157.4 5.8 %collective-permute-start.17 = (f32[1,128]{1,0:T(1,128)S(1)}, f32[1,128]{1,0:T(1,128)S(1)}, u32[]{:S(2)}, u32[]{:S(2)}) collective-permute-start(f32[1,128]{1,0:T(1,128)S(1)} %add.42), channel_id=1, source_target_pairs={{0,64},{16,80},{32,96},{48,112},{64,0},{80,16},{96,32},{112,48},{1... | collective-permute-start | bytes 1544 | tf_op jit(solution)/shard_map/ppermute | solution.py:39
  163.2 1.7 collective-permute-done.17
  164.9 2.2 %collective-permute-start.18 = (f32[1,128]{1,0:T(1,128)S(1)}, f32[1,128]{1,0:T(1,128)S(1)}, u32[]{:S(2)}, u32[]{:S(2)}) collective-permute-start(f32[1,128]{1,0:T(1,128)S(1)} %add.43), channel_id=1, source_target_pairs={{0,128},{16,144},{32,160},{48,176},{64,192},{80,208},{96,224},{112... | collective-permute-start | bytes 1544 | tf_op jit(solution)/shard_map/ppermute | solution.py:39
  167.0 2.9 %collective-permute-done.18 = f32[1,128]{1,0:T(1,128)S(1)} collective-permute-done((f32[1,128]{1,0:T(1,128)S(1)}, f32[1,128]{1,0:T(1,128)S(1)}, u32[]{:S(2)}, u32[]{:S(2)}) %collective-permute-start.18) | collective-permute-done | bytes 544 | tf_op jit(solution)/shard_map/ppermute | solution.py:39
  170.0 0.6 broadcast_divide_fusion
  170.6 22.3 %collective-permute-done.12 = bf16[1,1,3,384,1536]{4,3,2,1,0:T(8,128)(2,1)S(1)} collective-permute-done((bf16[1,1,3,384,1536]{4,3,2,1,0:T(8,128)(2,1)}, bf16[1,1,3,384,1536]{4,3,2,1,0:T(8,128)(2,1)S(1)}, u32[]{:S(2)}, u32[]{:S(2)}) %collective-permute-start.12) | collective-permute-done | bytes 3538976 | tf_op jit(solution)/shard_map/ppermute | solution.py:32
  192.9 1.8 copy.10
  (30 shorter events, 0.1 us)
Async XLA Ops:
  2.1 14.9 %copy-start = (bf16[1,1,3,384,1536]{4,3,2,1,0:T(8,128)(2,1)S(1)}, bf16[1,1,3,384,1536]{4,3,2,1,0:T(8,128)(2,1)}, u32[]{:S(2)}) copy-start(bf16[1,1,3,384,1536]{4,3,2,1,0:T(8,128)(2,1)} %own_ref.1) | copy-start | bytes 10616836
  2.1 17.2 %collective-permute-start.1 = (f32[1,1664]{1,0:T(1,128)S(1)}, f32[1,1664]{1,0:T(1,128)S(1)}, u32[]{:S(2)}, u32[]{:S(2)}) collective-permute-start(f32[1,1664]{1,0:T(1,128)S(1)} %concatenate.3), channel_id=1, source_target_pairs={{0,240},{16,0},{32,16},{48,32},{64,48},{80,64},{96,80},{112,96},{1... | collective-permute-start | bytes 19976 | tf_op jit(solution)/shard_map/ppermute | solution.py:32
  9.7 63.5 %collective-permute-start = (f32[1,1664]{1,0:T(1,128)S(1)}, f32[1,1664]{1,0:T(1,128)S(1)}, u32[]{:S(2)}, u32[]{:S(2)}) collective-permute-start(f32[1,1664]{1,0:T(1,128)S(1)} %concatenate.3), channel_id=1, source_target_pairs={{0,240},{16,16},{32,32},{48,192},{64,176},{80,80},{96,96},{112,128... | collective-permute-start | bytes 19976 | tf_op jit(solution)/shard_map/ppermute | solution.py:32
  14.0 63.8 %collective-permute-start.2 = (bf16[1,1,3,112,1536]{4,3,2,1,0:T(8,128)(2,1)S(1)}, bf16[1,1,3,112,1536]{4,3,2,1,0:T(8,128)(2,1)}, u32[]{:S(2)}, u32[]{:S(2)}) collective-permute-start(bf16[1,1,3,112,1536]{4,3,2,1,0:T(8,128)(2,1)S(1)} %slice.23), channel_id=1, source_target_pairs={{0,0},{16,224},{32,208},{48,48},{64,64},{80,160},{96,144},{112,112... | collective-permute-start | bytes 3096584 | tf_op jit(solution)/shard_map/ppermute | solution.py:32
  19.3 58.6 %copy-start.8 = (f32[1,1664]{1,0:T(1,128)}, f32[1,1664]{1,0:T(1,128)S(1)}, u32[]{:S(2)}) copy-start(f32[1,1664]{1,0:T(1,128)S(1)} %collective-permute-done.1.gain_ref.tail_ref) | copy-start | bytes 19972
  73.2 9.5 %copy-start.6 = (f32[1,1664]{1,0:T(1,128)}, f32[1,1664]{1,0:T(1,128)S(1)}, u32[]{:S(2)}) copy-start(f32[1,1664]{1,0:T(1,128)S(1)} %collective-permute-done.gain_ref.tail_ref) | copy-start | bytes 19972
  73.2 9.6 %copy-start.2 = (bf16[1,1,3,64,1536]{4,3,2,1,0:T(8,128)(2,1)S(1)}, bf16[1,1,3,64,1536]{4,3,2,1,0:T(8,128)(2,1)}, u32[]{:S(2)}) copy-start(bf16[1,1,3,64,1536]{4,3,2,1,0:T(8,128)(2,1)} %slice.21) | copy-start | bytes 1769476
  73.2 3.7 %collective-permute-start.3 = (bf16[1,1,192,1536]{3,2,1,0:T(8,128)(2,1)S(1)}, bf16[1,1,192,1536]{3,2,1,0:T(8,128)(2,1)S(1)}, u32[]{:S(2)}, u32[]{:S(2)}) collective-permute-start(bf16[1,1,192,1536]{3,2,1,0:T(8,128)(2,1)S(1)} %get-tuple-element.27), channel_id=1, source_target_pairs={{0,0},{16,240},{32,16},{48,32},{64,192},{80,176},{96,80},{112,96},... | collective-permute-start | bytes 1769480 | tf_op jit(solution)/shard_map/ppermute | solution.py:32
  74.1 2.9 %collective-permute-start.4 = (bf16[1,1,192,1536]{3,2,1,0:T(8,128)(2,1)S(1)}, bf16[1,1,192,1536]{3,2,1,0:T(8,128)(2,1)S(1)}, u32[]{:S(2)}, u32[]{:S(2)}) collective-permute-start(bf16[1,1,192,1536]{3,2,1,0:T(8,128)(2,1)S(1)} %get-tuple-element.28), channel_id=1, source_target_pairs={{0,0},{16,240},{32,16},{48,32},{64,192},{80,176},{96,80},{112,96},... | collective-permute-start | bytes 1769480 | tf_op jit(solution)/shard_map/ppermute | solution.py:32
  74.8 10.3 %collective-permute-start.7 = (bf16[1,1,3,208,1536]{4,3,2,1,0:T(8,128)(2,1)}, bf16[1,1,3,208,1536]{4,3,2,1,0:T(8,128)(2,1)S(1)}, u32[]{:S(2)}, u32[]{:S(2)}) collective-permute-start(bf16[1,1,3,208,1536]{4,3,2,1,0:T(8,128)(2,1)} %slice.22), channel_id=1, source_target_pairs={{0,0},{16,224},{32,208},{48,48},{64,64},{80,160},{96,144},{112,112... | collective-permute-start | bytes 5750792 | tf_op jit(solution)/shard_map/ppermute | solution.py:32
  77.0 5.8 %copy-start.3 = (bf16[1,1,192,1536]{3,2,1,0:T(8,128)(2,1)}, bf16[1,1,192,1536]{3,2,1,0:T(8,128)(2,1)S(1)}, u32[]{:S(2)}) copy-start(bf16[1,1,192,1536]{3,2,1,0:T(8,128)(2,1)S(1)} %collective-permute-done.3.low_ref) | copy-start | bytes 1769476
  77.0 0.9 copy-start.4
  82.7 29.2 %collective-permute-start.11 = (bf16[1,1,384,1536]{3,2,1,0:T(8,128)(2,1)}, bf16[1,1,384,1536]{3,2,1,0:T(8,128)(2,1)}, u32[]{:S(2)}, u32[]{:S(2)}) collective-permute-start(bf16[1,1,384,1536]{3,2,1,0:T(8,128)(2,1)} %forward.1), channel_id=1, source_target_pairs={{0,16},{16,32},{32,48},{48,64},{64,80},{80,96},{96,112},{112,128},... | collective-permute-start | bytes 3538952 | tf_op jit(solution)/shard_map/ppermute | solution.py:32
  82.8 2.2 %collective-permute-start.5 = (bf16[1,1,3,64,1536]{4,3,2,1,0:T(8,128)(2,1)S(1)}, bf16[1,1,3,64,1536]{4,3,2,1,0:T(8,128)(2,1)S(1)}, u32[]{:S(2)}, u32[]{:S(2)}) collective-permute-start(bf16[1,1,3,64,1536]{4,3,2,1,0:T(8,128)(2,1)S(1)} %copy-done.2), channel_id=1, source_target_pairs={{96,144},{224,16},{97,145},{225,17},{98,146},{226,18},{99,147},{22... | collective-permute-start | bytes 1769480 | tf_op jit(solution)/shard_map/ppermute | solution.py:32
  83.5 1.5 collective-permute-start.6
  85.0 0.8 copy-start.5
  85.1 1.5 copy-start.1
  94.9 1.5 collective-permute-start.8
  97.1 5.3 %collective-permute-start.9 = (f32[1,1536]{1,0:T(1,128)S(1)}, f32[1,1536]{1,0:T(1,128)S(1)}, u32[]{:S(2)}, u32[]{:S(2)}) collective-permute-start(f32[1,1536]{1,0:T(1,128)S(1)} %add.37), channel_id=1, source_target_pairs={{0,2},{1,3},{2,0},{3,1},{4,6},{5,7},{6,4},{7,5},{8,10},{9,11},{10,... | collective-permute-start | bytes 18440 | tf_op jit(solution)/shard_map/ppermute | solution.py:39
  102.4 12.9 %copy-start.7 = (f32[1,1536]{1,0:T(1,128)}, f32[1,1536]{1,0:T(1,128)S(1)}, u32[]{:S(2)}) copy-start(f32[1,1536]{1,0:T(1,128)S(1)} %add.38.total_ref) | copy-start | bytes 18436
  102.4 14.5 %collective-permute-start.10 = (f32[1,1536]{1,0:T(1,128)S(1)}, f32[1,1536]{1,0:T(1,128)S(1)}, u32[]{:S(2)}, u32[]{:S(2)}) collective-permute-start(f32[1,1536]{1,0:T(1,128)S(1)} %add.38.total_ref), channel_id=1, source_target_pairs={{0,240},{16,16},{32,32},{48,192},{64,176},{80,80},{96,96},{112,128... | collective-permute-start | bytes 18440 | tf_op jit(solution)/shard_map/ppermute | solution.py:32
  108.2 84.7 %collective-permute-start.12 = (bf16[1,1,3,384,1536]{4,3,2,1,0:T(8,128)(2,1)}, bf16[1,1,3,384,1536]{4,3,2,1,0:T(8,128)(2,1)S(1)}, u32[]{:S(2)}, u32[]{:S(2)}) collective-permute-start(bf16[1,1,3,384,1536]{4,3,2,1,0:T(8,128)(2,1)} %get-tuple-element.46), channel_id=1, source_target_pairs={{0,240},{16,16},{32,32},{48,192},{64,176},{80,80},{96,96},{112,128... | collective-permute-start | bytes 10616840 | tf_op jit(solution)/shard_map/ppermute | solution.py:32
  118.3 3.8 %collective-permute-start.13 = (f32[1,128]{1,0:T(1,128)}, f32[1,128]{1,0:T(1,128)S(1)}, u32[]{:S(2)}, u32[]{:S(2)}) collective-permute-start(f32[1,128]{1,0:T(1,128)} %squares.1), channel_id=1, source_target_pairs={{0,4},{4,0},{8,12},{12,8},{1,5},{5,1},{9,13},{13,9},{2,6},{6,2},{1... | collective-permute-start | bytes 1544 | tf_op jit(solution)/shard_map/ppermute | solution.py:39
  122.7 5.0 %collective-permute-start.14 = (f32[1,128]{1,0:T(1,128)S(1)}, f32[1,128]{1,0:T(1,128)S(1)}, u32[]{:S(2)}, u32[]{:S(2)}) collective-permute-start(f32[1,128]{1,0:T(1,128)S(1)} %add.39), channel_id=1, source_target_pairs={{0,8},{4,12},{8,0},{12,4},{1,9},{5,13},{9,1},{13,5},{2,10},{6,14},... | collective-permute-start | bytes 1544 | tf_op jit(solution)/shard_map/ppermute | solution.py:39
  127.7 25.3 %collective-permute-start.15 = (f32[1,128]{1,0:T(1,128)S(1)}, f32[1,128]{1,0:T(1,128)S(1)}, u32[]{:S(2)}, u32[]{:S(2)}) collective-permute-start(f32[1,128]{1,0:T(1,128)S(1)} %add.40), channel_id=1, source_target_pairs={{0,16},{16,0},{32,48},{48,32},{64,80},{80,64},{96,112},{112,96},{1... | collective-permute-start | bytes 1544 | tf_op jit(solution)/shard_map/ppermute | solution.py:39
  153.0 4.4 %collective-permute-start.16 = (f32[1,128]{1,0:T(1,128)S(1)}, f32[1,128]{1,0:T(1,128)S(1)}, u32[]{:S(2)}, u32[]{:S(2)}) collective-permute-start(f32[1,128]{1,0:T(1,128)S(1)} %add.41), channel_id=1, source_target_pairs={{0,32},{16,48},{32,0},{48,16},{64,96},{80,112},{96,64},{112,80},{1... | collective-permute-start | bytes 1544 | tf_op jit(solution)/shard_map/ppermute | solution.py:39
  157.4 7.5 %collective-permute-start.17 = (f32[1,128]{1,0:T(1,128)S(1)}, f32[1,128]{1,0:T(1,128)S(1)}, u32[]{:S(2)}, u32[]{:S(2)}) collective-permute-start(f32[1,128]{1,0:T(1,128)S(1)} %add.42), channel_id=1, source_target_pairs={{0,64},{16,80},{32,96},{48,112},{64,0},{80,16},{96,32},{112,48},{1... | collective-permute-start | bytes 1544 | tf_op jit(solution)/shard_map/ppermute | solution.py:39
  164.9 5.0 %collective-permute-start.18 = (f32[1,128]{1,0:T(1,128)S(1)}, f32[1,128]{1,0:T(1,128)S(1)}, u32[]{:S(2)}, u32[]{:S(2)}) collective-permute-start(f32[1,128]{1,0:T(1,128)S(1)} %add.43), channel_id=1, source_target_pairs={{0,128},{16,144},{32,160},{48,176},{64,192},{80,208},{96,224},{112... | collective-permute-start | bytes 1544 | tf_op jit(solution)/shard_map/ppermute | solution.py:39
